TPU v7x, 32 devices: a whole 2x2x4 slice. The times are simulated.
32 devices in a mesh: rows: 4 (over y, x), feat: 8 (over z, core).
Axes of the slice: x: 2, y: 2, z: 4, core: 2. Of those that a mesh axis runs over, the one named last changes fastest.
Arguments:
- node_feats: bfloat16 [2048, 1024], P('rows', 'feat'), may hold values from -6 to 6
- weight: bfloat16 [1024, 1024], P(None, 'feat'), may hold values from -0.1875 to 0.1875
- root_weight: bfloat16 [1024, 1024], P(None, 'feat'), may hold values from -0.1875 to 0.1875
- grad_out: bfloat16 [2048, 1024], P('rows', 'feat'), may hold values from -6 to 6
- block_counts: int32 [16], P('rows'), may hold values from 1 to 40, as said below
- tile_cols: int32 [320], P('rows'), may hold values from 0 to 15
- tile_vals: bfloat16 [320, 128, 128], P('rows'), may hold values from -0.125 to 0.125
Outputs:
- grad_feats: bfloat16 [2048, 1024], P('rows', 'feat')
- grad_weight: float32 [1024, 1024], P(None, 'feat')
- grad_root: float32 [1024, 1024], P(None, 'feat')
Inputs may be any that keep to these rules, and one draw needn't show every extreme that they name: `block_counts`: the counts of the 4 row blocks of one index of rows sum to at most 80; in every draw one index of rows fills all its 80 slots and one of its blocks has 40 tiles.
All inputs are finite; a program needn't handle non-finite values.
Results may differ from a plain program's by a relative error of at most 0.0059.
Values may be sent and summed in bfloat16 or wider, within the bound.
No kernel may reach another device: no remote copies, remote signals or barrier semaphores. Data moves between devices by JAX's collectives and lax.ppermute only.
A program may use at most 64 MiB of HBM per device.

v0:
```python
import jax
import jax.numpy as jnp
from jax import lax
from jax.sharding import PartitionSpec as P


def on_device(node_feats, weight, root_weight, grad_out, block_counts, tile_cols, tile_vals):
    rows_dev, width_part = node_feats.shape
    nblocks = block_counts.shape[0]
    tile = tile_vals.shape[1]
    capacity = tile_cols.shape[0]
    all_blocks = nblocks * lax.axis_size("rows")
    weights_cat = jnp.concatenate([weight, root_weight], 1)
    whole_feats = lax.all_gather(node_feats, "feat", axis=1, tiled=True)
    both = jnp.dot(whole_feats, weights_cat, preferred_element_type=jnp.float32)
    hidden = both[:, :width_part].astype(jnp.bfloat16)
    own = both[:, width_part:]
    gathered = lax.all_gather(hidden, "rows", axis=0, tiled=True)
    hblocks = gathered.reshape(all_blocks, tile, width_part)
    ends = jnp.cumsum(block_counts)
    slots = jnp.arange(capacity, dtype=jnp.int32)
    owner = jnp.sum((ends[None, :] <= slots[:, None]).astype(jnp.int32), axis=1)
    live = (owner < nblocks).astype(jnp.float32)
    prod = jnp.einsum(
        "tij,tjf->tif", tile_vals, hblocks[tile_cols], preferred_element_type=jnp.float32
    )
    summed = jax.ops.segment_sum(prod, owner, num_segments=nblocks + 1)[:nblocks]
    pre = summed.reshape(rows_dev, width_part) + own
    sig = jax.nn.sigmoid(pre)
    grad_pre = (grad_out.astype(jnp.float32) * sig * (1.0 + pre * (1.0 - sig))).astype(jnp.bfloat16)
    dblocks = grad_pre.reshape(nblocks, tile, width_part)
    clipped = jnp.minimum(owner, nblocks - 1)
    contrib = (
        jnp.einsum("tij,tif->tjf", tile_vals, dblocks[clipped], preferred_element_type=jnp.float32)
        * live[:, None, None]
    )
    partial_grads = jax.ops.segment_sum(contrib, tile_cols, num_segments=all_blocks)
    grad_sum = lax.psum_scatter(
        partial_grads.reshape(all_blocks * tile, width_part),
        "rows",
        scatter_dimension=0,
        tiled=True,
    )
    grad_hidden = grad_sum.astype(jnp.bfloat16)
    grads_cat = jnp.concatenate([grad_hidden, grad_pre], 1)
    local_weights = lax.dot_general(
        whole_feats, grads_cat, (((0,), (0,)), ((), ())), preferred_element_type=jnp.float32
    )
    weight_sums = lax.psum(local_weights, "rows")
    grad_feats = lax.psum_scatter(
        lax.dot_general(
            weights_cat, grads_cat, (((1,), (1,)), ((), ())), preferred_element_type=jnp.float32
        ),
        "feat",
        scatter_dimension=0,
        tiled=True,
    ).T.astype(jnp.bfloat16)
    return (grad_feats, weight_sums[:, :width_part], weight_sums[:, width_part:])


def solution(mesh):
    placed = (
        P("rows", "feat"),
        P(None, "feat"),
        P(None, "feat"),
        P("rows", "feat"),
        P("rows"),
        P("rows"),
        P("rows", None, None),
    )
    return jax.shard_map(
        on_device,
        mesh=mesh,
        in_specs=placed,
        out_specs=(P("rows", "feat"), P(None, "feat"), P(None, "feat")),
        check_vma=False,
    )
```

profile of v0, /device:TPU:0, one launch (start us, length us, event | category | flops | bytes accessed | tf_op | source)
XLA Modules:
  0.0 241.1 jit_solution(13079584376305969430)
XLA Ops:
  7.2 0.7 all-gather.2.cloned.1.call-update
  8.0 1.0 copy.30
  9.0 0.8 reduce-window.8
  10.6 1.0 constant_dynamic-update-slice_fusion.1
  11.6 1.0 constant_dynamic-update-slice_fusion
  12.6 23.7 %all-gather.2.cloned.1.call-done = bf16[512,1024]{1,0:T(8,128)(2,1)} async-done(((bf16[512,128]{1,0:T(8,128)(2,1)}), bf16[512,1024]{1,0:T(8,128)(2,1)}) %all-gather.2.cloned.1.call-update) | async-done | bytes 1048592 | tf_op jit(solution)/shard_map/all_gather | solution.py:14
  36.3 1.7 convolution_bitcast_fusion.2
  38.1 0.7 copy-done.3
  38.8 10.5 %all_gather.7 = bf16[2048,128]{0,1:T(8,128)(2,1)} all-gather(bf16[512,128]{0,1:T(8,128)(2,1)S(1)} %slice.34), channel_id=1, replica_groups=mesh['rows'=4,'feat'=8] {'rows'}, dimensions={0}, use_global_device_ids=true | all-gather | bytes 655360 | tf_op jit(solution)/shard_map/all_gather | solution.py:18
  49.4 1.3 copy.44
  50.7 2.5 %gather_fusion = bf16[80,128,128]{2,1,0:T(8,128)(2,1)} fusion(bf16[16,128,128]{2,1,0:T(8,128)(2,1)S(1)} %bitcast.30, s32[1024]{0:T(1024)S(1)} %pad_clamp_fusion.1), kind=kCustom, calls=%fused_computation | custom fusion | bytes 5243200 | tf_op jit(solution)/shard_map/gather | solution.py:25
  53.2 6.0 %convolution_bitcast_fusion = f32[80,128,128]{1,2,0:T(8,128)} fusion(bf16[80,128,128]{2,1,0:T(8,128)(2,1)} %gather_fusion, bf16[80,128,128]{2,1,0:T(8,128)(2,1)S(1)} %copy-done), kind=kOutput, calls=%fused_computation.5 | convolution fusion | flops 335544320 | bytes 10485760 | tf_op jit(solution)/shard_map/tij,tjf->tif/dot_general | solution.py:24
  59.3 6.0 %copy.33 = f32[80,128,128]{2,1,0:T(8,128)} copy(f32[80,128,128]{1,2,0:T(8,128)} %convolution_bitcast_fusion) | data formatting | bytes 10485760 | tf_op jit(solution)/shard_map/tij,tjf->tif/dot_general | solution.py:24
  65.2 10.8 %scatter_fusion = f32[5,128,128]{2,1,0:T(8,128)S(1)} fusion(f32[5,128,128]{2,1,0:T(8,128)S(1)} %broadcast_in_dim.21, s32[80]{0:T(128)S(1)} %convert_reduce_fusion, f32[80,128,128]{2,1,0:T(8,128)} %copy.33), kind=kCustom, calls=%fused_computation.2 | custom fusion | flops 1310720 | bytes 15728960 | tf_op jit(solution)/shard_map/scatter-add | solution.py:27
  76.2 1.1 multiply_convert_fusion
  77.4 2.5 %gather_fusion.1 = bf16[80,128,128]{2,1,0:T(8,128)(2,1)} fusion(bf16[4,128,128]{2,1,0:T(8,128)(2,1)S(1)} %bitcast.28, s32[1024]{0:T(1024)S(1)} %pad_clamp_fusion), kind=kCustom, calls=%fused_computation.1 | custom fusion | bytes 5243200 | tf_op jit(solution)/shard_map/gather | solution.py:34
  80.0 5.4 %multiply_bitcast_fusion = f32[80,128,128]{1,2,0:T(8,128)} fusion(f32[80]{0:T(128)S(1)} %compare_convert_fusion, bf16[80,128,128]{2,1,0:T(8,128)(2,1)} %gather_fusion.1, bf16[80,128,128]{2,1,0:T(8,128)(2,1)S(1)} %copy-done), kind=kOutput, calls=%fused_computation.4 | convolution fusion | flops 336855040 | bytes 10486080 | tf_op jit(solution)/shard_map/tij,tif->tjf/dot_general | solution.py:34
  85.4 5.9 %copy.37 = f32[80,128,128]{2,1,0:T(8,128)} copy(f32[80,128,128]{1,2,0:T(8,128)} %multiply_bitcast_fusion) | data formatting | bytes 10485760 | tf_op jit(solution)/shard_map/mul | solution.py:34
  91.3 1.1 broadcast_in_dim.19
  92.4 16.5 %scatter_fusion.1 = f32[16,128,128]{2,1,0:T(8,128)} fusion(f32[16,128,128]{2,1,0:T(8,128)} %broadcast_in_dim.19, s32[80]{0:T(128)S(1)} %copy-done.4, f32[80,128,128]{2,1,0:T(8,128)} %copy.37), kind=kCustom, calls=%fused_computation.3 | custom fusion | flops 1310720 | bytes 15728960 | tf_op jit(solution)/shard_map/scatter-add | solution.py:37
  108.9 2.6 %copy.47 = f32[2048,128]{0,1:T(8,128)} copy(f32[2048,128]{1,0:T(8,128)} %bitcast.29) | data formatting | bytes 2097152 | tf_op jit(solution)/shard_map/reshape | solution.py:39
  111.6 26.9 %reduce-scatter.3.cloned.1.call-done = f32[512,128]{0,1:T(8,128)} async-done(((f32[2048,128]{0,1:T(8,128)}), f32[512,128]{0,1:T(8,128)}) %reduce-scatter.3.cloned.1.call-update) | async-done | bytes 262160 | tf_op jit(solution)/shard_map/reduce_scatter | solution.py:38
  138.4 1.0 convert_element_type.30
  139.4 2.7 %convolution_bitcast_fusion.1 = f32[1024,256]{0,1:T(8,128)} fusion(bf16[512,1024]{1,0:T(8,128)(2,1)} %all-gather.2.cloned.1.call-done, bf16[512,128]{0,1:T(8,128)(2,1)S(1)} %multiply_convert_fusion, bf16[512,128]{0,1:T(8,128)(2,1)S(1)} %convert_element_type.30), kind=kOutput, calls=%fused_computation.6 | convolution fusion | flops 268959744 | bytes 2359296 | tf_op jit(solution)/shard_map/dot_general | solution.py:46
  142.2 1.8 fusion
  144.0 50.8 %all-reduce.2.cloned.1.call-done = f32[1024,256]{0,1:T(8,128)} async-done(((f32[1024,256]{0,1:T(8,128)}), f32[1024,256]{0,1:T(8,128)}) %all-reduce.2.cloned.1.call-update) | async-done | bytes 1048592 | tf_op jit(solution)/shard_map/psum | solution.py:49
  194.8 2.1 fusion.4
  196.9 2.0 copy.40
  198.9 1.0 copy.41
  199.9 33.0 %reduce-scatter.5.cloned.1.call-done = f32[128,512]{1,0:T(8,128)} async-done(((f32[1024,512]{1,0:T(8,128)}), f32[128,512]{1,0:T(8,128)}) %reduce-scatter.5.cloned.1.call-update) | async-done | bytes 262160 | tf_op jit(solution)/shard_map/reduce_scatter | solution.py:50
  232.9 1.0 convert_bitcast_fusion
  233.8 0.8 copy.39
  (27 shorter events, 1.3 us)
Async XLA Ops:
  7.2 46.1 %copy-start = (bf16[80,128,128]{2,1,0:T(8,128)(2,1)S(1)}, bf16[80,128,128]{2,1,0:T(8,128)(2,1)}, u32[]{:S(2)}) copy-start(bf16[80,128,128]{2,1,0:T(8,128)(2,1)} %param.13) | copy-start | bytes 7864324
  7.2 29.1 %all-gather.2.cloned.1.call-start = ((), (), s32[]{:S(2)}) async-start(), calls=%async_computation.2 | async-start | bytes 1179648 | tf_op jit(solution)/shard_map/all_gather | solution.py:14
  7.9 130.5 %reduce-scatter.3.cloned.1.call-start = ((), (), s32[]{:S(2)}) async-start(), calls=%async_computation.3 | async-start | bytes 1310720 | tf_op jit(solution)/shard_map/reduce_scatter | solution.py:38
  12.6 25.5 %copy-start.1 = (bf16[1024,256]{1,0:T(8,128)(2,1)}, bf16[1024,256]{1,0:T(8,128)(2,1)S(1)}, u32[]{:S(2)}) copy-start(bf16[1024,256]{1,0:T(8,128)(2,1)S(1)} %constant_dynamic-update-slice_fusion) | copy-start | bytes 1572868
  38.0 0.8 copy-start.3
  85.4 7.1 %copy-start.4 = (s32[80]{0:T(128)S(1)}, s32[80]{0:T(128)}, u32[]{:S(2)}) copy-start(s32[80]{0:T(128)} %param.12) | copy-start | bytes 964
  111.5 30.7 %copy-start.2 = (bf16[1024,256]{1,0:T(8,128)(2,1)S(1)}, bf16[1024,256]{1,0:T(8,128)(2,1)}, u32[]{:S(2)}) copy-start(bf16[1024,256]{1,0:T(8,128)(2,1)} %copy-done.1) | copy-start | bytes 1572868
  111.5 83.3 %all-reduce.2.cloned.1.call-start = ((), (), s32[]{:S(2)}) async-start(), calls=%async_computation.5 | async-start | bytes 2097152 | tf_op jit(solution)/shard_map/psum | solution.py:49
  142.1 90.8 %reduce-scatter.5.cloned.1.call-start = ((), (), s32[]{:S(2)}) async-start(), calls=%async_computation.4 | async-start | bytes 2359296 | tf_op jit(solution)/shard_map/reduce_scatter | solution.py:50
Sparse Core Ops, SparseCore 0:
  9.6 26.6 all-gather.1
  111.6 26.7 reduce-scatter.2
  142.2 52.5 all-reduce.1
  197.0 35.7 reduce-scatter.4
where the time goes:
time: 242 us; the launch traced here: 241 us
  waiting for transfers between devices  135 us (56%)
  local copies, waits for them, and re-layouts  31.9 us (13%)
  other arithmetic  31.9 us (13%)
  matrix products  17.5 us (7%)
  between operations  13.9 us (6%)
  blocking collectives  10.5 us (4%)
    psum x1, waiting for transfers between devices, on_device(): weight_sums = lax.psum(local_weights, 'rows')  50.8 us
    reduce_scatter x1, waiting for transfers between devices, on_device(): lax.psum_scatter(lax.dot_general(weights_cat, grads_cat, (((1,), (1,)), (...  33 us
    reduce_scatter x1, waiting for transfers between devices, on_device(): lax.psum_scatter(partial_grads.reshape(all_blocks * tile, width_part), 'r...  26.9 us
    all_gather x1, waiting for transfers between devices, on_device(): whole_feats = lax.all_gather(node_feats, 'feat', axis=1, tiled=True)  23.7 us
    scatter-add x1, other arithmetic, on_device(): jax.ops.segment_sum(contrib, tile_cols, num_segments=all_blocks)  16.5 us
    scatter-add x1, other arithmetic, on_device(): jax.ops.segment_sum(prod, owner, num_segments=nblocks + 1)[:nblocks]  10.8 us
    all_gather x1, blocking collectives, on_device(): gathered = lax.all_gather(hidden, 'rows', axis=0, tiled=True)  10.5 us
    unnamed x15, local copies, waits for them, and re-layouts  6.56 us
  transfers between devices with their start and end apart: 4, of which 4 were waited for; matrix products, arithmetic and copies ran while one was open for 5% of the time, Pallas kernels for 0%

commit v1 on v0

v1 whole, which is shorter than its diff:
```python
import functools

import jax
import jax.numpy as jnp
from jax import lax
from jax.experimental import pallas as pl
from jax.experimental.pallas import tpu as pltpu
from jax.sharding import PartitionSpec as P

BF = jnp.bfloat16
F32 = jnp.float32
VMEM = pl.BlockSpec(memory_space=pltpu.VMEM)
SMEM = pl.BlockSpec(memory_space=pltpu.SMEM)


def dot(a, b):
    return jnp.dot(a, b, preferred_element_type=F32)


def dot_nt(a, b):
    return lax.dot_general(a, b, (((1,), (1,)), ((), ())), preferred_element_type=F32)


def call(body, outs, specs, args, flops=0, scratch=(), limit=None):
    moved = sum(a.size * a.dtype.itemsize for a in args)
    moved += sum(o.size * o.dtype.itemsize for o in outs)
    return pl.pallas_call(
        body,
        out_shape=outs,
        in_specs=specs,
        out_specs=[VMEM] * len(outs),
        scratch_shapes=scratch,
        compiler_params=pltpu.CompilerParams(vmem_limit_bytes=limit or 32 * 1024 * 1024),
        cost_estimate=pl.CostEstimate(flops=flops, bytes_accessed=moved, transcendentals=0),
    )(*args)


def sds(shape, dtype):
    return jax.ShapeDtypeStruct(shape, dtype)


def assemble_kernel(counts, cols, vals, adj, adj_t, acc):
    nblocks = counts.shape[0]
    tile = vals.shape[1]
    all_blocks = adj.shape[1] // tile
    acc[...] = jnp.zeros_like(acc)
    start = jnp.int32(0)
    for b in range(nblocks):
        rows = slice(b * tile, (b + 1) * tile)

        def add(t, carry, rows=rows):
            place = pl.ds(pl.multiple_of(cols[t] * tile, tile), tile)
            acc[rows, place] += vals[t].astype(F32)
            return carry

        end = start + counts[b]
        lax.fori_loop(start, end, add, 0)
        start = end

    def finish(c, carry):
        place = pl.ds(pl.multiple_of(c * tile, tile), tile)
        block = acc[:, place]
        adj[:, place] = block.astype(BF)
        adj_t[place, :] = block.T.astype(BF)
        return carry

    lax.fori_loop(0, all_blocks, finish, 0)


def forward_kernel(nf, *refs):
    pieces, (weight, root, hidden, own) = refs[:nf], refs[nf:]
    me = lax.axis_index("feat")
    width = weight.shape[1]
    total = None
    for k in range(nf // 2):
        even = pl.ds(pl.multiple_of((me ^ (2 * k)) * width, width), width)
        odd = pl.ds(pl.multiple_of((me ^ (2 * k + 1)) * width, width), width)
        left = jnp.concatenate([pieces[2 * k][...], pieces[2 * k + 1][...]], 1)
        right = jnp.concatenate(
            [
                jnp.concatenate([weight[even, :], root[even, :]], 1),
                jnp.concatenate([weight[odd, :], root[odd, :]], 1),
            ],
            0,
        )
        part = dot(left, right)
        total = part if total is None else total + part
    hidden[...] = total[:, :width].astype(BF)
    own[...] = total[:, width:]


def transpose_kernel(nf, *refs):
    pieces, out = refs[:nf], refs[nf]
    me = lax.axis_index("feat")
    width = pieces[0].shape[1]
    for m in range(nf):
        rows = pl.ds(pl.multiple_of((me ^ m) * width, width), width)
        out[rows, :] = pieces[m][...].T


def aggregate_kernel(nr, *refs):
    hidden = refs[:nr]
    adj, adj_t, own, grad_out, grad_pre, kept = refs[nr : nr + 6]
    sent = refs[nr + 6 :]
    me = lax.axis_index("rows")
    rows = own.shape[0]
    pre = own[...]
    for j in range(nr):
        place = pl.ds(pl.multiple_of((me ^ j) * rows, rows), rows)
        pre = pre + dot(adj[:, place], hidden[j][...])
    sig = jax.nn.sigmoid(pre)
    grad = (grad_out[...].astype(F32) * sig * (1.0 + pre * (1.0 - sig))).astype(BF)
    grad_pre[...] = grad
    for j in range(nr):
        place = pl.ds(pl.multiple_of((me ^ j) * rows, rows), rows)
        part = dot(adj_t[place, :], grad)
        if j == 0:
            kept[...] = part
        else:
            sent[j - 1][...] = part.astype(BF)


def sum_kernel(n, *refs):
    total = refs[0][...].astype(F32)
    for ref in refs[1:n]:
        total = total + ref[...].astype(F32)
    refs[n][...] = total.astype(refs[n].dtype)


def feats_kernel(nz, hidden, pre, hidden_2, pre_2, weight, root, weight_2, root_2, kept, *sent):
    me = lax.axis_index("feat")
    width = weight.shape[1]
    left = jnp.concatenate([hidden[...], pre[...], hidden_2[...], pre_2[...]], 1)
    for k in range(nz):
        rows = pl.ds(pl.multiple_of((me ^ (2 * k)) * width, width), width)
        right = jnp.concatenate(
            [weight[rows, :], root[rows, :], weight_2[rows, :], root_2[rows, :]], 1
        )
        part = dot_nt(left, right)
        if k == 0:
            kept[...] = part
        else:
            sent[k - 1][...] = part.astype(BF)


def weights_kernel(nr, feats_t, hidden, pre, kept, *rest):
    sent, whole = rest[:-1], rest[-1]
    me = lax.axis_index("rows")
    share = kept.shape[0]
    whole[...] = dot(feats_t[...], jnp.concatenate([hidden[...], pre[...]], 1))
    for j in range(nr):
        part = whole[pl.ds(pl.multiple_of((me ^ j) * share, share), share), :]
        if j == 0:
            kept[...] = part
        else:
            sent[j - 1][...] = part.astype(BF)


def place_kernel(nr, *refs):
    pieces, (weight, root) = refs[:nr], refs[nr:]
    me = lax.axis_index("rows")
    share, width = pieces[0].shape[0], weight.shape[1]
    for j in range(nr):
        rows = pl.ds(pl.multiple_of((me ^ j) * share, share), share)
        block = pieces[j][...].astype(F32)
        weight[rows, :] = block[:, :width]
        root[rows, :] = block[:, width:]


def on_device(node_feats, weight, root_weight, grad_out, block_counts, tile_cols, tile_vals):
    rows, width = node_feats.shape
    depth = weight.shape[0]
    nr, nf = lax.axis_size("rows"), lax.axis_size("feat")
    nz = nf // 2
    nodes = rows * nr
    share = depth // nr

    def swap(array, axis, mask):
        return lax.ppermute(array, axis, [(i, i ^ mask) for i in range(lax.axis_size(axis))])

    mine = [node_feats] + [swap(node_feats, "feat", 2 * k) for k in range(1, nz)]
    pieces = []
    for piece in mine:
        pieces += [piece, swap(piece, "feat", 1)]
    weight_2, root_2 = swap(weight, "feat", 1), swap(root_weight, "feat", 1)

    adj, adj_t = call(
        assemble_kernel,
        [sds((rows, nodes), BF), sds((nodes, rows), BF)],
        [SMEM, SMEM, VMEM],
        (block_counts, tile_cols, tile_vals),
        flops=4 * rows * nodes,
        scratch=[pltpu.VMEM((rows, nodes), F32)],
        limit=16 * rows * nodes,
    )
    hidden, own = call(
        functools.partial(forward_kernel, nf),
        [sds((rows, width), BF), sds((rows, width), F32)],
        [VMEM] * (nf + 2),
        (*pieces, weight, root_weight),
        flops=4 * rows * depth * width,
    )
    gathered = [hidden] + [swap(hidden, "rows", j) for j in range(1, nr)]
    (feats_t,) = call(
        functools.partial(transpose_kernel, nf),
        [sds((depth, rows), BF)],
        [VMEM] * nf,
        pieces,
    )
    grad_pre, kept, *sent = call(
        functools.partial(aggregate_kernel, nr),
        [sds((rows, width), BF), sds((rows, width), F32)] + [sds((rows, width), BF)] * (nr - 1),
        [VMEM] * (nr + 4),
        (*gathered, adj, adj_t, own, grad_out),
        flops=4 * rows * nodes * width,
        limit=max(32 * 1024 * 1024, 10 * rows * nodes),
    )
    pre_2 = swap(grad_pre, "feat", 1)
    sums = [kept] + [swap(part, "rows", j + 1) for j, part in enumerate(sent)]
    (grad_hidden,) = call(
        functools.partial(sum_kernel, nr), [sds((rows, width), BF)], [VMEM] * nr, sums
    )
    hidden_2 = swap(grad_hidden, "feat", 1)
    kept_w, *sent_w = call(
        functools.partial(weights_kernel, nr),
        [sds((share, 2 * width), F32)] + [sds((share, 2 * width), BF)] * (nr - 1),
        [VMEM] * 3,
        (feats_t, grad_hidden, grad_pre),
        flops=4 * rows * depth * width,
        scratch=[pltpu.VMEM((depth, 2 * width), F32)],
    )
    kept_f, *sent_f = call(
        functools.partial(feats_kernel, nz),
        [sds((rows, width), F32)] + [sds((rows, width), BF)] * (nz - 1),
        [VMEM] * 8,
        (grad_hidden, grad_pre, hidden_2, pre_2, weight, root_weight, weight_2, root_2),
        flops=4 * rows * depth * width,
    )
    sums_f = [kept_f] + [swap(part, "feat", 2 * (k + 1)) for k, part in enumerate(sent_f)]
    sums_w = [kept_w] + [swap(part, "rows", j + 1) for j, part in enumerate(sent_w)]
    (shared,) = call(
        functools.partial(sum_kernel, nr), [sds((share, 2 * width), BF)], [VMEM] * nr, sums_w
    )
    all_shared = [shared] + [swap(shared, "rows", j) for j in range(1, nr)]
    grad_weight, grad_root = call(
        functools.partial(place_kernel, nr),
        [sds((depth, width), F32)] * 2,
        [VMEM] * nr,
        all_shared,
    )
    (grad_feats,) = call(
        functools.partial(sum_kernel, nz), [sds((rows, width), BF)], [VMEM] * nz, sums_f
    )
    return grad_feats, grad_weight, grad_root


def solution(mesh):
    placed = (
        P("rows", "feat"),
        P(None, "feat"),
        P(None, "feat"),
        P("rows", "feat"),
        P("rows"),
        P("rows"),
        P("rows", None, None),
    )
    return jax.shard_map(
        on_device,
        mesh=mesh,
        in_specs=placed,
        out_specs=(P("rows", "feat"), P(None, "feat"), P(None, "feat")),
        check_vma=False,
    )
```

time: 242 us -> 71.5 us (0.30)
  waiting for transfers between devices: 135 us -> 30.4 us
  other arithmetic: 31.9 us -> 0 us
  local copies, waits for them, and re-layouts: 31.9 us -> 5.87 us
  starting transfers between devices: 0.16 us -> 25.7 us
  matrix products: 17.5 us -> 0 us
  between operations: 13.9 us -> 0.75 us
  blocking collectives: 10.5 us -> 0 us
  Pallas kernels: 0 us -> 9.34 us
    reduce_scatter x2 -> x0, waiting for transfers between devices: 59.8 us -> none  [the longest x1 33 us: on_device(): lax.psum_scatter(lax.dot_general(weights_cat, grads_cat, (((1,), (1,)), (...]
    psum x1 -> x0, waiting for transfers between devices: 50.8 us -> none  [on_device(): weight_sums = lax.psum(local_weights, 'rows')]
    ppermute x0 -> x26, waiting for transfers between devices: none -> 30.4 us  [swap(): lax.ppermute(array, axis, [(i, i ^ mask) for i in range(lax.axis_size(axi...]
    scatter-add x2 -> x0, other arithmetic: 27.3 us -> none  [the longest x1 16.5 us: on_device(): jax.ops.segment_sum(contrib, tile_cols, num_segments=all_blocks)]
    ppermute x0 -> x26, starting transfers between devices: none -> 25.7 us  [swap(): lax.ppermute(array, axis, [(i, i ^ mask) for i in range(lax.axis_size(axi...]
    all_gather x1 -> x0, waiting for transfers between devices: 23.7 us -> none  [on_device(): whole_feats = lax.all_gather(node_feats, 'feat', axis=1, tiled=True)]
    dot_general x5 -> x0, matrix products: 17.5 us -> none  [the longest x1 6.03 us: on_device(): jnp.einsum('tij,tjf->tif', tile_vals, hblocks[tile_cols], preferred_eleme...]
    all_gather x1 -> x0, blocking collectives: 10.5 us -> none  [on_device(): gathered = lax.all_gather(hidden, 'rows', axis=0, tiled=True)]
  transfers between devices with their start and end apart: 4 -> 26, of which waited for: 4 -> 12; matrix products, arithmetic and copies ran while one was open for 5% -> 0% of each run, Pallas kernels for 0% -> 8%
where the time goes in v1:
time: 71.5 us; the launch traced here: 72 us
  waiting for transfers between devices  30.4 us (43%)
  starting transfers between devices  25.7 us (36%)
  Pallas kernels  9.34 us (13%)
  local copies, waits for them, and re-layouts  5.87 us (8%)
  between operations  0.75 us (1%)
    ppermute x26, waiting for transfers between devices, swap(): lax.ppermute(array, axis, [(i, i ^ mask) for i in range(lax.axis_size(axi...  30.4 us
    ppermute x26, starting transfers between devices, swap(): lax.ppermute(array, axis, [(i, i ^ mask) for i in range(lax.axis_size(axi...  25.7 us
    pallas_call x10, Pallas kernels, call(): pl.pallas_call(body, out_shape=outs, in_specs=specs, out_specs=[VMEM] * l...  9.34 us
    unnamed x20, local copies, waits for them, and re-layouts  5.87 us
  transfers between devices with their start and end apart: 26, of which 12 were waited for; matrix products, arithmetic and copies ran while one was open for 0% of the time, Pallas kernels for 8%

profile of v1, /device:TPU:0, one launch (start us, length us, event | category | flops | bytes accessed | tf_op | source)
XLA Modules:
  0.0 72.0 jit_solution(16597728316604122883)
XLA Ops:
  0.6 3.1 %collective-permute-start.1 = (bf16[512,128]{1,0:T(8,128)(2,1)}, bf16[512,128]{1,0:T(8,128)(2,1)S(1)}, u32[]{:S(2)}, u32[]{:S(2)}) collective-permute-start(bf16[512,128]{1,0:T(8,128)(2,1)} %refs_0_.3), channel_id=1, source_target_pairs={{0,2},{1,3},{2,0},{3,1},{4,6},{5,7},{6,4},{7,5},{8,10},{9,11},{10,... | collective-permute-start | bytes 393224 | tf_op jit(solution)/shard_map/ppermute | solution.py:179
  3.7 2.6 %collective-permute-start.3 = (bf16[512,128]{1,0:T(8,128)(2,1)}, bf16[512,128]{1,0:T(8,128)(2,1)S(1)}, u32[]{:S(2)}, u32[]{:S(2)}) collective-permute-start(bf16[512,128]{1,0:T(8,128)(2,1)} %refs_0_.3), channel_id=1, source_target_pairs={{0,4},{1,5},{2,6},{3,7},{4,0},{5,1},{6,2},{7,3},{8,12},{9,13},{10,... | collective-permute-start | bytes 393224 | tf_op jit(solution)/shard_map/ppermute | solution.py:179
  6.3 2.7 %collective-permute-done.1.refs_2_ = bf16[512,128]{1,0:T(8,128)(2,1)S(1)} collective-permute-done((bf16[512,128]{1,0:T(8,128)(2,1)}, bf16[512,128]{1,0:T(8,128)(2,1)S(1)}, u32[]{:S(2)}, u32[]{:S(2)}) %collective-permute-start.1) | collective-permute-done | bytes 131104 | tf_op jit(solution)/shard_map/ppermute | solution.py:179
  9.0 7.9 %collective-permute-done.3.refs_4_ = bf16[512,128]{1,0:T(8,128)(2,1)S(1)} collective-permute-done((bf16[512,128]{1,0:T(8,128)(2,1)}, bf16[512,128]{1,0:T(8,128)(2,1)S(1)}, u32[]{:S(2)}, u32[]{:S(2)}) %collective-permute-start.3) | collective-permute-done | bytes 131104 | tf_op jit(solution)/shard_map/ppermute | solution.py:179
  17.4 0.8 %collective-permute-done.4.refs_5_ = bf16[512,128]{1,0:T(8,128)(2,1)S(1)} collective-permute-done((bf16[512,128]{1,0:T(8,128)(2,1)S(1)}, bf16[512,128]{1,0:T(8,128)(2,1)S(1)}, u32[]{:S(2)}, u32[]{:S(2)}) %collective-permute-start.4) | collective-permute-done | bytes 131104 | tf_op jit(solution)/shard_map/ppermute | solution.py:179
  18.4 0.9 %copy-done.1 = bf16[1024,128]{1,0:T(8,128)(2,1)S(1)} copy-done((bf16[1024,128]{1,0:T(8,128)(2,1)S(1)}, bf16[1024,128]{1,0:T(8,128)(2,1)}, u32[]{:S(2)}) %copy-start.1) | copy-done | bytes 262168
  19.4 0.9 %copy-done.3 = bf16[1024,128]{1,0:T(8,128)(2,1)S(1)} copy-done((bf16[1024,128]{1,0:T(8,128)(2,1)S(1)}, bf16[1024,128]{1,0:T(8,128)(2,1)}, u32[]{:S(2)}) %copy-start.3) | copy-done | bytes 262168
  20.3 0.9 %copy-done.5 = bf16[512,128]{1,0:T(8,128)(2,1)S(1)} copy-done((bf16[512,128]{1,0:T(8,128)(2,1)S(1)}, bf16[512,128]{1,0:T(8,128)(2,1)}, u32[]{:S(2)}) %copy-start.5) | copy-done | bytes 131096
  21.7 1.6 %collective-permute-start.7 = (bf16[512,128]{1,0:T(8,128)(2,1)S(1)}, bf16[512,128]{1,0:T(8,128)(2,1)S(1)}, u32[]{:S(2)}, u32[]{:S(2)}) collective-permute-start(bf16[512,128]{1,0:T(8,128)(2,1)S(1)} %get-tuple-element.22.refs_0_), channel_id=1, source_target_pairs={{0,8},{8,0},{16,24},{24,16},{1,9},{9,1},{17,25},{25,17},{2,10},{10... | collective-permute-start | bytes 393224 | tf_op jit(solution)/shard_map/ppermute | solution.py:179
  23.2 1.5 %collective-permute-start.8 = (bf16[512,128]{1,0:T(8,128)(2,1)S(1)}, bf16[512,128]{1,0:T(8,128)(2,1)S(1)}, u32[]{:S(2)}, u32[]{:S(2)}) collective-permute-start(bf16[512,128]{1,0:T(8,128)(2,1)S(1)} %get-tuple-element.22.refs_0_), channel_id=1, source_target_pairs={{0,16},{8,24},{16,0},{24,8},{1,17},{9,25},{17,1},{25,9},{2,18},{10... | collective-permute-start | bytes 393224 | tf_op jit(solution)/shard_map/ppermute | solution.py:179
  25.2 1.7 %copy-done = bf16[80,128,128]{2,1,0:T(8,128)(2,1)S(1)} copy-done((bf16[80,128,128]{2,1,0:T(8,128)(2,1)S(1)}, bf16[80,128,128]{2,1,0:T(8,128)(2,1)}, u32[]{:S(2)}) %copy-start) | copy-done | bytes 2621464
  28.3 3.1 %shard_map.95 = (bf16[512,2048]{1,0:T(8,128)(2,1)S(1)}, bf16[2048,512]{1,0:T(8,128)(2,1)S(1)}) custom-call(s32[4]{0:T(128)S(1)} %copy-done.8, s32[80]{0:T(128)S(1)} %copy-done.9, bf16[80,128,128]{2,1,0:T(8,128)(2,1)S(1)} %copy-done), custom_call_target="tpu_custom_call" | custom-call | flops 4194304 | bytes 6816080 | tf_op jit(solution)/shard_map/pallas_call | solution.py:27
  31.5 2.4 %shard_map.96 = (bf16[512,128]{1,0:T(8,128)(2,1)S(1)}, f32[512,128]{1,0:T(8,128)S(1)}, bf16[512,128]{1,0:T(8,128)(2,1)S(1)}, bf16[512,128]{1,0:T(8,128)(2,1)S(1)}, bf16[512,128]{1,0:T(8,128)(2,1)S(1)}) custom-call(bf16[512,128]{1,0:T(8,128)(2,1)S(1)} %get-tuple-element.22.refs_0_, bf16[512,128]{1,0:T(8,128)(2,1)S(1)} %collective-permute-done.7.refs_1_, ...), custom_call_target="tpu_custom_call" | custom-call | flops 536870912 | bytes 5898240 | tf_op jit(solution)/shard_map/pallas_call | solution.py:27
  33.9 1.7 %collective-permute-start.10 = (bf16[512,128]{1,0:T(8,128)(2,1)S(1)}, bf16[512,128]{1,0:T(8,128)(2,1)S(1)}, u32[]{:S(2)}, u32[]{:S(2)}) collective-permute-start(bf16[512,128]{1,0:T(8,128)(2,1)S(1)} %get-tuple-element.27), channel_id=1, source_target_pairs={{0,8},{8,0},{16,24},{24,16},{1,9},{9,1},{17,25},{25,17},{2,10},{10... | collective-permute-start | bytes 393224 | tf_op jit(solution)/shard_map/ppermute | solution.py:179
  35.6 2.2 %collective-permute-start.11 = (bf16[512,128]{1,0:T(8,128)(2,1)S(1)}, bf16[512,128]{1,0:T(8,128)(2,1)S(1)}, u32[]{:S(2)}, u32[]{:S(2)}) collective-permute-start(bf16[512,128]{1,0:T(8,128)(2,1)S(1)} %get-tuple-element.28), channel_id=1, source_target_pairs={{0,16},{8,24},{16,0},{24,8},{1,17},{9,25},{17,1},{25,9},{2,18},{10... | collective-permute-start | bytes 393224 | tf_op jit(solution)/shard_map/ppermute | solution.py:179
  39.1 3.6 %collective-permute-done.11.refs_2_ = bf16[512,128]{1,0:T(8,128)(2,1)S(1)} collective-permute-done((bf16[512,128]{1,0:T(8,128)(2,1)S(1)}, bf16[512,128]{1,0:T(8,128)(2,1)S(1)}, u32[]{:S(2)}, u32[]{:S(2)}) %collective-permute-start.11) | collective-permute-done | bytes 131104 | tf_op jit(solution)/shard_map/ppermute | solution.py:179
  42.7 0.9 %collective-permute-done.12.refs_3_ = bf16[512,128]{1,0:T(8,128)(2,1)S(1)} collective-permute-done((bf16[512,128]{1,0:T(8,128)(2,1)S(1)}, bf16[512,128]{1,0:T(8,128)(2,1)S(1)}, u32[]{:S(2)}, u32[]{:S(2)}) %collective-permute-start.12) | collective-permute-done | bytes 131104 | tf_op jit(solution)/shard_map/ppermute | solution.py:179
  44.2 1.3 %collective-permute-start.20 = (bf16[256,256]{1,0:T(8,128)(2,1)S(1)}, bf16[256,256]{1,0:T(8,128)(2,1)S(1)}, u32[]{:S(2)}, u32[]{:S(2)}) collective-permute-start(bf16[256,256]{1,0:T(8,128)(2,1)S(1)} %get-tuple-element.36), channel_id=1, source_target_pairs={{0,8},{8,0},{16,24},{24,16},{1,9},{9,1},{17,25},{25,17},{2,10},{10... | collective-permute-start | bytes 393224 | tf_op jit(solution)/shard_map/ppermute | solution.py:179
  46.2 1.5 %collective-permute-start.22 = (bf16[256,256]{1,0:T(8,128)(2,1)S(1)}, bf16[256,256]{1,0:T(8,128)(2,1)S(1)}, u32[]{:S(2)}, u32[]{:S(2)}) collective-permute-start(bf16[256,256]{1,0:T(8,128)(2,1)S(1)} %get-tuple-element.38), channel_id=1, source_target_pairs={{0,24},{8,16},{16,8},{24,0},{1,25},{9,17},{17,9},{25,1},{2,26},{10... | collective-permute-start | bytes 393224 | tf_op jit(solution)/shard_map/ppermute | solution.py:179
  47.7 2.4 %collective-permute-done.20.refs_1_ = bf16[256,256]{1,0:T(8,128)(2,1)S(1)} collective-permute-done((bf16[256,256]{1,0:T(8,128)(2,1)S(1)}, bf16[256,256]{1,0:T(8,128)(2,1)S(1)}, u32[]{:S(2)}, u32[]{:S(2)}) %collective-permute-start.20) | collective-permute-done | bytes 131104 | tf_op jit(solution)/shard_map/ppermute | solution.py:179
  50.1 2.5 %collective-permute-done.21.refs_2_ = bf16[256,256]{1,0:T(8,128)(2,1)S(1)} collective-permute-done((bf16[256,256]{1,0:T(8,128)(2,1)S(1)}, bf16[256,256]{1,0:T(8,128)(2,1)S(1)}, u32[]{:S(2)}, u32[]{:S(2)}) %collective-permute-start.21) | collective-permute-done | bytes 131104 | tf_op jit(solution)/shard_map/ppermute | solution.py:179
  52.7 1.5 %collective-permute-start.23 = (bf16[256,256]{1,0:T(8,128)(2,1)S(1)}, bf16[256,256]{1,0:T(8,128)(2,1)S(1)}, u32[]{:S(2)}, u32[]{:S(2)}) collective-permute-start(bf16[256,256]{1,0:T(8,128)(2,1)S(1)} %shard_map.102.refs_0_), channel_id=1, source_target_pairs={{0,8},{8,0},{16,24},{24,16},{1,9},{9,1},{17,25},{25,17},{2,10},{10... | collective-permute-start | bytes 393224 | tf_op jit(solution)/shard_map/ppermute | solution.py:179
  54.2 0.8 %collective-permute-start.24 = (bf16[256,256]{1,0:T(8,128)(2,1)S(1)}, bf16[256,256]{1,0:T(8,128)(2,1)S(1)}, u32[]{:S(2)}, u32[]{:S(2)}) collective-permute-start(bf16[256,256]{1,0:T(8,128)(2,1)S(1)} %shard_map.102.refs_0_), channel_id=1, source_target_pairs={{0,16},{8,24},{16,0},{24,8},{1,17},{9,25},{17,1},{25,9},{2,18},{10... | collective-permute-start | bytes 393224 | tf_op jit(solution)/shard_map/ppermute | solution.py:179
  54.9 1.3 %collective-permute-start.25 = (bf16[256,256]{1,0:T(8,128)(2,1)S(1)}, bf16[256,256]{1,0:T(8,128)(2,1)S(1)}, u32[]{:S(2)}, u32[]{:S(2)}) collective-permute-start(bf16[256,256]{1,0:T(8,128)(2,1)S(1)} %shard_map.102.refs_0_), channel_id=1, source_target_pairs={{0,24},{8,16},{16,8},{24,0},{1,25},{9,17},{17,9},{25,1},{2,26},{10... | collective-permute-start | bytes 393224 | tf_op jit(solution)/shard_map/ppermute | solution.py:179
  56.2 0.7 shard_map.98
  56.9 1.6 %collective-permute-start.17 = (bf16[512,128]{1,0:T(8,128)(2,1)S(1)}, bf16[512,128]{1,0:T(8,128)(2,1)S(1)}, u32[]{:S(2)}, u32[]{:S(2)}) collective-permute-start(bf16[512,128]{1,0:T(8,128)(2,1)S(1)} %get-tuple-element.32), channel_id=1, source_target_pairs={{0,2},{1,3},{2,0},{3,1},{4,6},{5,7},{6,4},{7,5},{8,10},{9,11},{10,... | collective-permute-start | bytes 393224 | tf_op jit(solution)/shard_map/ppermute | solution.py:179
  58.5 1.3 %collective-permute-start.18 = (bf16[512,128]{1,0:T(8,128)(2,1)S(1)}, bf16[512,128]{1,0:T(8,128)(2,1)S(1)}, u32[]{:S(2)}, u32[]{:S(2)}) collective-permute-start(bf16[512,128]{1,0:T(8,128)(2,1)S(1)} %get-tuple-element.33), channel_id=1, source_target_pairs={{0,4},{1,5},{2,6},{3,7},{4,0},{5,1},{6,2},{7,3},{8,12},{9,13},{10,... | collective-permute-start | bytes 393224 | tf_op jit(solution)/shard_map/ppermute | solution.py:179
  59.9 1.5 %collective-permute-start.19 = (bf16[512,128]{1,0:T(8,128)(2,1)S(1)}, bf16[512,128]{1,0:T(8,128)(2,1)S(1)}, u32[]{:S(2)}, u32[]{:S(2)}) collective-permute-start(bf16[512,128]{1,0:T(8,128)(2,1)S(1)} %get-tuple-element.34), channel_id=1, source_target_pairs={{0,6},{1,7},{2,4},{3,5},{4,2},{5,3},{6,0},{7,1},{8,14},{9,15},{10,... | collective-permute-start | bytes 393224 | tf_op jit(solution)/shard_map/ppermute | solution.py:179
  61.4 1.2 %collective-permute-done.24.refs_2_ = bf16[256,256]{1,0:T(8,128)(2,1)S(1)} collective-permute-done((bf16[256,256]{1,0:T(8,128)(2,1)S(1)}, bf16[256,256]{1,0:T(8,128)(2,1)S(1)}, u32[]{:S(2)}, u32[]{:S(2)}) %collective-permute-start.24) | collective-permute-done | bytes 131104 | tf_op jit(solution)/shard_map/ppermute | solution.py:179
  62.6 1.0 %shard_map.103 = (f32[1024,128]{1,0:T(8,128)}, f32[1024,128]{1,0:T(8,128)}) custom-call(bf16[256,256]{1,0:T(8,128)(2,1)S(1)} %shard_map.102.refs_0_, bf16[256,256]{1,0:T(8,128)(2,1)S(1)} %collective-permute-done.23.refs_1_, bf16[256,256]{1,0:T(8,128)(2,1)S(1)} %collective-permute-done.24.refs_2_, bf16[256,256]{1,0:T(8,128)(2,1)S(1)} %collective-permute-done.25.refs_3_), custom_call_target="tpu_custom_call" | custom-call | bytes 1572864 | tf_op jit(solution)/shard_map/pallas_call | solution.py:27
  63.6 7.6 %collective-permute-done.18.refs_2_ = bf16[512,128]{1,0:T(8,128)(2,1)S(1)} collective-permute-done((bf16[512,128]{1,0:T(8,128)(2,1)S(1)}, bf16[512,128]{1,0:T(8,128)(2,1)S(1)}, u32[]{:S(2)}, u32[]{:S(2)}) %collective-permute-start.18) | collective-permute-done | bytes 131104 | tf_op jit(solution)/shard_map/ppermute | solution.py:179
  71.3 0.7 shard_map.99
  (50 shorter events, 5.7 us)
Async XLA Ops:
  0.6 8.3 %collective-permute-start.1 = (bf16[512,128]{1,0:T(8,128)(2,1)}, bf16[512,128]{1,0:T(8,128)(2,1)S(1)}, u32[]{:S(2)}, u32[]{:S(2)}) collective-permute-start(bf16[512,128]{1,0:T(8,128)(2,1)} %refs_0_.3), channel_id=1, source_target_pairs={{0,2},{1,3},{2,0},{3,1},{4,6},{5,7},{6,4},{7,5},{8,10},{9,11},{10,... | collective-permute-start | bytes 393224 | tf_op jit(solution)/shard_map/ppermute | solution.py:179
  3.7 13.2 %collective-permute-start.3 = (bf16[512,128]{1,0:T(8,128)(2,1)}, bf16[512,128]{1,0:T(8,128)(2,1)S(1)}, u32[]{:S(2)}, u32[]{:S(2)}) collective-permute-start(bf16[512,128]{1,0:T(8,128)(2,1)} %refs_0_.3), channel_id=1, source_target_pairs={{0,4},{1,5},{2,6},{3,7},{4,0},{5,1},{6,2},{7,3},{8,12},{9,13},{10,... | collective-permute-start | bytes 393224 | tf_op jit(solution)/shard_map/ppermute | solution.py:179
  6.3 10.6 %collective-permute-start.5 = (bf16[512,128]{1,0:T(8,128)(2,1)}, bf16[512,128]{1,0:T(8,128)(2,1)S(1)}, u32[]{:S(2)}, u32[]{:S(2)}) collective-permute-start(bf16[512,128]{1,0:T(8,128)(2,1)} %refs_0_.3), channel_id=1, source_target_pairs={{0,6},{1,7},{2,4},{3,5},{4,2},{5,3},{6,0},{7,1},{8,14},{9,15},{10,... | collective-permute-start | bytes 393224 | tf_op jit(solution)/shard_map/ppermute | solution.py:179
  6.3 11.1 %collective-permute-start = (bf16[512,128]{1,0:T(8,128)(2,1)}, bf16[512,128]{1,0:T(8,128)(2,1)S(1)}, u32[]{:S(2)}, u32[]{:S(2)}) collective-permute-start(bf16[512,128]{1,0:T(8,128)(2,1)} %refs_0_.3), channel_id=1, source_target_pairs={{0,1},{1,0},{2,3},{3,2},{4,5},{5,4},{6,7},{7,6},{8,9},{9,8},{10,11... | collective-permute-start | bytes 393224 | tf_op jit(solution)/shard_map/ppermute | solution.py:179
  9.0 8.4 %collective-permute-start.2 = (bf16[512,128]{1,0:T(8,128)(2,1)S(1)}, bf16[512,128]{1,0:T(8,128)(2,1)S(1)}, u32[]{:S(2)}, u32[]{:S(2)}) collective-permute-start(bf16[512,128]{1,0:T(8,128)(2,1)S(1)} %collective-permute-done.1.refs_2_), channel_id=1, source_target_pairs={{0,1},{1,0},{2,3},{3,2},{4,5},{5,4},{6,7},{7,6},{8,9},{9,8},{10,11... | collective-permute-start | bytes 393224 | tf_op jit(solution)/shard_map/ppermute | solution.py:179
  16.9 1.3 %collective-permute-start.4 = (bf16[512,128]{1,0:T(8,128)(2,1)S(1)}, bf16[512,128]{1,0:T(8,128)(2,1)S(1)}, u32[]{:S(2)}, u32[]{:S(2)}) collective-permute-start(bf16[512,128]{1,0:T(8,128)(2,1)S(1)} %collective-permute-done.3.refs_4_), channel_id=1, source_target_pairs={{0,1},{1,0},{2,3},{3,2},{4,5},{5,4},{6,7},{7,6},{8,9},{9,8},{10,11... | collective-permute-start | bytes 393224 | tf_op jit(solution)/shard_map/ppermute | solution.py:179
  16.9 1.5 %collective-permute-start.6 = (bf16[512,128]{1,0:T(8,128)(2,1)S(1)}, bf16[512,128]{1,0:T(8,128)(2,1)S(1)}, u32[]{:S(2)}, u32[]{:S(2)}) collective-permute-start(bf16[512,128]{1,0:T(8,128)(2,1)S(1)} %collective-permute-done.5.refs_6_), channel_id=1, source_target_pairs={{0,1},{1,0},{2,3},{3,2},{4,5},{5,4},{6,7},{7,6},{8,9},{9,8},{10,11... | collective-permute-start | bytes 393224 | tf_op jit(solution)/shard_map/ppermute | solution.py:179
  18.4 1.0 %copy-start.1 = (bf16[1024,128]{1,0:T(8,128)(2,1)S(1)}, bf16[1024,128]{1,0:T(8,128)(2,1)}, u32[]{:S(2)}) copy-start(bf16[1024,128]{1,0:T(8,128)(2,1)} %weight.1) | copy-start | bytes 786436
  21.2 10.3 %copy-start.7 = (bf16[512,128]{1,0:T(8,128)(2,1)S(1)}, bf16[512,128]{1,0:T(8,128)(2,1)}, u32[]{:S(2)}) copy-start(bf16[512,128]{1,0:T(8,128)(2,1)} %refs_7_.1) | copy-start | bytes 393220
  21.7 9.7 %collective-permute-start.7 = (bf16[512,128]{1,0:T(8,128)(2,1)S(1)}, bf16[512,128]{1,0:T(8,128)(2,1)S(1)}, u32[]{:S(2)}, u32[]{:S(2)}) collective-permute-start(bf16[512,128]{1,0:T(8,128)(2,1)S(1)} %get-tuple-element.22.refs_0_), channel_id=1, source_target_pairs={{0,8},{8,0},{16,24},{24,16},{1,9},{9,1},{17,25},{25,17},{2,10},{10... | collective-permute-start | bytes 393224 | tf_op jit(solution)/shard_map/ppermute | solution.py:179
  23.2 8.3 %collective-permute-start.8 = (bf16[512,128]{1,0:T(8,128)(2,1)S(1)}, bf16[512,128]{1,0:T(8,128)(2,1)S(1)}, u32[]{:S(2)}, u32[]{:S(2)}) collective-permute-start(bf16[512,128]{1,0:T(8,128)(2,1)S(1)} %get-tuple-element.22.refs_0_), channel_id=1, source_target_pairs={{0,16},{8,24},{16,0},{24,8},{1,17},{9,25},{17,1},{25,9},{2,18},{10... | collective-permute-start | bytes 393224 | tf_op jit(solution)/shard_map/ppermute | solution.py:179
  24.7 6.7 %collective-permute-start.9 = (bf16[512,128]{1,0:T(8,128)(2,1)S(1)}, bf16[512,128]{1,0:T(8,128)(2,1)S(1)}, u32[]{:S(2)}, u32[]{:S(2)}) collective-permute-start(bf16[512,128]{1,0:T(8,128)(2,1)S(1)} %get-tuple-element.22.refs_0_), channel_id=1, source_target_pairs={{0,24},{8,16},{16,8},{24,0},{1,25},{9,17},{17,9},{25,1},{2,26},{10... | collective-permute-start | bytes 393224 | tf_op jit(solution)/shard_map/ppermute | solution.py:179
  25.2 1.7 %copy-start = (bf16[80,128,128]{2,1,0:T(8,128)(2,1)S(1)}, bf16[80,128,128]{2,1,0:T(8,128)(2,1)}, u32[]{:S(2)}) copy-start(bf16[80,128,128]{2,1,0:T(8,128)(2,1)} %vals.1) | copy-start | bytes 7864324
  31.5 6.3 %copy-start.2 = (bf16[1024,128]{1,0:T(8,128)(2,1)S(1)}, bf16[1024,128]{1,0:T(8,128)(2,1)}, u32[]{:S(2)}) copy-start(bf16[1024,128]{1,0:T(8,128)(2,1)} %weight.1) | copy-start | bytes 786436
  31.5 6.3 %copy-start.4 = (bf16[1024,128]{1,0:T(8,128)(2,1)S(1)}, bf16[1024,128]{1,0:T(8,128)(2,1)}, u32[]{:S(2)}) copy-start(bf16[1024,128]{1,0:T(8,128)(2,1)} %root.1) | copy-start | bytes 786436
  31.5 6.8 %copy-start.6 = (bf16[512,128]{1,0:T(8,128)(2,1)S(1)}, bf16[512,128]{1,0:T(8,128)(2,1)}, u32[]{:S(2)}) copy-start(bf16[512,128]{1,0:T(8,128)(2,1)} %refs_0_.3) | copy-start | bytes 393220
  33.9 5.2 %collective-permute-start.10 = (bf16[512,128]{1,0:T(8,128)(2,1)S(1)}, bf16[512,128]{1,0:T(8,128)(2,1)S(1)}, u32[]{:S(2)}, u32[]{:S(2)}) collective-permute-start(bf16[512,128]{1,0:T(8,128)(2,1)S(1)} %get-tuple-element.27), channel_id=1, source_target_pairs={{0,8},{8,0},{16,24},{24,16},{1,9},{9,1},{17,25},{25,17},{2,10},{10... | collective-permute-start | bytes 393224 | tf_op jit(solution)/shard_map/ppermute | solution.py:179
  35.6 7.1 %collective-permute-start.11 = (bf16[512,128]{1,0:T(8,128)(2,1)S(1)}, bf16[512,128]{1,0:T(8,128)(2,1)S(1)}, u32[]{:S(2)}, u32[]{:S(2)}) collective-permute-start(bf16[512,128]{1,0:T(8,128)(2,1)S(1)} %get-tuple-element.28), channel_id=1, source_target_pairs={{0,16},{8,24},{16,0},{24,8},{1,17},{9,25},{17,1},{25,9},{2,18},{10... | collective-permute-start | bytes 393224 | tf_op jit(solution)/shard_map/ppermute | solution.py:179
  37.7 5.9 %collective-permute-start.12 = (bf16[512,128]{1,0:T(8,128)(2,1)S(1)}, bf16[512,128]{1,0:T(8,128)(2,1)S(1)}, u32[]{:S(2)}, u32[]{:S(2)}) collective-permute-start(bf16[512,128]{1,0:T(8,128)(2,1)S(1)} %get-tuple-element.29), channel_id=1, source_target_pairs={{0,24},{8,16},{16,8},{24,0},{1,25},{9,17},{17,9},{25,1},{2,26},{10... | collective-permute-start | bytes 393224 | tf_op jit(solution)/shard_map/ppermute | solution.py:179
  37.7 16.4 %collective-permute-start.15 = (bf16[1024,128]{1,0:T(8,128)(2,1)S(1)}, bf16[1024,128]{1,0:T(8,128)(2,1)S(1)}, u32[]{:S(2)}, u32[]{:S(2)}) collective-permute-start(bf16[1024,128]{1,0:T(8,128)(2,1)S(1)} %copy-done.2), channel_id=1, source_target_pairs={{0,1},{1,0},{2,3},{3,2},{4,5},{5,4},{6,7},{7,6},{8,9},{9,8},{10,11... | collective-permute-start | bytes 786440 | tf_op jit(solution)/shard_map/ppermute | solution.py:179
  37.7 17.2 %collective-permute-start.16 = (bf16[1024,128]{1,0:T(8,128)(2,1)S(1)}, bf16[1024,128]{1,0:T(8,128)(2,1)S(1)}, u32[]{:S(2)}, u32[]{:S(2)}) collective-permute-start(bf16[1024,128]{1,0:T(8,128)(2,1)S(1)} %copy-done.4), channel_id=1, source_target_pairs={{0,1},{1,0},{2,3},{3,2},{4,5},{5,4},{6,7},{7,6},{8,9},{9,8},{10,11... | collective-permute-start | bytes 786440 | tf_op jit(solution)/shard_map/ppermute | solution.py:179
  44.2 5.9 %collective-permute-start.20 = (bf16[256,256]{1,0:T(8,128)(2,1)S(1)}, bf16[256,256]{1,0:T(8,128)(2,1)S(1)}, u32[]{:S(2)}, u32[]{:S(2)}) collective-permute-start(bf16[256,256]{1,0:T(8,128)(2,1)S(1)} %get-tuple-element.36), channel_id=1, source_target_pairs={{0,8},{8,0},{16,24},{24,16},{1,9},{9,1},{17,25},{25,17},{2,10},{10... | collective-permute-start | bytes 393224 | tf_op jit(solution)/shard_map/ppermute | solution.py:179
  45.5 7.1 %collective-permute-start.21 = (bf16[256,256]{1,0:T(8,128)(2,1)S(1)}, bf16[256,256]{1,0:T(8,128)(2,1)S(1)}, u32[]{:S(2)}, u32[]{:S(2)}) collective-permute-start(bf16[256,256]{1,0:T(8,128)(2,1)S(1)} %get-tuple-element.37), channel_id=1, source_target_pairs={{0,16},{8,24},{16,0},{24,8},{1,17},{9,25},{17,1},{25,9},{2,18},{10... | collective-permute-start | bytes 393224 | tf_op jit(solution)/shard_map/ppermute | solution.py:179
  46.2 6.4 %collective-permute-start.22 = (bf16[256,256]{1,0:T(8,128)(2,1)S(1)}, bf16[256,256]{1,0:T(8,128)(2,1)S(1)}, u32[]{:S(2)}, u32[]{:S(2)}) collective-permute-start(bf16[256,256]{1,0:T(8,128)(2,1)S(1)} %get-tuple-element.38), channel_id=1, source_target_pairs={{0,24},{8,16},{16,8},{24,0},{1,25},{9,17},{17,9},{25,1},{2,26},{10... | collective-permute-start | bytes 393224 | tf_op jit(solution)/shard_map/ppermute | solution.py:179
  50.1 6.1 %collective-permute-start.14 = (bf16[512,128]{1,0:T(8,128)(2,1)S(1)}, bf16[512,128]{1,0:T(8,128)(2,1)S(1)}, u32[]{:S(2)}, u32[]{:S(2)}) collective-permute-start(bf16[512,128]{1,0:T(8,128)(2,1)S(1)} %get-tuple-element.30.pre), channel_id=1, source_target_pairs={{0,1},{1,0},{2,3},{3,2},{4,5},{5,4},{6,7},{7,6},{8,9},{9,8},{10,11... | collective-permute-start | bytes 393224 | tf_op jit(solution)/shard_map/ppermute | solution.py:179
  52.6 3.6 %collective-permute-start.13 = (bf16[512,128]{1,0:T(8,128)(2,1)S(1)}, bf16[512,128]{1,0:T(8,128)(2,1)S(1)}, u32[]{:S(2)}, u32[]{:S(2)}) collective-permute-start(bf16[512,128]{1,0:T(8,128)(2,1)S(1)} %shard_map.97.hidden), channel_id=1, source_target_pairs={{0,1},{1,0},{2,3},{3,2},{4,5},{5,4},{6,7},{7,6},{8,9},{9,8},{10,11... | collective-permute-start | bytes 393224 | tf_op jit(solution)/shard_map/ppermute | solution.py:179
  52.7 7.2 %collective-permute-start.23 = (bf16[256,256]{1,0:T(8,128)(2,1)S(1)}, bf16[256,256]{1,0:T(8,128)(2,1)S(1)}, u32[]{:S(2)}, u32[]{:S(2)}) collective-permute-start(bf16[256,256]{1,0:T(8,128)(2,1)S(1)} %shard_map.102.refs_0_), channel_id=1, source_target_pairs={{0,8},{8,0},{16,24},{24,16},{1,9},{9,1},{17,25},{25,17},{2,10},{10... | collective-permute-start | bytes 393224 | tf_op jit(solution)/shard_map/ppermute | solution.py:179
  54.2 8.4 %collective-permute-start.24 = (bf16[256,256]{1,0:T(8,128)(2,1)S(1)}, bf16[256,256]{1,0:T(8,128)(2,1)S(1)}, u32[]{:S(2)}, u32[]{:S(2)}) collective-permute-start(bf16[256,256]{1,0:T(8,128)(2,1)S(1)} %shard_map.102.refs_0_), channel_id=1, source_target_pairs={{0,16},{8,24},{16,0},{24,8},{1,17},{9,25},{17,1},{25,9},{2,18},{10... | collective-permute-start | bytes 393224 | tf_op jit(solution)/shard_map/ppermute | solution.py:179
  54.9 7.7 %collective-permute-start.25 = (bf16[256,256]{1,0:T(8,128)(2,1)S(1)}, bf16[256,256]{1,0:T(8,128)(2,1)S(1)}, u32[]{:S(2)}, u32[]{:S(2)}) collective-permute-start(bf16[256,256]{1,0:T(8,128)(2,1)S(1)} %shard_map.102.refs_0_), channel_id=1, source_target_pairs={{0,24},{8,16},{16,8},{24,0},{1,25},{9,17},{17,9},{25,1},{2,26},{10... | collective-permute-start | bytes 393224 | tf_op jit(solution)/shard_map/ppermute | solution.py:179
  56.9 6.7 %collective-permute-start.17 = (bf16[512,128]{1,0:T(8,128)(2,1)S(1)}, bf16[512,128]{1,0:T(8,128)(2,1)S(1)}, u32[]{:S(2)}, u32[]{:S(2)}) collective-permute-start(bf16[512,128]{1,0:T(8,128)(2,1)S(1)} %get-tuple-element.32), channel_id=1, source_target_pairs={{0,2},{1,3},{2,0},{3,1},{4,6},{5,7},{6,4},{7,5},{8,10},{9,11},{10,... | collective-permute-start | bytes 393224 | tf_op jit(solution)/shard_map/ppermute | solution.py:179
  58.5 12.8 %collective-permute-start.18 = (bf16[512,128]{1,0:T(8,128)(2,1)S(1)}, bf16[512,128]{1,0:T(8,128)(2,1)S(1)}, u32[]{:S(2)}, u32[]{:S(2)}) collective-permute-start(bf16[512,128]{1,0:T(8,128)(2,1)S(1)} %get-tuple-element.33), channel_id=1, source_target_pairs={{0,4},{1,5},{2,6},{3,7},{4,0},{5,1},{6,2},{7,3},{8,12},{9,13},{10,... | collective-permute-start | bytes 393224 | tf_op jit(solution)/shard_map/ppermute | solution.py:179
  59.9 11.4 %collective-permute-start.19 = (bf16[512,128]{1,0:T(8,128)(2,1)S(1)}, bf16[512,128]{1,0:T(8,128)(2,1)S(1)}, u32[]{:S(2)}, u32[]{:S(2)}) collective-permute-start(bf16[512,128]{1,0:T(8,128)(2,1)S(1)} %get-tuple-element.34), channel_id=1, source_target_pairs={{0,6},{1,7},{2,4},{3,5},{4,2},{5,3},{6,0},{7,1},{8,14},{9,15},{10,... | collective-permute-start | bytes 393224 | tf_op jit(solution)/shard_map/ppermute | solution.py:179
  (4 other events, 3.2 us)

commit v2 on v1

--- a/solution.py
+++ b/solution.py
@@ -11,6 +11,7 @@
 F32 = jnp.float32
 VMEM = pl.BlockSpec(memory_space=pltpu.VMEM)
 SMEM = pl.BlockSpec(memory_space=pltpu.SMEM)
+ANY = pl.BlockSpec(memory_space=pl.ANY)
 
 
 def dot(a, b):
@@ -39,18 +40,33 @@
     return jax.ShapeDtypeStruct(shape, dtype)
 
 
-def assemble_kernel(counts, cols, vals, adj, adj_t, acc):
+def prepare_kernel(
+    nf, counts, cols, vals, feats, weight, root, adj, adj_t, mine, near, far, tiles, acc, sems
+):
     nblocks = counts.shape[0]
     tile = vals.shape[1]
     all_blocks = adj.shape[1] // tile
+    width = weight.shape[1]
+    me = lax.axis_index("feat")
+    copies = [pltpu.make_async_copy(vals, tiles, sems.at[0])]
+    copies.append(pltpu.make_async_copy(feats, mine, sems.at[1]))
+    for k in range(nf // 2):
+        for flip, out in ((0, near), (1, far)):
+            rows = pl.ds(pl.multiple_of((me ^ (2 * k + flip)) * width, width), width)
+            for half, array in enumerate((weight, root)):
+                place = out.at[half, k * width : (k + 1) * width, :]
+                copies.append(pltpu.make_async_copy(array.at[rows, :], place, sems.at[len(copies)]))
+    for copy in copies:
+        copy.start()
     acc[...] = jnp.zeros_like(acc)
+    copies[0].wait()
     start = jnp.int32(0)
     for b in range(nblocks):
         rows = slice(b * tile, (b + 1) * tile)
 
         def add(t, carry, rows=rows):
             place = pl.ds(pl.multiple_of(cols[t] * tile, tile), tile)
-            acc[rows, place] += vals[t].astype(F32)
+            acc[rows, place] += tiles[t].astype(F32)
             return carry
 
         end = start + counts[b]
@@ -65,25 +81,20 @@
         return carry
 
     lax.fori_loop(0, all_blocks, finish, 0)
+    for copy in copies[1:]:
+        copy.wait()
 
 
 def forward_kernel(nf, *refs):
-    pieces, (weight, root, hidden, own) = refs[:nf], refs[nf:]
-    me = lax.axis_index("feat")
-    width = weight.shape[1]
+    pieces, (near, far, hidden, own) = refs[:nf], refs[nf:]
+    width = hidden.shape[1]
     total = None
     for k in range(nf // 2):
-        even = pl.ds(pl.multiple_of((me ^ (2 * k)) * width, width), width)
-        odd = pl.ds(pl.multiple_of((me ^ (2 * k + 1)) * width, width), width)
+        place = slice(k * width, (k + 1) * width)
         left = jnp.concatenate([pieces[2 * k][...], pieces[2 * k + 1][...]], 1)
-        right = jnp.concatenate(
-            [
-                jnp.concatenate([weight[even, :], root[even, :]], 1),
-                jnp.concatenate([weight[odd, :], root[odd, :]], 1),
-            ],
-            0,
-        )
-        part = dot(left, right)
+        top = jnp.concatenate([near[0, place, :], near[1, place, :]], 1)
+        bottom = jnp.concatenate([far[0, place, :], far[1, place, :]], 1)
+        part = dot(left, jnp.concatenate([top, bottom], 0))
         total = part if total is None else total + part
     hidden[...] = total[:, :width].astype(BF)
     own[...] = total[:, width:]
@@ -127,23 +138,20 @@
     refs[n][...] = total.astype(refs[n].dtype)
 
 
-def feats_kernel(nz, hidden, pre, hidden_2, pre_2, weight, root, weight_2, root_2, kept, *sent):
-    me = lax.axis_index("feat")
-    width = weight.shape[1]
+def feats_kernel(nz, hidden, pre, hidden_2, pre_2, near, near_2, kept, *sent):
+    width = hidden.shape[1]
     left = jnp.concatenate([hidden[...], pre[...], hidden_2[...], pre_2[...]], 1)
     for k in range(nz):
-        rows = pl.ds(pl.multiple_of((me ^ (2 * k)) * width, width), width)
-        right = jnp.concatenate(
-            [weight[rows, :], root[rows, :], weight_2[rows, :], root_2[rows, :]], 1
-        )
-        part = dot_nt(left, right)
+        place = slice(k * width, (k + 1) * width)
+        right = [near[0, place, :], near[1, place, :], near_2[0, place, :], near_2[1, place, :]]
+        part = dot_nt(left, jnp.concatenate(right, 1))
         if k == 0:
             kept[...] = part
         else:
             sent[k - 1][...] = part.astype(BF)
 
 
-def weights_kernel(nr, feats_t, hidden, pre, kept, *rest):
+def weights_kernel(nr, feats_t, hidden, pre, after, kept, *rest):
     sent, whole = rest[:-1], rest[-1]
     me = lax.axis_index("rows")
     share = kept.shape[0]
@@ -178,26 +186,36 @@
     def swap(array, axis, mask):
         return lax.ppermute(array, axis, [(i, i ^ mask) for i in range(lax.axis_size(axis))])
 
-    mine = [node_feats] + [swap(node_feats, "feat", 2 * k) for k in range(1, nz)]
+    moved = [node_feats] + [swap(node_feats, "feat", 2 * k) for k in range(1, nz)]
+    adj, adj_t, mine, near, far = call(
+        functools.partial(prepare_kernel, nf),
+        [
+            sds((rows, nodes), BF),
+            sds((nodes, rows), BF),
+            sds((rows, width), BF),
+            sds((2, depth // 2, width), BF),
+            sds((2, depth // 2, width), BF),
+        ],
+        [SMEM, SMEM] + [ANY] * 4,
+        (block_counts, tile_cols, tile_vals, node_feats, weight, root_weight),
+        flops=4 * rows * nodes,
+        scratch=[
+            pltpu.VMEM(tile_vals.shape, BF),
+            pltpu.VMEM((rows, nodes), F32),
+            pltpu.SemaphoreType.DMA((2 + 2 * nf,)),
+        ],
+        limit=18 * rows * nodes,
+    )
+    arrived = lax.optimization_barrier((mine, *moved[1:], near))[:-1]
     pieces = []
-    for piece in mine:
+    for piece in arrived:
         pieces += [piece, swap(piece, "feat", 1)]
-    weight_2, root_2 = swap(weight, "feat", 1), swap(root_weight, "feat", 1)
-
-    adj, adj_t = call(
-        assemble_kernel,
-        [sds((rows, nodes), BF), sds((nodes, rows), BF)],
-        [SMEM, SMEM, VMEM],
-        (block_counts, tile_cols, tile_vals),
-        flops=4 * rows * nodes,
-        scratch=[pltpu.VMEM((rows, nodes), F32)],
-        limit=16 * rows * nodes,
-    )
+    near_2 = swap(far, "feat", 1)
     hidden, own = call(
         functools.partial(forward_kernel, nf),
         [sds((rows, width), BF), sds((rows, width), F32)],
         [VMEM] * (nf + 2),
-        (*pieces, weight, root_weight),
+        (*pieces, near, far),
         flops=4 * rows * depth * width,
     )
     gathered = [hidden] + [swap(hidden, "rows", j) for j in range(1, nr)]
@@ -221,20 +239,20 @@
         functools.partial(sum_kernel, nr), [sds((rows, width), BF)], [VMEM] * nr, sums
     )
     hidden_2 = swap(grad_hidden, "feat", 1)
+    kept_f, *sent_f = call(
+        functools.partial(feats_kernel, nz),
+        [sds((rows, width), F32)] + [sds((rows, width), BF)] * (nz - 1),
+        [VMEM] * 6,
+        (grad_hidden, grad_pre, hidden_2, pre_2, near, near_2),
+        flops=4 * rows * depth * width,
+    )
     kept_w, *sent_w = call(
         functools.partial(weights_kernel, nr),
         [sds((share, 2 * width), F32)] + [sds((share, 2 * width), BF)] * (nr - 1),
-        [VMEM] * 3,
-        (feats_t, grad_hidden, grad_pre),
+        [VMEM] * 3 + [ANY],
+        (feats_t, grad_hidden, grad_pre, kept_f),
         flops=4 * rows * depth * width,
         scratch=[pltpu.VMEM((depth, 2 * width), F32)],
-    )
-    kept_f, *sent_f = call(
-        functools.partial(feats_kernel, nz),
-        [sds((rows, width), F32)] + [sds((rows, width), BF)] * (nz - 1),
-        [VMEM] * 8,
-        (grad_hidden, grad_pre, hidden_2, pre_2, weight, root_weight, weight_2, root_2),
-        flops=4 * rows * depth * width,
     )
     sums_f = [kept_f] + [swap(part, "feat", 2 * (k + 1)) for k, part in enumerate(sent_f)]
     sums_w = [kept_w] + [swap(part, "rows", j + 1) for j, part in enumerate(sent_w)]

time: 71.5 us -> 63.3 us (0.89); the launches traced: 72 us -> 63 us
  waiting for transfers between devices: 30.4 us -> 18.8 us
  Pallas kernels: 9.34 us -> 10.6 us
  starting transfers between devices: 25.7 us -> 26.9 us
    ppermute x26 -> x25, waiting for transfers between devices: 30.4 us -> 18.8 us  [swap(): lax.ppermute(array, axis, [(i, i ^ mask) for i in range(lax.axis_size(axi...]
    pallas_call x10, Pallas kernels: 9.34 us -> 10.6 us  [call(): pl.pallas_call(body, out_shape=outs, in_specs=specs, out_specs=[VMEM] * l...]
    ppermute x26 -> x25, starting transfers between devices: 25.7 us -> 26.9 us  [swap(): lax.ppermute(array, axis, [(i, i ^ mask) for i in range(lax.axis_size(axi...]
    unnamed x20 -> x14, local copies, waits for them, and re-layouts: 5.87 us -> 5.86 us
  transfers between devices with their start and end apart: 26 -> 25, of which waited for: 12 -> 12; matrix products, arithmetic and copies ran while one was open for 0% -> 0% of each run, Pallas kernels for 8% -> 9%
where the time goes in v2:
time: 63.3 us; the launch traced here: 63 us
  starting transfers between devices  26.9 us (42%)
  waiting for transfers between devices  18.8 us (30%)
  Pallas kernels  10.6 us (17%)
  local copies, waits for them, and re-layouts  5.86 us (9%)
  between operations  0.75 us (1%)
    ppermute x25, starting transfers between devices, swap(): lax.ppermute(array, axis, [(i, i ^ mask) for i in range(lax.axis_size(axi...  26.9 us
    ppermute x25, waiting for transfers between devices, swap(): lax.ppermute(array, axis, [(i, i ^ mask) for i in range(lax.axis_size(axi...  18.8 us
    pallas_call x10, Pallas kernels, call(): pl.pallas_call(body, out_shape=outs, in_specs=specs, out_specs=[VMEM] * l...  10.6 us
    unnamed x14, local copies, waits for them, and re-layouts  5.86 us
  transfers between devices with their start and end apart: 25, of which 12 were waited for; matrix products, arithmetic and copies ran while one was open for 0% of the time, Pallas kernels for 9%

profile of v2, /device:TPU:0, one launch (start us, length us, event | category | flops | bytes accessed | tf_op | source)
XLA Modules:
  0.0 63.0 jit_solution(15047859261530189187)
XLA Ops:
  0.6 3.1 %collective-permute-start = (bf16[512,128]{1,0:T(8,128)(2,1)}, bf16[512,128]{1,0:T(8,128)(2,1)S(1)}, u32[]{:S(2)}, u32[]{:S(2)}) collective-permute-start(bf16[512,128]{1,0:T(8,128)(2,1)} %feats.1), channel_id=1, source_target_pairs={{0,2},{1,3},{2,0},{3,1},{4,6},{5,7},{6,4},{7,5},{8,10},{9,11},{10,... | collective-permute-start | bytes 393224 | tf_op jit(solution)/shard_map/ppermute | solution.py:187
  3.7 2.5 %collective-permute-start.2 = (bf16[512,128]{1,0:T(8,128)(2,1)}, bf16[512,128]{1,0:T(8,128)(2,1)S(1)}, u32[]{:S(2)}, u32[]{:S(2)}) collective-permute-start(bf16[512,128]{1,0:T(8,128)(2,1)} %feats.1), channel_id=1, source_target_pairs={{0,6},{1,7},{2,4},{3,5},{4,2},{5,3},{6,0},{7,1},{8,14},{9,15},{10,... | collective-permute-start | bytes 393224 | tf_op jit(solution)/shard_map/ppermute | solution.py:187
  6.3 1.7 %copy-done = bf16[80,128,128]{2,1,0:T(8,128)(2,1)S(1)} copy-done((bf16[80,128,128]{2,1,0:T(8,128)(2,1)S(1)}, bf16[80,128,128]{2,1,0:T(8,128)(2,1)}, u32[]{:S(2)}) %copy-start) | copy-done | bytes 2621464
  8.1 0.9 %copy-done.1 = bf16[1024,128]{1,0:T(8,128)(2,1)S(1)} copy-done((bf16[1024,128]{1,0:T(8,128)(2,1)S(1)}, bf16[1024,128]{1,0:T(8,128)(2,1)}, u32[]{:S(2)}) %copy-start.1) | copy-done | bytes 262168
  9.0 0.9 %copy-done.2 = bf16[1024,128]{1,0:T(8,128)(2,1)S(1)} copy-done((bf16[1024,128]{1,0:T(8,128)(2,1)S(1)}, bf16[1024,128]{1,0:T(8,128)(2,1)}, u32[]{:S(2)}) %copy-start.2) | copy-done | bytes 262168
  10.0 0.9 %copy-done.3 = bf16[512,128]{1,0:T(8,128)(2,1)S(1)} copy-done((bf16[512,128]{1,0:T(8,128)(2,1)S(1)}, bf16[512,128]{1,0:T(8,128)(2,1)}, u32[]{:S(2)}) %copy-start.3) | copy-done | bytes 131096
  10.9 0.7 %copy-done.5 = s32[4]{0:T(128)S(1)} copy-done((s32[4]{0:T(128)S(1)}, s32[4]{0:T(128)}, u32[]{:S(2)}) %copy-start.5) | copy-done | bytes 40
  11.5 0.7 %copy-done.6 = s32[80]{0:T(128)S(1)} copy-done((s32[80]{0:T(128)S(1)}, s32[80]{0:T(128)}, u32[]{:S(2)}) %copy-start.6) | copy-done | bytes 344
  12.2 4.4 %shard_map.94 = (bf16[512,2048]{1,0:T(8,128)(2,1)S(1)}, bf16[2048,512]{1,0:T(8,128)(2,1)S(1)}, bf16[512,128]{1,0:T(8,128)(2,1)S(1)}, bf16[2,512,128]{2,1,0:T(8,128)(2,1)S(1)}, bf16[2,512,128]{2,1,0:T(8,128)(2,1)S(1)}) custom-call(s32[4]{0:T(128)S(1)} %copy-done.5, s32[80]{0:T(128)S(1)} %copy-done.6, bf16[80,128,128]{2,1,0:T(8,128)(2,1)S(1)} %copy-done, ...), custom_call_target="tpu_custom_call" | custom-call | flops 4194304 | bytes 8126800 | tf_op jit(solution)/shard_map/pallas_call | solution.py:28
  16.6 1.6 %collective-permute-done.1.refs_4_ = bf16[512,128]{1,0:T(8,128)(2,1)S(1)} collective-permute-done((bf16[512,128]{1,0:T(8,128)(2,1)}, bf16[512,128]{1,0:T(8,128)(2,1)S(1)}, u32[]{:S(2)}, u32[]{:S(2)}) %collective-permute-start.1) | collective-permute-done | bytes 131104 | tf_op jit(solution)/shard_map/ppermute | solution.py:187
  20.7 2.5 %collective-permute-start.9 = (bf16[512,128]{1,0:T(8,128)(2,1)S(1)}, bf16[512,128]{1,0:T(8,128)(2,1)S(1)}, u32[]{:S(2)}, u32[]{:S(2)}) collective-permute-start(bf16[512,128]{1,0:T(8,128)(2,1)S(1)} %get-tuple-element.36.refs_0_), channel_id=1, source_target_pairs={{0,24},{8,16},{16,8},{24,0},{1,25},{9,17},{17,9},{25,1},{2,26},{10... | collective-permute-start | bytes 393224 | tf_op jit(solution)/shard_map/ppermute | solution.py:187
  24.2 3.4 %collective-permute-done.9.refs_3_ = bf16[512,128]{1,0:T(8,128)(2,1)S(1)} collective-permute-done((bf16[512,128]{1,0:T(8,128)(2,1)S(1)}, bf16[512,128]{1,0:T(8,128)(2,1)S(1)}, u32[]{:S(2)}, u32[]{:S(2)}) %collective-permute-start.9) | collective-permute-done | bytes 131104 | tf_op jit(solution)/shard_map/ppermute | solution.py:187
  27.7 2.5 %collective-permute-done.8.refs_2_ = bf16[512,128]{1,0:T(8,128)(2,1)S(1)} collective-permute-done((bf16[512,128]{1,0:T(8,128)(2,1)S(1)}, bf16[512,128]{1,0:T(8,128)(2,1)S(1)}, u32[]{:S(2)}, u32[]{:S(2)}) %collective-permute-start.8) | collective-permute-done | bytes 131104 | tf_op jit(solution)/shard_map/ppermute | solution.py:187
  30.3 2.4 %shard_map.96 = (bf16[512,128]{1,0:T(8,128)(2,1)S(1)}, f32[512,128]{1,0:T(8,128)S(1)}, bf16[512,128]{1,0:T(8,128)(2,1)S(1)}, bf16[512,128]{1,0:T(8,128)(2,1)S(1)}, bf16[512,128]{1,0:T(8,128)(2,1)S(1)}) custom-call(bf16[512,128]{1,0:T(8,128)(2,1)S(1)} %get-tuple-element.36.refs_0_, bf16[512,128]{1,0:T(8,128)(2,1)S(1)} %collective-permute-done.7.refs_1_, ...), custom_call_target="tpu_custom_call" | custom-call | flops 536870912 | bytes 5898240 | tf_op jit(solution)/shard_map/pallas_call | solution.py:28
  32.7 1.6 %collective-permute-start.10 = (bf16[512,128]{1,0:T(8,128)(2,1)S(1)}, bf16[512,128]{1,0:T(8,128)(2,1)S(1)}, u32[]{:S(2)}, u32[]{:S(2)}) collective-permute-start(bf16[512,128]{1,0:T(8,128)(2,1)S(1)} %get-tuple-element.41), channel_id=1, source_target_pairs={{0,8},{8,0},{16,24},{24,16},{1,9},{9,1},{17,25},{25,17},{2,10},{10... | collective-permute-start | bytes 393224 | tf_op jit(solution)/shard_map/ppermute | solution.py:187
  34.2 0.7 %collective-permute-start.11 = (bf16[512,128]{1,0:T(8,128)(2,1)S(1)}, bf16[512,128]{1,0:T(8,128)(2,1)S(1)}, u32[]{:S(2)}, u32[]{:S(2)}) collective-permute-start(bf16[512,128]{1,0:T(8,128)(2,1)S(1)} %get-tuple-element.42), channel_id=1, source_target_pairs={{0,16},{8,24},{16,0},{24,8},{1,17},{9,25},{17,1},{25,9},{2,18},{10... | collective-permute-start | bytes 393224 | tf_op jit(solution)/shard_map/ppermute | solution.py:187
  34.9 1.3 %collective-permute-start.12 = (bf16[512,128]{1,0:T(8,128)(2,1)S(1)}, bf16[512,128]{1,0:T(8,128)(2,1)S(1)}, u32[]{:S(2)}, u32[]{:S(2)}) collective-permute-start(bf16[512,128]{1,0:T(8,128)(2,1)S(1)} %get-tuple-element.43), channel_id=1, source_target_pairs={{0,24},{8,16},{16,8},{24,0},{1,25},{9,17},{17,9},{25,1},{2,26},{10... | collective-permute-start | bytes 393224 | tf_op jit(solution)/shard_map/ppermute | solution.py:187
  36.7 1.7 %collective-permute-done.10.refs_1_ = bf16[512,128]{1,0:T(8,128)(2,1)S(1)} collective-permute-done((bf16[512,128]{1,0:T(8,128)(2,1)S(1)}, bf16[512,128]{1,0:T(8,128)(2,1)S(1)}, u32[]{:S(2)}, u32[]{:S(2)}) %collective-permute-start.10) | collective-permute-done | bytes 131104 | tf_op jit(solution)/shard_map/ppermute | solution.py:187
  38.4 3.7 %collective-permute-done.11.refs_2_ = bf16[512,128]{1,0:T(8,128)(2,1)S(1)} collective-permute-done((bf16[512,128]{1,0:T(8,128)(2,1)S(1)}, bf16[512,128]{1,0:T(8,128)(2,1)S(1)}, u32[]{:S(2)}, u32[]{:S(2)}) %collective-permute-start.11) | collective-permute-done | bytes 131104 | tf_op jit(solution)/shard_map/ppermute | solution.py:187
  42.6 1.0 %collective-permute-done.13.hidden_2 = bf16[512,128]{1,0:T(8,128)(2,1)S(1)} collective-permute-done((bf16[512,128]{1,0:T(8,128)(2,1)S(1)}, bf16[512,128]{1,0:T(8,128)(2,1)S(1)}, u32[]{:S(2)}, u32[]{:S(2)}) %collective-permute-start.13) | collective-permute-done | bytes 131104 | tf_op jit(solution)/shard_map/ppermute | solution.py:187
  43.6 0.7 %shard_map.98 = (f32[512,128]{1,0:T(8,128)S(1)}, bf16[512,128]{1,0:T(8,128)(2,1)S(1)}, bf16[512,128]{1,0:T(8,128)(2,1)S(1)}, bf16[512,128]{1,0:T(8,128)(2,1)S(1)}) custom-call(bf16[512,128]{1,0:T(8,128)(2,1)S(1)} %shard_map.97.hidden, bf16[512,128]{1,0:T(8,128)(2,1)S(1)} %get-tuple-element.44.pre, bf16[512,128]{1,0:T(8,128)(2,1)S(1)} %collective-permute-done.13.hidden_2, ...), custom_call_target="tpu_custom_call" | custom-call | flops 268435456 | bytes 1703936 | tf_op jit(solution)/shard_map/pallas_call | solution.py:28
  44.8 0.6 collective-permute-start.19
  45.4 1.6 %collective-permute-start.20 = (bf16[256,256]{1,0:T(8,128)(2,1)S(1)}, bf16[256,256]{1,0:T(8,128)(2,1)S(1)}, u32[]{:S(2)}, u32[]{:S(2)}) collective-permute-start(bf16[256,256]{1,0:T(8,128)(2,1)S(1)} %get-tuple-element.51), channel_id=1, source_target_pairs={{0,16},{8,24},{16,0},{24,8},{1,17},{9,25},{17,1},{25,9},{2,18},{10... | collective-permute-start | bytes 393224 | tf_op jit(solution)/shard_map/ppermute | solution.py:187
  46.9 1.4 %collective-permute-start.21 = (bf16[256,256]{1,0:T(8,128)(2,1)S(1)}, bf16[256,256]{1,0:T(8,128)(2,1)S(1)}, u32[]{:S(2)}, u32[]{:S(2)}) collective-permute-start(bf16[256,256]{1,0:T(8,128)(2,1)S(1)} %get-tuple-element.52), channel_id=1, source_target_pairs={{0,24},{8,16},{16,8},{24,0},{1,25},{9,17},{17,9},{25,1},{2,26},{10... | collective-permute-start | bytes 393224 | tf_op jit(solution)/shard_map/ppermute | solution.py:187
  48.8 2.8 %collective-permute-start.17 = (bf16[512,128]{1,0:T(8,128)(2,1)S(1)}, bf16[512,128]{1,0:T(8,128)(2,1)S(1)}, u32[]{:S(2)}, u32[]{:S(2)}) collective-permute-start(bf16[512,128]{1,0:T(8,128)(2,1)S(1)} %get-tuple-element.47), channel_id=1, source_target_pairs={{0,4},{1,5},{2,6},{3,7},{4,0},{5,1},{6,2},{7,3},{8,12},{9,13},{10,... | collective-permute-start | bytes 393224 | tf_op jit(solution)/shard_map/ppermute | solution.py:187
  51.5 2.3 %collective-permute-start.18 = (bf16[512,128]{1,0:T(8,128)(2,1)S(1)}, bf16[512,128]{1,0:T(8,128)(2,1)S(1)}, u32[]{:S(2)}, u32[]{:S(2)}) collective-permute-start(bf16[512,128]{1,0:T(8,128)(2,1)S(1)} %get-tuple-element.48), channel_id=1, source_target_pairs={{0,6},{1,7},{2,4},{3,5},{4,2},{5,3},{6,0},{7,1},{8,14},{9,15},{10,... | collective-permute-start | bytes 393224 | tf_op jit(solution)/shard_map/ppermute | solution.py:187
  53.9 1.6 %collective-permute-start.24 = (bf16[256,256]{1,0:T(8,128)(2,1)S(1)}, bf16[256,256]{1,0:T(8,128)(2,1)S(1)}, u32[]{:S(2)}, u32[]{:S(2)}) collective-permute-start(bf16[256,256]{1,0:T(8,128)(2,1)S(1)} %shard_map.102.refs_0_), channel_id=1, source_target_pairs={{0,24},{8,16},{16,8},{24,0},{1,25},{9,17},{17,9},{25,1},{2,26},{10... | collective-permute-start | bytes 393224 | tf_op jit(solution)/shard_map/ppermute | solution.py:187
  55.5 1.1 %collective-permute-start.23 = (bf16[256,256]{1,0:T(8,128)(2,1)S(1)}, bf16[256,256]{1,0:T(8,128)(2,1)S(1)}, u32[]{:S(2)}, u32[]{:S(2)}) collective-permute-start(bf16[256,256]{1,0:T(8,128)(2,1)S(1)} %shard_map.102.refs_0_), channel_id=1, source_target_pairs={{0,16},{8,24},{16,0},{24,8},{1,17},{9,25},{17,1},{25,9},{2,18},{10... | collective-permute-start | bytes 393224 | tf_op jit(solution)/shard_map/ppermute | solution.py:187
  56.6 0.9 %collective-permute-start.22 = (bf16[256,256]{1,0:T(8,128)(2,1)S(1)}, bf16[256,256]{1,0:T(8,128)(2,1)S(1)}, u32[]{:S(2)}, u32[]{:S(2)}) collective-permute-start(bf16[256,256]{1,0:T(8,128)(2,1)S(1)} %shard_map.102.refs_0_), channel_id=1, source_target_pairs={{0,8},{8,0},{16,24},{24,16},{1,9},{9,1},{17,25},{25,17},{2,10},{10... | collective-permute-start | bytes 393224 | tf_op jit(solution)/shard_map/ppermute | solution.py:187
  57.4 3.8 %collective-permute-done.17.refs_2_ = bf16[512,128]{1,0:T(8,128)(2,1)S(1)} collective-permute-done((bf16[512,128]{1,0:T(8,128)(2,1)S(1)}, bf16[512,128]{1,0:T(8,128)(2,1)S(1)}, u32[]{:S(2)}, u32[]{:S(2)}) %collective-permute-start.17) | collective-permute-done | bytes 131104 | tf_op jit(solution)/shard_map/ppermute | solution.py:187
  61.2 0.7 %shard_map.99 = bf16[512,128]{1,0:T(8,128)(2,1)} custom-call(f32[512,128]{1,0:T(8,128)S(1)} %get-tuple-element.45.refs_0_.after, bf16[512,128]{1,0:T(8,128)(2,1)S(1)} %collective-permute-done.16.refs_1_, bf16[512,128]{1,0:T(8,128)(2,1)S(1)} %collective-permute-done.17.refs_2_, bf16[512,128]{1,0:T(8,128)(2,1)S(1)} %collective-permute-done.18.refs_3_), custom_call_target="tpu_custom_call" | custom-call | bytes 786432 | tf_op jit(solution)/shard_map/pallas_call | solution.py:28
  61.9 1.0 %shard_map.103 = (f32[1024,128]{1,0:T(8,128)}, f32[1024,128]{1,0:T(8,128)}) custom-call(bf16[256,256]{1,0:T(8,128)(2,1)S(1)} %shard_map.102.refs_0_, bf16[256,256]{1,0:T(8,128)(2,1)S(1)} %collective-permute-done.22.refs_1_, bf16[256,256]{1,0:T(8,128)(2,1)S(1)} %collective-permute-done.23.refs_2_, bf16[256,256]{1,0:T(8,128)(2,1)S(1)} %collective-permute-done.24.refs_3_), custom_call_target="tpu_custom_call" | custom-call | bytes 1572864 | tf_op jit(solution)/shard_map/pallas_call | solution.py:28
  (42 shorter events, 5.8 us)
Async XLA Ops:
  0.6 16.0 %collective-permute-start = (bf16[512,128]{1,0:T(8,128)(2,1)}, bf16[512,128]{1,0:T(8,128)(2,1)S(1)}, u32[]{:S(2)}, u32[]{:S(2)}) collective-permute-start(bf16[512,128]{1,0:T(8,128)(2,1)} %feats.1), channel_id=1, source_target_pairs={{0,2},{1,3},{2,0},{3,1},{4,6},{5,7},{6,4},{7,5},{8,10},{9,11},{10,... | collective-permute-start | bytes 393224 | tf_op jit(solution)/shard_map/ppermute | solution.py:187
  3.7 12.9 %collective-permute-start.2 = (bf16[512,128]{1,0:T(8,128)(2,1)}, bf16[512,128]{1,0:T(8,128)(2,1)S(1)}, u32[]{:S(2)}, u32[]{:S(2)}) collective-permute-start(bf16[512,128]{1,0:T(8,128)(2,1)} %feats.1), channel_id=1, source_target_pairs={{0,6},{1,7},{2,4},{3,5},{4,2},{5,3},{6,0},{7,1},{8,14},{9,15},{10,... | collective-permute-start | bytes 393224 | tf_op jit(solution)/shard_map/ppermute | solution.py:187
  6.2 12.0 %collective-permute-start.1 = (bf16[512,128]{1,0:T(8,128)(2,1)}, bf16[512,128]{1,0:T(8,128)(2,1)S(1)}, u32[]{:S(2)}, u32[]{:S(2)}) collective-permute-start(bf16[512,128]{1,0:T(8,128)(2,1)} %feats.1), channel_id=1, source_target_pairs={{0,4},{1,5},{2,6},{3,7},{4,0},{5,1},{6,2},{7,3},{8,12},{9,13},{10,... | collective-permute-start | bytes 393224 | tf_op jit(solution)/shard_map/ppermute | solution.py:187
  6.3 1.7 %copy-start = (bf16[80,128,128]{2,1,0:T(8,128)(2,1)S(1)}, bf16[80,128,128]{2,1,0:T(8,128)(2,1)}, u32[]{:S(2)}) copy-start(bf16[80,128,128]{2,1,0:T(8,128)(2,1)} %vals.1) | copy-start | bytes 7864324
  8.1 0.9 %copy-start.1 = (bf16[1024,128]{1,0:T(8,128)(2,1)S(1)}, bf16[1024,128]{1,0:T(8,128)(2,1)}, u32[]{:S(2)}) copy-start(bf16[1024,128]{1,0:T(8,128)(2,1)} %weight.1) | copy-start | bytes 786436
  9.0 0.9 %copy-start.2 = (bf16[1024,128]{1,0:T(8,128)(2,1)S(1)}, bf16[1024,128]{1,0:T(8,128)(2,1)}, u32[]{:S(2)}) copy-start(bf16[1024,128]{1,0:T(8,128)(2,1)} %root.1) | copy-start | bytes 786436
  10.0 0.9 %copy-start.3 = (bf16[512,128]{1,0:T(8,128)(2,1)S(1)}, bf16[512,128]{1,0:T(8,128)(2,1)}, u32[]{:S(2)}) copy-start(bf16[512,128]{1,0:T(8,128)(2,1)} %feats.1) | copy-start | bytes 393220
  10.9 0.7 %copy-start.5 = (s32[4]{0:T(128)S(1)}, s32[4]{0:T(128)}, u32[]{:S(2)}) copy-start(s32[4]{0:T(128)} %counts.1) | copy-start | bytes 52
  11.5 0.7 %copy-start.6 = (s32[80]{0:T(128)S(1)}, s32[80]{0:T(128)}, u32[]{:S(2)}) copy-start(s32[80]{0:T(128)} %cols.1) | copy-start | bytes 964
  12.2 18.1 %copy-start.4 = (bf16[512,128]{1,0:T(8,128)(2,1)S(1)}, bf16[512,128]{1,0:T(8,128)(2,1)}, u32[]{:S(2)}) copy-start(bf16[512,128]{1,0:T(8,128)(2,1)} %refs_7_.1) | copy-start | bytes 393220
  18.2 1.3 %collective-permute-start.3 = (bf16[512,128]{1,0:T(8,128)(2,1)S(1)}, bf16[512,128]{1,0:T(8,128)(2,1)S(1)}, u32[]{:S(2)}, u32[]{:S(2)}) collective-permute-start(bf16[512,128]{1,0:T(8,128)(2,1)S(1)} %get-tuple-element.31.refs_0_), channel_id=1, source_target_pairs={{0,1},{1,0},{2,3},{3,2},{4,5},{5,4},{6,7},{7,6},{8,9},{9,8},{10,11... | collective-permute-start | bytes 393224 | tf_op jit(solution)/shard_map/ppermute | solution.py:187
  18.2 1.5 %collective-permute-start.4 = (bf16[512,128]{1,0:T(8,128)(2,1)S(1)}, bf16[512,128]{1,0:T(8,128)(2,1)S(1)}, u32[]{:S(2)}, u32[]{:S(2)}) collective-permute-start(bf16[512,128]{1,0:T(8,128)(2,1)S(1)} %collective-permute-done.refs_2_), channel_id=1, source_target_pairs={{0,1},{1,0},{2,3},{3,2},{4,5},{5,4},{6,7},{7,6},{8,9},{9,8},{10,11... | collective-permute-start | bytes 393224 | tf_op jit(solution)/shard_map/ppermute | solution.py:187
  18.7 1.3 %collective-permute-start.5 = (bf16[512,128]{1,0:T(8,128)(2,1)S(1)}, bf16[512,128]{1,0:T(8,128)(2,1)S(1)}, u32[]{:S(2)}, u32[]{:S(2)}) collective-permute-start(bf16[512,128]{1,0:T(8,128)(2,1)S(1)} %collective-permute-done.1.refs_4_), channel_id=1, source_target_pairs={{0,1},{1,0},{2,3},{3,2},{4,5},{5,4},{6,7},{7,6},{8,9},{9,8},{10,11... | collective-permute-start | bytes 393224 | tf_op jit(solution)/shard_map/ppermute | solution.py:187
  18.7 1.5 %collective-permute-start.6 = (bf16[512,128]{1,0:T(8,128)(2,1)S(1)}, bf16[512,128]{1,0:T(8,128)(2,1)S(1)}, u32[]{:S(2)}, u32[]{:S(2)}) collective-permute-start(bf16[512,128]{1,0:T(8,128)(2,1)S(1)} %collective-permute-done.2.refs_6_), channel_id=1, source_target_pairs={{0,1},{1,0},{2,3},{3,2},{4,5},{5,4},{6,7},{7,6},{8,9},{9,8},{10,11... | collective-permute-start | bytes 393224 | tf_op jit(solution)/shard_map/ppermute | solution.py:187
  20.7 7.0 %collective-permute-start.9 = (bf16[512,128]{1,0:T(8,128)(2,1)S(1)}, bf16[512,128]{1,0:T(8,128)(2,1)S(1)}, u32[]{:S(2)}, u32[]{:S(2)}) collective-permute-start(bf16[512,128]{1,0:T(8,128)(2,1)S(1)} %get-tuple-element.36.refs_0_), channel_id=1, source_target_pairs={{0,24},{8,16},{16,8},{24,0},{1,25},{9,17},{17,9},{25,1},{2,26},{10... | collective-permute-start | bytes 393224 | tf_op jit(solution)/shard_map/ppermute | solution.py:187
  23.2 7.0 %collective-permute-start.8 = (bf16[512,128]{1,0:T(8,128)(2,1)S(1)}, bf16[512,128]{1,0:T(8,128)(2,1)S(1)}, u32[]{:S(2)}, u32[]{:S(2)}) collective-permute-start(bf16[512,128]{1,0:T(8,128)(2,1)S(1)} %get-tuple-element.36.refs_0_), channel_id=1, source_target_pairs={{0,16},{8,24},{16,0},{24,8},{1,17},{9,25},{17,1},{25,9},{2,18},{10... | collective-permute-start | bytes 393224 | tf_op jit(solution)/shard_map/ppermute | solution.py:187
  23.7 6.6 %collective-permute-start.7 = (bf16[512,128]{1,0:T(8,128)(2,1)S(1)}, bf16[512,128]{1,0:T(8,128)(2,1)S(1)}, u32[]{:S(2)}, u32[]{:S(2)}) collective-permute-start(bf16[512,128]{1,0:T(8,128)(2,1)S(1)} %get-tuple-element.36.refs_0_), channel_id=1, source_target_pairs={{0,8},{8,0},{16,24},{24,16},{1,9},{9,1},{17,25},{25,17},{2,10},{10... | collective-permute-start | bytes 393224 | tf_op jit(solution)/shard_map/ppermute | solution.py:187
  32.7 5.8 %collective-permute-start.10 = (bf16[512,128]{1,0:T(8,128)(2,1)S(1)}, bf16[512,128]{1,0:T(8,128)(2,1)S(1)}, u32[]{:S(2)}, u32[]{:S(2)}) collective-permute-start(bf16[512,128]{1,0:T(8,128)(2,1)S(1)} %get-tuple-element.41), channel_id=1, source_target_pairs={{0,8},{8,0},{16,24},{24,16},{1,9},{9,1},{17,25},{25,17},{2,10},{10... | collective-permute-start | bytes 393224 | tf_op jit(solution)/shard_map/ppermute | solution.py:187
  34.2 7.9 %collective-permute-start.11 = (bf16[512,128]{1,0:T(8,128)(2,1)S(1)}, bf16[512,128]{1,0:T(8,128)(2,1)S(1)}, u32[]{:S(2)}, u32[]{:S(2)}) collective-permute-start(bf16[512,128]{1,0:T(8,128)(2,1)S(1)} %get-tuple-element.42), channel_id=1, source_target_pairs={{0,16},{8,24},{16,0},{24,8},{1,17},{9,25},{17,1},{25,9},{2,18},{10... | collective-permute-start | bytes 393224 | tf_op jit(solution)/shard_map/ppermute | solution.py:187
  34.9 7.1 %collective-permute-start.12 = (bf16[512,128]{1,0:T(8,128)(2,1)S(1)}, bf16[512,128]{1,0:T(8,128)(2,1)S(1)}, u32[]{:S(2)}, u32[]{:S(2)}) collective-permute-start(bf16[512,128]{1,0:T(8,128)(2,1)S(1)} %get-tuple-element.43), channel_id=1, source_target_pairs={{0,24},{8,16},{16,8},{24,0},{1,25},{9,17},{17,9},{25,1},{2,26},{10... | collective-permute-start | bytes 393224 | tf_op jit(solution)/shard_map/ppermute | solution.py:187
  36.2 6.3 %collective-permute-start.15 = (bf16[2,512,128]{2,1,0:T(8,128)(2,1)S(1)}, bf16[2,512,128]{2,1,0:T(8,128)(2,1)S(1)}, u32[]{:S(2)}, u32[]{:S(2)}) collective-permute-start(bf16[2,512,128]{2,1,0:T(8,128)(2,1)S(1)} %get-tuple-element.35.refs_9_), channel_id=1, source_target_pairs={{0,1},{1,0},{2,3},{3,2},{4,5},{5,4},{6,7},{7,6},{8,9},{9,8},{10,11... | collective-permute-start | bytes 786440 | tf_op jit(solution)/shard_map/ppermute | solution.py:187
  36.2 6.4 %collective-permute-start.14 = (bf16[512,128]{1,0:T(8,128)(2,1)S(1)}, bf16[512,128]{1,0:T(8,128)(2,1)S(1)}, u32[]{:S(2)}, u32[]{:S(2)}) collective-permute-start(bf16[512,128]{1,0:T(8,128)(2,1)S(1)} %get-tuple-element.44.pre), channel_id=1, source_target_pairs={{0,1},{1,0},{2,3},{3,2},{4,5},{5,4},{6,7},{7,6},{8,9},{9,8},{10,11... | collective-permute-start | bytes 393224 | tf_op jit(solution)/shard_map/ppermute | solution.py:187
  42.2 1.4 %collective-permute-start.13 = (bf16[512,128]{1,0:T(8,128)(2,1)S(1)}, bf16[512,128]{1,0:T(8,128)(2,1)S(1)}, u32[]{:S(2)}, u32[]{:S(2)}) collective-permute-start(bf16[512,128]{1,0:T(8,128)(2,1)S(1)} %shard_map.97.hidden), channel_id=1, source_target_pairs={{0,1},{1,0},{2,3},{3,2},{4,5},{5,4},{6,7},{7,6},{8,9},{9,8},{10,11... | collective-permute-start | bytes 393224 | tf_op jit(solution)/shard_map/ppermute | solution.py:187
  44.8 6.7 %collective-permute-start.19 = (bf16[256,256]{1,0:T(8,128)(2,1)S(1)}, bf16[256,256]{1,0:T(8,128)(2,1)S(1)}, u32[]{:S(2)}, u32[]{:S(2)}) collective-permute-start(bf16[256,256]{1,0:T(8,128)(2,1)S(1)} %get-tuple-element.50), channel_id=1, source_target_pairs={{0,8},{8,0},{16,24},{24,16},{1,9},{9,1},{17,25},{25,17},{2,10},{10... | collective-permute-start | bytes 393224 | tf_op jit(solution)/shard_map/ppermute | solution.py:187
  45.4 8.4 %collective-permute-start.20 = (bf16[256,256]{1,0:T(8,128)(2,1)S(1)}, bf16[256,256]{1,0:T(8,128)(2,1)S(1)}, u32[]{:S(2)}, u32[]{:S(2)}) collective-permute-start(bf16[256,256]{1,0:T(8,128)(2,1)S(1)} %get-tuple-element.51), channel_id=1, source_target_pairs={{0,16},{8,24},{16,0},{24,8},{1,17},{9,25},{17,1},{25,9},{2,18},{10... | collective-permute-start | bytes 393224 | tf_op jit(solution)/shard_map/ppermute | solution.py:187
  46.9 6.9 %collective-permute-start.21 = (bf16[256,256]{1,0:T(8,128)(2,1)S(1)}, bf16[256,256]{1,0:T(8,128)(2,1)S(1)}, u32[]{:S(2)}, u32[]{:S(2)}) collective-permute-start(bf16[256,256]{1,0:T(8,128)(2,1)S(1)} %get-tuple-element.52), channel_id=1, source_target_pairs={{0,24},{8,16},{16,8},{24,0},{1,25},{9,17},{17,9},{25,1},{2,26},{10... | collective-permute-start | bytes 393224 | tf_op jit(solution)/shard_map/ppermute | solution.py:187
  48.3 8.2 %collective-permute-start.16 = (bf16[512,128]{1,0:T(8,128)(2,1)S(1)}, bf16[512,128]{1,0:T(8,128)(2,1)S(1)}, u32[]{:S(2)}, u32[]{:S(2)}) collective-permute-start(bf16[512,128]{1,0:T(8,128)(2,1)S(1)} %get-tuple-element.46), channel_id=1, source_target_pairs={{0,2},{1,3},{2,0},{3,1},{4,6},{5,7},{6,4},{7,5},{8,10},{9,11},{10,... | collective-permute-start | bytes 393224 | tf_op jit(solution)/shard_map/ppermute | solution.py:187
  48.8 12.4 %collective-permute-start.17 = (bf16[512,128]{1,0:T(8,128)(2,1)S(1)}, bf16[512,128]{1,0:T(8,128)(2,1)S(1)}, u32[]{:S(2)}, u32[]{:S(2)}) collective-permute-start(bf16[512,128]{1,0:T(8,128)(2,1)S(1)} %get-tuple-element.47), channel_id=1, source_target_pairs={{0,4},{1,5},{2,6},{3,7},{4,0},{5,1},{6,2},{7,3},{8,12},{9,13},{10,... | collective-permute-start | bytes 393224 | tf_op jit(solution)/shard_map/ppermute | solution.py:187
  51.5 9.7 %collective-permute-start.18 = (bf16[512,128]{1,0:T(8,128)(2,1)S(1)}, bf16[512,128]{1,0:T(8,128)(2,1)S(1)}, u32[]{:S(2)}, u32[]{:S(2)}) collective-permute-start(bf16[512,128]{1,0:T(8,128)(2,1)S(1)} %get-tuple-element.48), channel_id=1, source_target_pairs={{0,6},{1,7},{2,4},{3,5},{4,2},{5,3},{6,0},{7,1},{8,14},{9,15},{10,... | collective-permute-start | bytes 393224 | tf_op jit(solution)/shard_map/ppermute | solution.py:187
  53.9 8.0 %collective-permute-start.24 = (bf16[256,256]{1,0:T(8,128)(2,1)S(1)}, bf16[256,256]{1,0:T(8,128)(2,1)S(1)}, u32[]{:S(2)}, u32[]{:S(2)}) collective-permute-start(bf16[256,256]{1,0:T(8,128)(2,1)S(1)} %shard_map.102.refs_0_), channel_id=1, source_target_pairs={{0,24},{8,16},{16,8},{24,0},{1,25},{9,17},{17,9},{25,1},{2,26},{10... | collective-permute-start | bytes 393224 | tf_op jit(solution)/shard_map/ppermute | solution.py:187
  55.5 6.5 %collective-permute-start.23 = (bf16[256,256]{1,0:T(8,128)(2,1)S(1)}, bf16[256,256]{1,0:T(8,128)(2,1)S(1)}, u32[]{:S(2)}, u32[]{:S(2)}) collective-permute-start(bf16[256,256]{1,0:T(8,128)(2,1)S(1)} %shard_map.102.refs_0_), channel_id=1, source_target_pairs={{0,16},{8,24},{16,0},{24,8},{1,17},{9,25},{17,1},{25,9},{2,18},{10... | collective-permute-start | bytes 393224 | tf_op jit(solution)/shard_map/ppermute | solution.py:187
  56.6 5.4 %collective-permute-start.22 = (bf16[256,256]{1,0:T(8,128)(2,1)S(1)}, bf16[256,256]{1,0:T(8,128)(2,1)S(1)}, u32[]{:S(2)}, u32[]{:S(2)}) collective-permute-start(bf16[256,256]{1,0:T(8,128)(2,1)S(1)} %shard_map.102.refs_0_), channel_id=1, source_target_pairs={{0,8},{8,0},{16,24},{24,16},{1,9},{9,1},{17,25},{25,17},{2,10},{10... | collective-permute-start | bytes 393224 | tf_op jit(solution)/shard_map/ppermute | solution.py:187

commit v3 on v2

v3 whole, which is shorter than its diff:
```python
import functools

import jax
import jax.numpy as jnp
from jax import lax
from jax.experimental import pallas as pl
from jax.experimental.pallas import tpu as pltpu
from jax.sharding import PartitionSpec as P

BF = jnp.bfloat16
F32 = jnp.float32
VMEM = pl.BlockSpec(memory_space=pltpu.VMEM)
SMEM = pl.BlockSpec(memory_space=pltpu.SMEM)
HBM = pl.BlockSpec(memory_space=pltpu.HBM)


def dot(a, b):
    return jnp.dot(a, b, preferred_element_type=F32)


def dot_nt(a, b):
    return lax.dot_general(a, b, (((1,), (1,)), ((), ())), preferred_element_type=F32)


def call(body, outs, specs, args, flops=0, scratch=(), limit=None):
    moved = sum(a.size * a.dtype.itemsize for a in args)
    moved += sum(o.size * o.dtype.itemsize for o in outs)
    return pl.pallas_call(
        body,
        out_shape=outs,
        in_specs=specs,
        out_specs=[VMEM] * len(outs),
        scratch_shapes=scratch,
        compiler_params=pltpu.CompilerParams(vmem_limit_bytes=limit or 32 * 1024 * 1024),
        cost_estimate=pl.CostEstimate(flops=flops, bytes_accessed=moved, transcendentals=0),
    )(*args)


def sds(shape, dtype):
    return jax.ShapeDtypeStruct(shape, dtype)


def assemble_kernel(all_counts, all_cols, vals, adj, counts, cols, tiles, acc, sems):
    nblocks = counts.shape[0]
    tile = vals.shape[1]
    pairs = ((all_counts, counts), (all_cols, cols), (vals, tiles))
    copies = [pltpu.make_async_copy(*pair, sems.at[i]) for i, pair in enumerate(pairs)]
    for copy in copies:
        copy.start()
    acc[...] = jnp.zeros_like(acc)
    for copy in copies:
        copy.wait()
    start = jnp.int32(0)
    for b in range(nblocks):
        rows = slice(b * tile, (b + 1) * tile)

        def add(t, carry, rows=rows):
            place = pl.ds(pl.multiple_of(cols[t] * tile, tile), tile)
            acc[rows, place] += tiles[t].astype(F32)
            return carry

        end = start + counts[b]
        lax.fori_loop(start, end, add, 0)
        start = end
    adj[...] = acc[...].astype(BF)


def flip_kernel(tile, adj, adj_t):
    def flip(c, carry):
        place = pl.ds(pl.multiple_of(c * tile, tile), tile)
        adj_t[place, :] = adj[:, place].T
        return carry

    lax.fori_loop(0, adj.shape[1] // tile, flip, 0)


def prepare_kernel(nf, feats, weight, root, mine, near, far):
    width = weight.shape[1]
    me = lax.axis_index("feat")
    mine[...] = feats[...]
    for k in range(nf // 2):
        place = slice(k * width, (k + 1) * width)
        for flip, out in ((0, near), (1, far)):
            rows = pl.ds(pl.multiple_of((me ^ (2 * k + flip)) * width, width), width)
            out[0, place, :] = weight[rows, :]
            out[1, place, :] = root[rows, :]


def forward_kernel(nf, *refs):
    pieces, (near, far, hidden, own) = refs[:nf], refs[nf:]
    width = hidden.shape[1]
    total = None
    for k in range(nf // 2):
        place = slice(k * width, (k + 1) * width)
        left = jnp.concatenate([pieces[2 * k][...], pieces[2 * k + 1][...]], 1)
        top = jnp.concatenate([near[0, place, :], near[1, place, :]], 1)
        bottom = jnp.concatenate([far[0, place, :], far[1, place, :]], 1)
        part = dot(left, jnp.concatenate([top, bottom], 0))
        total = part if total is None else total + part
    hidden[...] = total[:, :width].astype(BF)
    own[...] = total[:, width:]


def transpose_kernel(nf, *refs):
    pieces, out = refs[:nf], refs[nf]
    me = lax.axis_index("feat")
    width = pieces[0].shape[1]
    for m in range(nf):
        rows = pl.ds(pl.multiple_of((me ^ m) * width, width), width)
        out[rows, :] = pieces[m][...].T


def aggregate_kernel(nr, *refs):
    hidden = refs[:nr]
    adj, adj_t, own, grad_out, grad_pre, kept = refs[nr : nr + 6]
    sent = refs[nr + 6 :]
    me = lax.axis_index("rows")
    rows = own.shape[0]
    pre = own[...]
    for j in range(nr):
        place = pl.ds(pl.multiple_of((me ^ j) * rows, rows), rows)
        pre = pre + dot(adj[:, place], hidden[j][...])
    sig = jax.nn.sigmoid(pre)
    grad = (grad_out[...].astype(F32) * sig * (1.0 + pre * (1.0 - sig))).astype(BF)
    grad_pre[...] = grad
    for j in range(nr):
        place = pl.ds(pl.multiple_of((me ^ j) * rows, rows), rows)
        part = dot(adj_t[place, :], grad)
        if j == 0:
            kept[...] = part
        else:
            sent[j - 1][...] = part.astype(BF)


def sum_kernel(n, *refs):
    total = refs[0][...].astype(F32)
    for ref in refs[1:n]:
        total = total + ref[...].astype(F32)
    refs[n][...] = total.astype(refs[n].dtype)


def feats_kernel(nz, hidden, pre, hidden_2, pre_2, near, near_2, *out):
    width = hidden.shape[1]
    left = jnp.concatenate([hidden[...], pre[...], hidden_2[...], pre_2[...]], 1)
    for k in range(nz):
        place = slice(k * width, (k + 1) * width)
        right = [near[0, place, :], near[1, place, :], near_2[0, place, :], near_2[1, place, :]]
        out[k][...] = dot_nt(left, jnp.concatenate(right, 1)).astype(out[k].dtype)


def weights_kernel(feats_t, hidden, pre, weight, root):
    width = weight.shape[1]
    both = dot(feats_t[...], jnp.concatenate([hidden[...], pre[...]], 1))
    weight[...] = both[:, :width].astype(BF)
    root[...] = both[:, width:].astype(BF)


def pair_sum_kernel(weight, weight_2, root, root_2, weight_sum, root_sum):
    for out, terms in ((weight_sum, (weight, weight_2)), (root_sum, (root, root_2))):
        total = terms[0][...].astype(F32) + terms[1][...].astype(F32)
        out[...] = total.astype(out.dtype)


def on_device(node_feats, weight, root_weight, grad_out, block_counts, tile_cols, tile_vals):
    rows, width = node_feats.shape
    depth = weight.shape[0]
    nr, nf = lax.axis_size("rows"), lax.axis_size("feat")
    nz = nf // 2
    nodes = rows * nr

    def swap(array, axis, mask):
        return lax.ppermute(array, axis, [(i, i ^ mask) for i in range(lax.axis_size(axis))])

    (adj,) = call(
        assemble_kernel,
        [sds((rows, nodes), BF)],
        [HBM] * 3,
        (block_counts, tile_cols, tile_vals),
        flops=4 * rows * nodes,
        scratch=[
            pltpu.SMEM(block_counts.shape, jnp.int32),
            pltpu.SMEM(tile_cols.shape, jnp.int32),
            pltpu.VMEM(tile_vals.shape, BF),
            pltpu.VMEM((rows, nodes), F32),
            pltpu.SemaphoreType.DMA((3,)),
        ],
        limit=58 * 1024 * 1024,
    )
    mine, near, far = call(
        functools.partial(prepare_kernel, nf),
        [sds((rows, width), BF)] + [sds((2, depth // 2, width), BF)] * 2,
        [VMEM] * 3,
        (node_feats, weight, root_weight),
    )
    (adj_t,) = call(
        functools.partial(flip_kernel, tile_vals.shape[1]), [sds((nodes, rows), BF)], [VMEM], (adj,)
    )
    masks = [1 << bit for bit in range(1, nf.bit_length() - 1)]
    moved = {0: node_feats}
    for mask in reversed(masks):
        if mask == masks[0]:
            ahead = {0: node_feats, mask: swap(node_feats, "feat", mask)}
            ahead |= {m: piece for m, piece in moved.items() if m}
            order = sorted(ahead, reverse=True)
            moved = dict(zip(order, lax.optimization_barrier((*[ahead[m] for m in order], adj))))
            moved |= {m | mask: swap(moved[m], "feat", mask) for m in order if m and m != mask}
        else:
            moved |= {m | mask: swap(piece, "feat", mask) for m, piece in moved.items()}
    moved[0] = mine
    late = [m for m in moved if m & masks[0] and m != masks[0]]
    moved |= dict(zip(late, lax.optimization_barrier((*[moved[m] for m in late], near))))
    pieces = []
    for m in sorted(moved):
        pieces += [moved[m], swap(moved[m], "feat", 1)]
    near_2 = swap(far, "feat", 1)
    hidden, own = call(
        functools.partial(forward_kernel, nf),
        [sds((rows, width), BF), sds((rows, width), F32)],
        [VMEM] * (nf + 2),
        (*pieces, near, far),
        flops=4 * rows * depth * width,
    )
    gathered = [hidden] + [swap(hidden, "rows", j) for j in range(1, nr)]
    (feats_t,) = call(
        functools.partial(transpose_kernel, nf),
        [sds((depth, rows), BF)],
        [VMEM] * nf,
        pieces,
    )
    grad_pre, kept, *sent = call(
        functools.partial(aggregate_kernel, nr),
        [sds((rows, width), BF), sds((rows, width), F32)] + [sds((rows, width), BF)] * (nr - 1),
        [VMEM] * (nr + 4),
        (*gathered, adj, adj_t, own, grad_out),
        flops=4 * rows * nodes * width,
        limit=max(32 * 1024 * 1024, 10 * rows * nodes),
    )
    pre_2 = swap(grad_pre, "feat", 1)
    sums = [kept] + [swap(part, "rows", j + 1) for j, part in enumerate(sent)]
    (grad_hidden,) = call(
        functools.partial(sum_kernel, nr), [sds((rows, width), BF)], [VMEM] * nr, sums
    )
    hidden_2 = swap(grad_hidden, "feat", 1)
    parts = call(
        functools.partial(feats_kernel, nz),
        [sds((rows, width), BF if k else F32) for k in range(nz)],
        [VMEM] * 6,
        (grad_hidden, grad_pre, hidden_2, pre_2, near, near_2),
        flops=4 * rows * depth * width,
    )
    grads = call(
        weights_kernel,
        [sds((depth, width), BF)] * 2,
        [VMEM] * 3,
        (feats_t, grad_hidden, grad_pre),
        flops=4 * rows * depth * width,
    )
    sums_f = [parts[0]] + [swap(part, "feat", 2 * k) for k, part in enumerate(parts) if k]
    steps = [1 << bit for bit in range(nr.bit_length() - 1)]
    *between, final = zip(reversed(steps), steps)
    for there, back in between:
        other = swap(grads[0], "rows", there), swap(grads[1], "rows", back)
        grads = call(
            pair_sum_kernel,
            [sds((depth, width), BF)] * 2,
            [VMEM] * 4,
            (grads[0], other[0], grads[1], other[1]),
        )

    def finish(grads):
        other = swap(grads[0], "rows", final[0]), swap(grads[1], "rows", final[1])
        return tuple(
            call(
                pair_sum_kernel,
                [sds((depth, width), F32)] * 2,
                [VMEM] * 4,
                (grads[0], other[0], grads[1], other[1]),
            )
        )

    def skip(grads):
        return (jnp.zeros((depth, width), F32),) * 2

    grad_weight, grad_root = lax.cond(block_counts[0] > 0, finish, skip, tuple(grads))
    *sums_f, grad_weight, grad_root = lax.optimization_barrier((*sums_f, grad_weight, grad_root))
    (grad_feats,) = call(
        functools.partial(sum_kernel, len(sums_f)), [sds((rows, width), BF)], [VMEM] * len(sums_f), sums_f
    )
    return grad_feats, grad_weight, grad_root


def solution(mesh):
    placed = (
        P("rows", "feat"),
        P(None, "feat"),
        P(None, "feat"),
        P("rows", "feat"),
        P("rows"),
        P("rows"),
        P("rows", None, None),
    )
    return jax.shard_map(
        on_device,
        mesh=mesh,
        in_specs=placed,
        out_specs=(P("rows", "feat"), P(None, "feat"), P(None, "feat")),
        check_vma=False,
    )
```

time: 63.3 us -> 59.6 us (0.942)
  local copies, waits for them, and re-layouts: 5.86 us -> 0.03 us
  waiting for transfers between devices: 18.8 us -> 23.9 us
  starting transfers between devices: 26.9 us -> 23 us
  Pallas kernels: 10.6 us -> 11.7 us
    unnamed x14 -> x12, local copies, waits for them, and re-layouts: 5.86 us -> 0.03 us
    ppermute x25 -> x23, waiting for transfers between devices: 18.8 us -> 23.9 us  [swap(): lax.ppermute(array, axis, [(i, i ^ mask) for i in range(lax.axis_size(axi...]
    ppermute x25 -> x23, starting transfers between devices: 26.9 us -> 23 us  [swap(): lax.ppermute(array, axis, [(i, i ^ mask) for i in range(lax.axis_size(axi...]
    pallas_call x10 -> x12, Pallas kernels: 10.6 us -> 11.7 us  [call(): pl.pallas_call(body, out_shape=outs, in_specs=specs, out_specs=[VMEM] * l...]
  transfers between devices with their start and end apart: 25 -> 23, of which waited for: 12 -> 13; matrix products, arithmetic and copies ran while one was open for 0% -> 0% of each run, Pallas kernels for 9% -> 14%
where the time goes in v3:
time: 59.6 us; the launch traced here: 59.4 us
  waiting for transfers between devices  23.9 us (40%)
  starting transfers between devices  23 us (39%)
  Pallas kernels  11.7 us (20%)
  between operations  0.84 us (1%)
    ppermute x23, waiting for transfers between devices, swap(): lax.ppermute(array, axis, [(i, i ^ mask) for i in range(lax.axis_size(axi...  23.9 us
    ppermute x23, starting transfers between devices, swap(): lax.ppermute(array, axis, [(i, i ^ mask) for i in range(lax.axis_size(axi...  23 us
    pallas_call x12, Pallas kernels, call(): pl.pallas_call(body, out_shape=outs, in_specs=specs, out_specs=[VMEM] * l...  11.7 us
  transfers between devices with their start and end apart: 23, of which 13 were waited for; matrix products, arithmetic and copies ran while one was open for 0% of the time, Pallas kernels for 14%

profile of v3, /device:TPU:0, one launch (start us, length us, event | category | flops | bytes accessed | tf_op | source)
XLA Modules:
  0.0 59.4 jit_solution(15672382824691595258)
XLA Ops:
  0.7 4.1 %collective-permute-start.3 = (bf16[512,128]{1,0:T(8,128)(2,1)}, bf16[512,128]{1,0:T(8,128)(2,1)S(1)}, u32[]{:S(2)}, u32[]{:S(2)}) collective-permute-start(bf16[512,128]{1,0:T(8,128)(2,1)} %feats.1), channel_id=1, source_target_pairs={{0,4},{1,5},{2,6},{3,7},{4,0},{5,1},{6,2},{7,3},{8,12},{9,13},{10,... | collective-permute-start | bytes 393224 | tf_op jit(solution)/shard_map/ppermute | solution.py:172
  4.8 1.6 %collective-permute-start.4 = (bf16[512,128]{1,0:T(8,128)(2,1)}, bf16[512,128]{1,0:T(8,128)(2,1)S(1)}, u32[]{:S(2)}, u32[]{:S(2)}) collective-permute-start(bf16[512,128]{1,0:T(8,128)(2,1)} %feats.1), channel_id=1, source_target_pairs={{0,2},{1,3},{2,0},{3,1},{4,6},{5,7},{6,4},{7,5},{8,10},{9,11},{10,... | collective-permute-start | bytes 393224 | tf_op jit(solution)/shard_map/ppermute | solution.py:172
  6.3 4.0 %shard_map.95.adj.refs_4_ = bf16[512,2048]{1,0:T(8,128)(2,1)} custom-call(s32[4]{0:T(128)} %all_counts.1, s32[80]{0:T(128)} %all_cols.1, bf16[80,128,128]{2,1,0:T(8,128)(2,1)} %vals.1), custom_call_target="tpu_custom_call" | custom-call | flops 4194304 | bytes 4718928 | tf_op jit(solution)/shard_map/pallas_call | solution.py:28
  10.4 1.0 %collective-permute-done.3.refs_4_ = bf16[512,128]{1,0:T(8,128)(2,1)S(1)} collective-permute-done((bf16[512,128]{1,0:T(8,128)(2,1)}, bf16[512,128]{1,0:T(8,128)(2,1)S(1)}, u32[]{:S(2)}, u32[]{:S(2)}) %collective-permute-start.3) | collective-permute-done | bytes 131104 | tf_op jit(solution)/shard_map/ppermute | solution.py:172
  11.6 1.4 %collective-permute-start.7 = (bf16[512,128]{1,0:T(8,128)(2,1)S(1)}, bf16[512,128]{1,0:T(8,128)(2,1)S(1)}, u32[]{:S(2)}, u32[]{:S(2)}) collective-permute-start(bf16[512,128]{1,0:T(8,128)(2,1)S(1)} %collective-permute-done.3.refs_4_), channel_id=1, source_target_pairs={{0,2},{1,3},{2,0},{3,1},{4,6},{5,7},{6,4},{7,5},{8,10},{9,11},{10,... | collective-permute-start | bytes 393224 | tf_op jit(solution)/shard_map/ppermute | solution.py:172
  13.2 0.5 collective-permute-start.6
  13.7 2.8 %collective-permute-done.7.refs_6_ = bf16[512,128]{1,0:T(8,128)(2,1)S(1)} collective-permute-done((bf16[512,128]{1,0:T(8,128)(2,1)S(1)}, bf16[512,128]{1,0:T(8,128)(2,1)S(1)}, u32[]{:S(2)}, u32[]{:S(2)}) %collective-permute-start.7) | collective-permute-done | bytes 131104 | tf_op jit(solution)/shard_map/ppermute | solution.py:172
  16.6 1.3 %collective-permute-done.8.refs_7_ = bf16[512,128]{1,0:T(8,128)(2,1)S(1)} collective-permute-done((bf16[512,128]{1,0:T(8,128)(2,1)S(1)}, bf16[512,128]{1,0:T(8,128)(2,1)S(1)}, u32[]{:S(2)}, u32[]{:S(2)}) %collective-permute-start.8) | collective-permute-done | bytes 131104 | tf_op jit(solution)/shard_map/ppermute | solution.py:172
  18.4 1.6 %collective-permute-start.10 = (bf16[512,128]{1,0:T(8,128)(2,1)S(1)}, bf16[512,128]{1,0:T(8,128)(2,1)S(1)}, u32[]{:S(2)}, u32[]{:S(2)}) collective-permute-start(bf16[512,128]{1,0:T(8,128)(2,1)S(1)} %get-tuple-element.42.refs_0_), channel_id=1, source_target_pairs={{0,16},{8,24},{16,0},{24,8},{1,17},{9,25},{17,1},{25,9},{2,18},{10... | collective-permute-start | bytes 393224 | tf_op jit(solution)/shard_map/ppermute | solution.py:172
  20.0 1.4 %collective-permute-start.11 = (bf16[512,128]{1,0:T(8,128)(2,1)S(1)}, bf16[512,128]{1,0:T(8,128)(2,1)S(1)}, u32[]{:S(2)}, u32[]{:S(2)}) collective-permute-start(bf16[512,128]{1,0:T(8,128)(2,1)S(1)} %get-tuple-element.42.refs_0_), channel_id=1, source_target_pairs={{0,24},{8,16},{16,8},{24,0},{1,25},{9,17},{17,9},{25,1},{2,26},{10... | collective-permute-start | bytes 393224 | tf_op jit(solution)/shard_map/ppermute | solution.py:172
  21.4 0.5 collective-permute-start.9
  21.9 1.4 %shard_map.97.refs_5_ = bf16[2048,512]{1,0:T(8,128)(2,1)S(1)} custom-call(bf16[512,2048]{1,0:T(8,128)(2,1)S(1)} %copy-done), custom_call_target="tpu_custom_call" | custom-call | bytes 4194304 | tf_op jit(solution)/shard_map/pallas_call | solution.py:28
  23.4 2.9 %collective-permute-done.10.refs_2_ = bf16[512,128]{1,0:T(8,128)(2,1)S(1)} collective-permute-done((bf16[512,128]{1,0:T(8,128)(2,1)S(1)}, bf16[512,128]{1,0:T(8,128)(2,1)S(1)}, u32[]{:S(2)}, u32[]{:S(2)}) %collective-permute-start.10) | collective-permute-done | bytes 131104 | tf_op jit(solution)/shard_map/ppermute | solution.py:172
  26.3 1.0 %collective-permute-done.11.refs_3_ = bf16[512,128]{1,0:T(8,128)(2,1)S(1)} collective-permute-done((bf16[512,128]{1,0:T(8,128)(2,1)S(1)}, bf16[512,128]{1,0:T(8,128)(2,1)S(1)}, u32[]{:S(2)}, u32[]{:S(2)}) %collective-permute-start.11) | collective-permute-done | bytes 131104 | tf_op jit(solution)/shard_map/ppermute | solution.py:172
  27.3 0.7 %collective-permute-done.9.refs_1_ = bf16[512,128]{1,0:T(8,128)(2,1)S(1)} collective-permute-done((bf16[512,128]{1,0:T(8,128)(2,1)S(1)}, bf16[512,128]{1,0:T(8,128)(2,1)S(1)}, u32[]{:S(2)}, u32[]{:S(2)}) %collective-permute-start.9) | collective-permute-done | bytes 131104 | tf_op jit(solution)/shard_map/ppermute | solution.py:172
  28.0 2.4 %shard_map.98 = (bf16[512,128]{1,0:T(8,128)(2,1)S(1)}, f32[512,128]{1,0:T(8,128)S(1)}, bf16[512,128]{1,0:T(8,128)(2,1)S(1)}, bf16[512,128]{1,0:T(8,128)(2,1)S(1)}, bf16[512,128]{1,0:T(8,128)(2,1)S(1)}) custom-call(bf16[512,128]{1,0:T(8,128)(2,1)S(1)} %get-tuple-element.42.refs_0_, bf16[512,128]{1,0:T(8,128)(2,1)S(1)} %collective-permute-done.9.refs_1_, ...), custom_call_target="tpu_custom_call" | custom-call | flops 536870912 | bytes 5898240 | tf_op jit(solution)/shard_map/pallas_call | solution.py:28
  30.4 1.6 %collective-permute-start.12 = (bf16[512,128]{1,0:T(8,128)(2,1)S(1)}, bf16[512,128]{1,0:T(8,128)(2,1)S(1)}, u32[]{:S(2)}, u32[]{:S(2)}) collective-permute-start(bf16[512,128]{1,0:T(8,128)(2,1)S(1)} %get-tuple-element.45), channel_id=1, source_target_pairs={{0,8},{8,0},{16,24},{24,16},{1,9},{9,1},{17,25},{25,17},{2,10},{10... | collective-permute-start | bytes 393224 | tf_op jit(solution)/shard_map/ppermute | solution.py:172
  32.0 1.5 %collective-permute-start.13 = (bf16[512,128]{1,0:T(8,128)(2,1)S(1)}, bf16[512,128]{1,0:T(8,128)(2,1)S(1)}, u32[]{:S(2)}, u32[]{:S(2)}) collective-permute-start(bf16[512,128]{1,0:T(8,128)(2,1)S(1)} %get-tuple-element.46), channel_id=1, source_target_pairs={{0,16},{8,24},{16,0},{24,8},{1,17},{9,25},{17,1},{25,9},{2,18},{10... | collective-permute-start | bytes 393224 | tf_op jit(solution)/shard_map/ppermute | solution.py:172
  34.3 0.6 collective-permute-start.16
  34.9 1.5 %collective-permute-done.12.refs_1_ = bf16[512,128]{1,0:T(8,128)(2,1)S(1)} collective-permute-done((bf16[512,128]{1,0:T(8,128)(2,1)S(1)}, bf16[512,128]{1,0:T(8,128)(2,1)S(1)}, u32[]{:S(2)}, u32[]{:S(2)}) %collective-permute-start.12) | collective-permute-done | bytes 131104 | tf_op jit(solution)/shard_map/ppermute | solution.py:172
  36.4 3.3 %collective-permute-done.13.refs_2_ = bf16[512,128]{1,0:T(8,128)(2,1)S(1)} collective-permute-done((bf16[512,128]{1,0:T(8,128)(2,1)S(1)}, bf16[512,128]{1,0:T(8,128)(2,1)S(1)}, u32[]{:S(2)}, u32[]{:S(2)}) %collective-permute-start.13) | collective-permute-done | bytes 131104 | tf_op jit(solution)/shard_map/ppermute | solution.py:172
  40.3 1.1 %collective-permute-start.21 = (bf16[1024,128]{1,0:T(8,128)(2,1)S(1)}, bf16[1024,128]{1,0:T(8,128)(2,1)S(1)}, u32[]{:S(2)}, u32[]{:S(2)}) collective-permute-start(bf16[1024,128]{1,0:T(8,128)(2,1)S(1)} %get-tuple-element.53.weight), channel_id=1, source_target_pairs={{0,16},{8,24},{16,0},{24,8},{1,17},{9,25},{17,1},{25,9},{2,18},{10... | collective-permute-start | bytes 786440 | tf_op jit(solution)/shard_map/ppermute | solution.py:172
  41.7 0.7 %shard_map.100 = (f32[512,128]{1,0:T(8,128)S(1)}, bf16[512,128]{1,0:T(8,128)(2,1)S(1)}, bf16[512,128]{1,0:T(8,128)(2,1)S(1)}, bf16[512,128]{1,0:T(8,128)(2,1)S(1)}) custom-call(bf16[512,128]{1,0:T(8,128)(2,1)S(1)} %shard_map.99.hidden, bf16[512,128]{1,0:T(8,128)(2,1)S(1)} %get-tuple-element.48.pre, bf16[512,128]{1,0:T(8,128)(2,1)S(1)} %collective-permute-done.15.hidden_2, ...), custom_call_target="tpu_custom_call" | custom-call | flops 268435456 | bytes 1703936 | tf_op jit(solution)/shard_map/pallas_call | solution.py:28
  42.4 1.5 %collective-permute-start.18 = (bf16[512,128]{1,0:T(8,128)(2,1)S(1)}, bf16[512,128]{1,0:T(8,128)(2,1)S(1)}, u32[]{:S(2)}, u32[]{:S(2)}) collective-permute-start(bf16[512,128]{1,0:T(8,128)(2,1)S(1)} %get-tuple-element.50), channel_id=1, source_target_pairs={{0,2},{1,3},{2,0},{3,1},{4,6},{5,7},{6,4},{7,5},{8,10},{9,11},{10,... | collective-permute-start | bytes 393224 | tf_op jit(solution)/shard_map/ppermute | solution.py:172
  43.9 2.8 %collective-permute-start.19 = (bf16[512,128]{1,0:T(8,128)(2,1)S(1)}, bf16[512,128]{1,0:T(8,128)(2,1)S(1)}, u32[]{:S(2)}, u32[]{:S(2)}) collective-permute-start(bf16[512,128]{1,0:T(8,128)(2,1)S(1)} %get-tuple-element.51), channel_id=1, source_target_pairs={{0,4},{1,5},{2,6},{3,7},{4,0},{5,1},{6,2},{7,3},{8,12},{9,13},{10,... | collective-permute-start | bytes 393224 | tf_op jit(solution)/shard_map/ppermute | solution.py:172
  46.9 2.2 %collective-permute-done.21.weight_2 = bf16[1024,128]{1,0:T(8,128)(2,1)S(1)} collective-permute-done((bf16[1024,128]{1,0:T(8,128)(2,1)S(1)}, bf16[1024,128]{1,0:T(8,128)(2,1)S(1)}, u32[]{:S(2)}, u32[]{:S(2)}) %collective-permute-start.21) | collective-permute-done | bytes 262176 | tf_op jit(solution)/shard_map/ppermute | solution.py:172
  49.1 0.7 %collective-permute-done.22.root_2 = bf16[1024,128]{1,0:T(8,128)(2,1)S(1)} collective-permute-done((bf16[1024,128]{1,0:T(8,128)(2,1)S(1)}, bf16[1024,128]{1,0:T(8,128)(2,1)S(1)}, u32[]{:S(2)}, u32[]{:S(2)}) %collective-permute-start.22) | collective-permute-done | bytes 262176 | tf_op jit(solution)/shard_map/ppermute | solution.py:172
  49.9 8.8 %conditional.1 = ((f32[1024,128]{1,0:T(8,128)}, f32[1024,128]{1,0:T(8,128)})) conditional(s32[]{:T(128)} %bitcast, () %tuple.19, (bf16[1024,128]{1,0:T(8,128)(2,1)S(1)}, bf16[1024,128]{1,0:T(8,128)(2,1)S(1)}) %shard_map.103), branch_computations={%region_0.0_spmd, %region_1.0_spmd} | conditional | bytes 4194392 | solution.py:284
  50.3 1.2 %collective-permute-start.1 = (bf16[1024,128]{1,0:T(8,128)(2,1)S(1)}, bf16[1024,128]{1,0:T(8,128)(2,1)S(1)}, u32[]{:S(2)}, u32[]{:S(2)}) collective-permute-start(bf16[1024,128]{1,0:T(8,128)(2,1)S(1)} %get-tuple-element.5.root), channel_id=1, source_target_pairs={{0,16},{8,24},{16,0},{24,8},{1,17},{9,25},{17,1},{25,9},{2,18},{10... | collective-permute-start | bytes 786440 | tf_op jit(solution)/shard_map/cond/branch_1_fun/ppermute | solution.py:172
  51.6 6.1 %collective-permute-done.weight_2 = bf16[1024,128]{1,0:T(8,128)(2,1)S(1)} collective-permute-done((bf16[1024,128]{1,0:T(8,128)(2,1)S(1)}, bf16[1024,128]{1,0:T(8,128)(2,1)S(1)}, u32[]{:S(2)}, u32[]{:S(2)}) %collective-permute-start) | collective-permute-done | bytes 262176 | tf_op jit(solution)/shard_map/cond/branch_1_fun/ppermute | solution.py:172
  57.7 1.0 %branch_1_fun.1 = (f32[1024,128]{1,0:T(8,128)}, f32[1024,128]{1,0:T(8,128)}) custom-call(bf16[1024,128]{1,0:T(8,128)(2,1)S(1)} %get-tuple-element.4.weight, bf16[1024,128]{1,0:T(8,128)(2,1)S(1)} %collective-permute-done.weight_2, bf16[1024,128]{1,0:T(8,128)(2,1)S(1)} %get-tuple-element.5.root, bf16[1024,128]{1,0:T(8,128)(2,1)S(1)} %collective-permute-done.1.root_2), custom_call_target="tpu_custom_call" | custom-call | bytes 2097152 | tf_op jit(solution)/shard_map/cond/branch_1_fun/pallas_call | solution.py:28
  58.7 0.7 %shard_map.104 = bf16[512,128]{1,0:T(8,128)(2,1)} custom-call(f32[512,128]{1,0:T(8,128)S(1)} %get-tuple-element.57.refs_0_, bf16[512,128]{1,0:T(8,128)(2,1)S(1)} %collective-permute-done.18.refs_1_, bf16[512,128]{1,0:T(8,128)(2,1)S(1)} %collective-permute-done.19.refs_2_, bf16[512,128]{1,0:T(8,128)(2,1)S(1)} %collective-permute-done.20.refs_3_), custom_call_target="tpu_custom_call" | custom-call | bytes 786432 | tf_op jit(solution)/shard_map/pallas_call | solution.py:28
  (39 shorter events, 3.2 us)
Async XLA Ops:
  0.6 12.4 %copy-start.3 = (bf16[512,128]{1,0:T(8,128)(2,1)S(1)}, bf16[512,128]{1,0:T(8,128)(2,1)}, u32[]{:S(2)}) copy-start(bf16[512,128]{1,0:T(8,128)(2,1)} %feats.1) | copy-start | bytes 393220
  0.6 12.4 %copy-start.1 = (bf16[1024,128]{1,0:T(8,128)(2,1)S(1)}, bf16[1024,128]{1,0:T(8,128)(2,1)}, u32[]{:S(2)}) copy-start(bf16[1024,128]{1,0:T(8,128)(2,1)} %weight.1) | copy-start | bytes 786436
  0.7 12.4 %copy-start.2 = (bf16[1024,128]{1,0:T(8,128)(2,1)S(1)}, bf16[1024,128]{1,0:T(8,128)(2,1)}, u32[]{:S(2)}) copy-start(bf16[1024,128]{1,0:T(8,128)(2,1)} %root.1) | copy-start | bytes 786436
  0.7 10.7 %collective-permute-start.3 = (bf16[512,128]{1,0:T(8,128)(2,1)}, bf16[512,128]{1,0:T(8,128)(2,1)S(1)}, u32[]{:S(2)}, u32[]{:S(2)}) collective-permute-start(bf16[512,128]{1,0:T(8,128)(2,1)} %feats.1), channel_id=1, source_target_pairs={{0,4},{1,5},{2,6},{3,7},{4,0},{5,1},{6,2},{7,3},{8,12},{9,13},{10,... | collective-permute-start | bytes 393224 | tf_op jit(solution)/shard_map/ppermute | solution.py:172
  4.8 6.8 %collective-permute-start.4 = (bf16[512,128]{1,0:T(8,128)(2,1)}, bf16[512,128]{1,0:T(8,128)(2,1)S(1)}, u32[]{:S(2)}, u32[]{:S(2)}) collective-permute-start(bf16[512,128]{1,0:T(8,128)(2,1)} %feats.1), channel_id=1, source_target_pairs={{0,2},{1,3},{2,0},{3,1},{4,6},{5,7},{6,4},{7,5},{8,10},{9,11},{10,... | collective-permute-start | bytes 393224 | tf_op jit(solution)/shard_map/ppermute | solution.py:172
  10.4 11.5 %copy-start = (bf16[512,2048]{1,0:T(8,128)(2,1)S(1)}, bf16[512,2048]{1,0:T(8,128)(2,1)}, u32[]{:S(2)}) copy-start(bf16[512,2048]{1,0:T(8,128)(2,1)} %shard_map.95.adj.refs_4_) | copy-start | bytes 6291460
  11.6 5.0 %collective-permute-start.7 = (bf16[512,128]{1,0:T(8,128)(2,1)S(1)}, bf16[512,128]{1,0:T(8,128)(2,1)S(1)}, u32[]{:S(2)}, u32[]{:S(2)}) collective-permute-start(bf16[512,128]{1,0:T(8,128)(2,1)S(1)} %collective-permute-done.3.refs_4_), channel_id=1, source_target_pairs={{0,2},{1,3},{2,0},{3,1},{4,6},{5,7},{6,4},{7,5},{8,10},{9,11},{10,... | collective-permute-start | bytes 393224 | tf_op jit(solution)/shard_map/ppermute | solution.py:172
  13.1 3.5 %collective-permute-start.2 = (bf16[512,128]{1,0:T(8,128)(2,1)S(1)}, bf16[512,128]{1,0:T(8,128)(2,1)S(1)}, u32[]{:S(2)}, u32[]{:S(2)}) collective-permute-start(bf16[512,128]{1,0:T(8,128)(2,1)S(1)} %get-tuple-element.36.refs_0_), channel_id=1, source_target_pairs={{0,1},{1,0},{2,3},{3,2},{4,5},{5,4},{6,7},{7,6},{8,9},{9,8},{10,11... | collective-permute-start | bytes 393224 | tf_op jit(solution)/shard_map/ppermute | solution.py:172
  13.2 3.4 %collective-permute-start.6 = (bf16[512,128]{1,0:T(8,128)(2,1)S(1)}, bf16[512,128]{1,0:T(8,128)(2,1)S(1)}, u32[]{:S(2)}, u32[]{:S(2)}) collective-permute-start(bf16[512,128]{1,0:T(8,128)(2,1)S(1)} %collective-permute-done.3.refs_4_), channel_id=1, source_target_pairs={{0,1},{1,0},{2,3},{3,2},{4,5},{5,4},{6,7},{7,6},{8,9},{9,8},{10,11... | collective-permute-start | bytes 393224 | tf_op jit(solution)/shard_map/ppermute | solution.py:172
  13.7 2.9 %collective-permute-start.5 = (bf16[512,128]{1,0:T(8,128)(2,1)S(1)}, bf16[512,128]{1,0:T(8,128)(2,1)S(1)}, u32[]{:S(2)}, u32[]{:S(2)}) collective-permute-start(bf16[512,128]{1,0:T(8,128)(2,1)S(1)} %collective-permute-done.4.refs_2_), channel_id=1, source_target_pairs={{0,1},{1,0},{2,3},{3,2},{4,5},{5,4},{6,7},{7,6},{8,9},{9,8},{10,11... | collective-permute-start | bytes 393224 | tf_op jit(solution)/shard_map/ppermute | solution.py:172
  16.6 1.3 %collective-permute-start.8 = (bf16[512,128]{1,0:T(8,128)(2,1)S(1)}, bf16[512,128]{1,0:T(8,128)(2,1)S(1)}, u32[]{:S(2)}, u32[]{:S(2)}) collective-permute-start(bf16[512,128]{1,0:T(8,128)(2,1)S(1)} %collective-permute-done.7.refs_6_), channel_id=1, source_target_pairs={{0,1},{1,0},{2,3},{3,2},{4,5},{5,4},{6,7},{7,6},{8,9},{9,8},{10,11... | collective-permute-start | bytes 393224 | tf_op jit(solution)/shard_map/ppermute | solution.py:172
  18.3 9.7 %copy-start.4 = (bf16[512,128]{1,0:T(8,128)(2,1)S(1)}, bf16[512,128]{1,0:T(8,128)(2,1)}, u32[]{:S(2)}) copy-start(bf16[512,128]{1,0:T(8,128)(2,1)} %refs_7_.1) | copy-start | bytes 393220
  18.4 7.9 %collective-permute-start.10 = (bf16[512,128]{1,0:T(8,128)(2,1)S(1)}, bf16[512,128]{1,0:T(8,128)(2,1)S(1)}, u32[]{:S(2)}, u32[]{:S(2)}) collective-permute-start(bf16[512,128]{1,0:T(8,128)(2,1)S(1)} %get-tuple-element.42.refs_0_), channel_id=1, source_target_pairs={{0,16},{8,24},{16,0},{24,8},{1,17},{9,25},{17,1},{25,9},{2,18},{10... | collective-permute-start | bytes 393224 | tf_op jit(solution)/shard_map/ppermute | solution.py:172
  20.0 7.3 %collective-permute-start.11 = (bf16[512,128]{1,0:T(8,128)(2,1)S(1)}, bf16[512,128]{1,0:T(8,128)(2,1)S(1)}, u32[]{:S(2)}, u32[]{:S(2)}) collective-permute-start(bf16[512,128]{1,0:T(8,128)(2,1)S(1)} %get-tuple-element.42.refs_0_), channel_id=1, source_target_pairs={{0,24},{8,16},{16,8},{24,0},{1,25},{9,17},{17,9},{25,1},{2,26},{10... | collective-permute-start | bytes 393224 | tf_op jit(solution)/shard_map/ppermute | solution.py:172
  21.4 6.6 %collective-permute-start.9 = (bf16[512,128]{1,0:T(8,128)(2,1)S(1)}, bf16[512,128]{1,0:T(8,128)(2,1)S(1)}, u32[]{:S(2)}, u32[]{:S(2)}) collective-permute-start(bf16[512,128]{1,0:T(8,128)(2,1)S(1)} %get-tuple-element.42.refs_0_), channel_id=1, source_target_pairs={{0,8},{8,0},{16,24},{24,16},{1,9},{9,1},{17,25},{25,17},{2,10},{10... | collective-permute-start | bytes 393224 | tf_op jit(solution)/shard_map/ppermute | solution.py:172
  30.4 6.0 %collective-permute-start.12 = (bf16[512,128]{1,0:T(8,128)(2,1)S(1)}, bf16[512,128]{1,0:T(8,128)(2,1)S(1)}, u32[]{:S(2)}, u32[]{:S(2)}) collective-permute-start(bf16[512,128]{1,0:T(8,128)(2,1)S(1)} %get-tuple-element.45), channel_id=1, source_target_pairs={{0,8},{8,0},{16,24},{24,16},{1,9},{9,1},{17,25},{25,17},{2,10},{10... | collective-permute-start | bytes 393224 | tf_op jit(solution)/shard_map/ppermute | solution.py:172
  32.0 7.7 %collective-permute-start.13 = (bf16[512,128]{1,0:T(8,128)(2,1)S(1)}, bf16[512,128]{1,0:T(8,128)(2,1)S(1)}, u32[]{:S(2)}, u32[]{:S(2)}) collective-permute-start(bf16[512,128]{1,0:T(8,128)(2,1)S(1)} %get-tuple-element.46), channel_id=1, source_target_pairs={{0,16},{8,24},{16,0},{24,8},{1,17},{9,25},{17,1},{25,9},{2,18},{10... | collective-permute-start | bytes 393224 | tf_op jit(solution)/shard_map/ppermute | solution.py:172
  33.5 6.2 %collective-permute-start.14 = (bf16[512,128]{1,0:T(8,128)(2,1)S(1)}, bf16[512,128]{1,0:T(8,128)(2,1)S(1)}, u32[]{:S(2)}, u32[]{:S(2)}) collective-permute-start(bf16[512,128]{1,0:T(8,128)(2,1)S(1)} %get-tuple-element.47), channel_id=1, source_target_pairs={{0,24},{8,16},{16,8},{24,0},{1,25},{9,17},{17,9},{25,1},{2,26},{10... | collective-permute-start | bytes 393224 | tf_op jit(solution)/shard_map/ppermute | solution.py:172
  33.9 7.7 %collective-permute-start.17 = (bf16[2,512,128]{2,1,0:T(8,128)(2,1)S(1)}, bf16[2,512,128]{2,1,0:T(8,128)(2,1)S(1)}, u32[]{:S(2)}, u32[]{:S(2)}) collective-permute-start(bf16[2,512,128]{2,1,0:T(8,128)(2,1)S(1)} %get-tuple-element.41.refs_9_), channel_id=1, source_target_pairs={{0,1},{1,0},{2,3},{3,2},{4,5},{5,4},{6,7},{7,6},{8,9},{9,8},{10,11... | collective-permute-start | bytes 786440 | tf_op jit(solution)/shard_map/ppermute | solution.py:172
  34.3 12.6 %copy-start.5 = (s32[4]{0:T(128)S(1)}, s32[4]{0:T(128)}, u32[]{:S(2)}) copy-start(s32[4]{0:T(128)} %all_counts.1) | copy-start | bytes 52
  34.3 7.4 %collective-permute-start.16 = (bf16[512,128]{1,0:T(8,128)(2,1)S(1)}, bf16[512,128]{1,0:T(8,128)(2,1)S(1)}, u32[]{:S(2)}, u32[]{:S(2)}) collective-permute-start(bf16[512,128]{1,0:T(8,128)(2,1)S(1)} %get-tuple-element.48.pre), channel_id=1, source_target_pairs={{0,1},{1,0},{2,3},{3,2},{4,5},{5,4},{6,7},{7,6},{8,9},{9,8},{10,11... | collective-permute-start | bytes 393224 | tf_op jit(solution)/shard_map/ppermute | solution.py:172
  39.8 1.9 %collective-permute-start.15 = (bf16[512,128]{1,0:T(8,128)(2,1)S(1)}, bf16[512,128]{1,0:T(8,128)(2,1)S(1)}, u32[]{:S(2)}, u32[]{:S(2)}) collective-permute-start(bf16[512,128]{1,0:T(8,128)(2,1)S(1)} %shard_map.99.hidden), channel_id=1, source_target_pairs={{0,1},{1,0},{2,3},{3,2},{4,5},{5,4},{6,7},{7,6},{8,9},{9,8},{10,11... | collective-permute-start | bytes 393224 | tf_op jit(solution)/shard_map/ppermute | solution.py:172
  40.3 8.8 %collective-permute-start.21 = (bf16[1024,128]{1,0:T(8,128)(2,1)S(1)}, bf16[1024,128]{1,0:T(8,128)(2,1)S(1)}, u32[]{:S(2)}, u32[]{:S(2)}) collective-permute-start(bf16[1024,128]{1,0:T(8,128)(2,1)S(1)} %get-tuple-element.53.weight), channel_id=1, source_target_pairs={{0,16},{8,24},{16,0},{24,8},{1,17},{9,25},{17,1},{25,9},{2,18},{10... | collective-permute-start | bytes 786440 | tf_op jit(solution)/shard_map/ppermute | solution.py:172
  41.4 8.4 %collective-permute-start.22 = (bf16[1024,128]{1,0:T(8,128)(2,1)S(1)}, bf16[1024,128]{1,0:T(8,128)(2,1)S(1)}, u32[]{:S(2)}, u32[]{:S(2)}) collective-permute-start(bf16[1024,128]{1,0:T(8,128)(2,1)S(1)} %get-tuple-element.54.root), channel_id=1, source_target_pairs={{0,8},{8,0},{16,24},{24,16},{1,9},{9,1},{17,25},{25,17},{2,10},{10... | collective-permute-start | bytes 786440 | tf_op jit(solution)/shard_map/ppermute | solution.py:172
  42.4 16.3 %collective-permute-start.18 = (bf16[512,128]{1,0:T(8,128)(2,1)S(1)}, bf16[512,128]{1,0:T(8,128)(2,1)S(1)}, u32[]{:S(2)}, u32[]{:S(2)}) collective-permute-start(bf16[512,128]{1,0:T(8,128)(2,1)S(1)} %get-tuple-element.50), channel_id=1, source_target_pairs={{0,2},{1,3},{2,0},{3,1},{4,6},{5,7},{6,4},{7,5},{8,10},{9,11},{10,... | collective-permute-start | bytes 393224 | tf_op jit(solution)/shard_map/ppermute | solution.py:172
  43.9 14.8 %collective-permute-start.19 = (bf16[512,128]{1,0:T(8,128)(2,1)S(1)}, bf16[512,128]{1,0:T(8,128)(2,1)S(1)}, u32[]{:S(2)}, u32[]{:S(2)}) collective-permute-start(bf16[512,128]{1,0:T(8,128)(2,1)S(1)} %get-tuple-element.51), channel_id=1, source_target_pairs={{0,4},{1,5},{2,6},{3,7},{4,0},{5,1},{6,2},{7,3},{8,12},{9,13},{10,... | collective-permute-start | bytes 393224 | tf_op jit(solution)/shard_map/ppermute | solution.py:172
  46.7 12.0 %collective-permute-start.20 = (bf16[512,128]{1,0:T(8,128)(2,1)S(1)}, bf16[512,128]{1,0:T(8,128)(2,1)S(1)}, u32[]{:S(2)}, u32[]{:S(2)}) collective-permute-start(bf16[512,128]{1,0:T(8,128)(2,1)S(1)} %get-tuple-element.52), channel_id=1, source_target_pairs={{0,6},{1,7},{2,4},{3,5},{4,2},{5,3},{6,0},{7,1},{8,14},{9,15},{10,... | collective-permute-start | bytes 393224 | tf_op jit(solution)/shard_map/ppermute | solution.py:172
  49.9 7.7 %collective-permute-start = (bf16[1024,128]{1,0:T(8,128)(2,1)S(1)}, bf16[1024,128]{1,0:T(8,128)(2,1)S(1)}, u32[]{:S(2)}, u32[]{:S(2)}) collective-permute-start(bf16[1024,128]{1,0:T(8,128)(2,1)S(1)} %get-tuple-element.4.weight), channel_id=1, source_target_pairs={{0,8},{8,0},{16,24},{24,16},{1,9},{9,1},{17,25},{25,17},{2,10},{10... | collective-permute-start | bytes 786440 | tf_op jit(solution)/shard_map/cond/branch_1_fun/ppermute | solution.py:172
  50.3 7.4 %collective-permute-start.1 = (bf16[1024,128]{1,0:T(8,128)(2,1)S(1)}, bf16[1024,128]{1,0:T(8,128)(2,1)S(1)}, u32[]{:S(2)}, u32[]{:S(2)}) collective-permute-start(bf16[1024,128]{1,0:T(8,128)(2,1)S(1)} %get-tuple-element.5.root), channel_id=1, source_target_pairs={{0,16},{8,24},{16,0},{24,8},{1,17},{9,25},{17,1},{25,9},{2,18},{10... | collective-permute-start | bytes 786440 | tf_op jit(solution)/shard_map/cond/branch_1_fun/ppermute | solution.py:172

commit v4 on v3

--- a/solution.py
+++ b/solution.py
@@ -110,26 +110,35 @@
         out[rows, :] = pieces[m][...].T
 
 
+def begin_kernel(adj, hidden, own, pre):
+    rows = own.shape[0]
+    place = pl.ds(pl.multiple_of(lax.axis_index("rows") * rows, rows), rows)
+    pre[...] = own[...] + dot(adj[:, place], hidden[...])
+
+
 def aggregate_kernel(nr, *refs):
-    hidden = refs[:nr]
-    adj, adj_t, own, grad_out, grad_pre, kept = refs[nr : nr + 6]
-    sent = refs[nr + 6 :]
+    hidden = refs[: nr - 1]
+    adj, adj_t, begun, grad_out, grad_pre = refs[nr - 1 : nr + 4]
+    sent = refs[nr + 4 :]
     me = lax.axis_index("rows")
-    rows = own.shape[0]
-    pre = own[...]
-    for j in range(nr):
+    rows = begun.shape[0]
+    pre = begun[...]
+    for j in range(1, nr):
         place = pl.ds(pl.multiple_of((me ^ j) * rows, rows), rows)
-        pre = pre + dot(adj[:, place], hidden[j][...])
+        pre = pre + dot(adj[:, place], hidden[j - 1][...])
     sig = jax.nn.sigmoid(pre)
     grad = (grad_out[...].astype(F32) * sig * (1.0 + pre * (1.0 - sig))).astype(BF)
     grad_pre[...] = grad
-    for j in range(nr):
+    for j in range(1, nr):
         place = pl.ds(pl.multiple_of((me ^ j) * rows, rows), rows)
-        part = dot(adj_t[place, :], grad)
-        if j == 0:
-            kept[...] = part
-        else:
-            sent[j - 1][...] = part.astype(BF)
+        sent[j - 1][...] = dot(adj_t[place, :], grad).astype(BF)
+
+
+def keep_kernel(adj_t, grad_pre, feats_t, kept, top, bottom):
+    rows = kept.shape[0]
+    place = pl.ds(pl.multiple_of(lax.axis_index("rows") * rows, rows), rows)
+    kept[...] = dot(adj_t[place, :], grad_pre[...])
+    weights_kernel(feats_t, grad_pre, top, bottom)
 
 
 def sum_kernel(n, *refs):
@@ -148,17 +157,32 @@
         out[k][...] = dot_nt(left, jnp.concatenate(right, 1)).astype(out[k].dtype)
 
 
-def weights_kernel(feats_t, hidden, pre, weight, root):
-    width = weight.shape[1]
-    both = dot(feats_t[...], jnp.concatenate([hidden[...], pre[...]], 1))
-    weight[...] = both[:, :width].astype(BF)
-    root[...] = both[:, width:].astype(BF)
-
-
-def pair_sum_kernel(weight, weight_2, root, root_2, weight_sum, root_sum):
-    for out, terms in ((weight_sum, (weight, weight_2)), (root_sum, (root, root_2))):
+def weights_kernel(feats_t, grads, top, bottom):
+    half = top.shape[0]
+    top[...] = dot(feats_t[:half, :], grads[...]).astype(BF)
+    bottom[...] = dot(feats_t[half:, :], grads[...]).astype(BF)
+
+
+def join_kernel(*refs):
+    terms, outs = refs[:8], refs[8:]
+    for half, out in enumerate(outs):
+        weight = terms[half][...].astype(F32) + terms[half + 2][...].astype(F32)
+        root = terms[half + 4][...].astype(F32) + terms[half + 6][...].astype(F32)
+        out[...] = jnp.concatenate([weight, root], 1).astype(BF)
+
+
+def pair_sum_kernel(top, top_2, bottom, bottom_2, top_sum, bottom_sum):
+    for out, terms in ((top_sum, (top, top_2)), (bottom_sum, (bottom, bottom_2))):
         total = terms[0][...].astype(F32) + terms[1][...].astype(F32)
-        out[...] = total.astype(out.dtype)
+        out[...] = total.astype(BF)
+
+
+def place_kernel(top, top_2, bottom, bottom_2, weight, root):
+    half, width = top.shape[0], weight.shape[1]
+    for at, terms in ((0, (top, top_2)), (half, (bottom, bottom_2))):
+        total = terms[0][...].astype(F32) + terms[1][...].astype(F32)
+        weight[at : at + half, :] = total[:, :width]
+        root[at : at + half, :] = total[:, width:]
 
 
 def on_device(node_feats, weight, root_weight, grad_out, block_counts, tile_cols, tile_vals):
@@ -195,19 +219,12 @@
     (adj_t,) = call(
         functools.partial(flip_kernel, tile_vals.shape[1]), [sds((nodes, rows), BF)], [VMEM], (adj,)
     )
-    masks = [1 << bit for bit in range(1, nf.bit_length() - 1)]
-    moved = {0: node_feats}
-    for mask in reversed(masks):
-        if mask == masks[0]:
-            ahead = {0: node_feats, mask: swap(node_feats, "feat", mask)}
-            ahead |= {m: piece for m, piece in moved.items() if m}
-            order = sorted(ahead, reverse=True)
-            moved = dict(zip(order, lax.optimization_barrier((*[ahead[m] for m in order], adj))))
-            moved |= {m | mask: swap(moved[m], "feat", mask) for m in order if m and m != mask}
-        else:
-            moved |= {m | mask: swap(piece, "feat", mask) for m, piece in moved.items()}
+    ranks = sorted(range(1, nz), key=lambda k: (k < nz // 2, k))
+    moved = {0: node_feats} | {2 * k: swap(node_feats, "feat", 2 * k) for k in ranks}
+    order = [2 * k for k in ranks]
+    moved |= dict(zip(order, lax.optimization_barrier((*[moved[m] for m in order], adj))))
     moved[0] = mine
-    late = [m for m in moved if m & masks[0] and m != masks[0]]
+    late = [m for m in moved if m == 2 * nz - 2]
     moved |= dict(zip(late, lax.optimization_barrier((*[moved[m] for m in late], near))))
     pieces = []
     for m in sorted(moved):
@@ -227,13 +244,28 @@
         [VMEM] * nf,
         pieces,
     )
-    grad_pre, kept, *sent = call(
+    adj_t, near_2 = lax.optimization_barrier((adj_t, near_2))
+    (begun,) = call(
+        begin_kernel,
+        [sds((rows, width), F32)],
+        [VMEM] * 3,
+        (adj, hidden, own),
+        flops=2 * rows * rows * width,
+    )
+    grad_pre, *sent = call(
         functools.partial(aggregate_kernel, nr),
-        [sds((rows, width), BF), sds((rows, width), F32)] + [sds((rows, width), BF)] * (nr - 1),
-        [VMEM] * (nr + 4),
-        (*gathered, adj, adj_t, own, grad_out),
+        [sds((rows, width), BF)] * nr,
+        [VMEM] * (nr + 3),
+        (*gathered[1:], adj, adj_t, begun, grad_out),
         flops=4 * rows * nodes * width,
         limit=max(32 * 1024 * 1024, 10 * rows * nodes),
+    )
+    kept, *root_part = call(
+        keep_kernel,
+        [sds((rows, width), F32)] + [sds((depth // 2, width), BF)] * 2,
+        [VMEM] * 3,
+        (adj_t, grad_pre, feats_t),
+        flops=4 * rows * depth * width,
     )
     pre_2 = swap(grad_pre, "feat", 1)
     sums = [kept] + [swap(part, "rows", j + 1) for j, part in enumerate(sent)]
@@ -248,33 +280,35 @@
         (grad_hidden, grad_pre, hidden_2, pre_2, near, near_2),
         flops=4 * rows * depth * width,
     )
+    weight_part = call(
+        weights_kernel,
+        [sds((depth // 2, width), BF)] * 2,
+        [VMEM] * 2,
+        (feats_t, grad_hidden),
+        flops=2 * rows * depth * width,
+    )
+    steps = [1 << bit for bit in range(nr.bit_length() - 1)]
+    first, *between, final = zip(steps, reversed(steps))
+    root_got = [swap(part, "rows", mask) for part, mask in zip(root_part, first)]
+    *weight_part, root_got[0], root_got[1] = lax.optimization_barrier((*weight_part, *root_got))
+    weight_got = [swap(part, "rows", mask) for part, mask in zip(weight_part, first)]
+    sums_f = [parts[0]] + [swap(parts[k], "feat", 2 * k) for k in ranks]
+    joined = [sds((depth // 2, 2 * width), BF)] * 2
     grads = call(
-        weights_kernel,
-        [sds((depth, width), BF)] * 2,
-        [VMEM] * 3,
-        (feats_t, grad_hidden, grad_pre),
-        flops=4 * rows * depth * width,
-    )
-    sums_f = [parts[0]] + [swap(part, "feat", 2 * k) for k, part in enumerate(parts) if k]
-    steps = [1 << bit for bit in range(nr.bit_length() - 1)]
-    *between, final = zip(reversed(steps), steps)
-    for there, back in between:
-        other = swap(grads[0], "rows", there), swap(grads[1], "rows", back)
-        grads = call(
-            pair_sum_kernel,
-            [sds((depth, width), BF)] * 2,
-            [VMEM] * 4,
-            (grads[0], other[0], grads[1], other[1]),
-        )
+        join_kernel, joined, [VMEM] * 8, (*weight_part, *weight_got, *root_part, *root_got)
+    )
+    for masks in between:
+        got = [swap(part, "rows", mask) for part, mask in zip(grads, masks)]
+        grads = call(pair_sum_kernel, joined, [VMEM] * 4, (grads[0], got[0], grads[1], got[1]))
 
     def finish(grads):
-        other = swap(grads[0], "rows", final[0]), swap(grads[1], "rows", final[1])
+        got = [swap(part, "rows", mask) for part, mask in zip(grads, final)]
         return tuple(
             call(
-                pair_sum_kernel,
+                place_kernel,
                 [sds((depth, width), F32)] * 2,
                 [VMEM] * 4,
-                (grads[0], other[0], grads[1], other[1]),
+                (grads[0], got[0], grads[1], got[1]),
             )
         )
 
@@ -284,7 +318,10 @@
     grad_weight, grad_root = lax.cond(block_counts[0] > 0, finish, skip, tuple(grads))
     *sums_f, grad_weight, grad_root = lax.optimization_barrier((*sums_f, grad_weight, grad_root))
     (grad_feats,) = call(
-        functools.partial(sum_kernel, len(sums_f)), [sds((rows, width), BF)], [VMEM] * len(sums_f), sums_f
+        functools.partial(sum_kernel, len(sums_f)),
+        [sds((rows, width), BF)],
+        [VMEM] * len(sums_f),
+        sums_f,
     )
     return grad_feats, grad_weight, grad_root
 

time: 59.6 us -> 58.3 us (0.978)
  waiting for transfers between devices: 23.9 us -> 15.5 us
  local copies, waits for them, and re-layouts: 0.03 us -> 4.41 us
  starting transfers between devices: 23 us -> 24.9 us
    ppermute x23 -> x25, waiting for transfers between devices: 23.9 us -> 15.5 us  [swap(): lax.ppermute(array, axis, [(i, i ^ mask) for i in range(lax.axis_size(axi...]
    unnamed x12, local copies, waits for them, and re-layouts: 0.03 us -> 4.41 us
    ppermute x23 -> x25, starting transfers between devices: 23 us -> 24.9 us  [swap(): lax.ppermute(array, axis, [(i, i ^ mask) for i in range(lax.axis_size(axi...]
    pallas_call x12 -> x14, Pallas kernels: 11.7 us -> 12.2 us  [call(): pl.pallas_call(body, out_shape=outs, in_specs=specs, out_specs=[VMEM] * l...]
  transfers between devices with their start and end apart: 23 -> 25, of which waited for: 13 -> 13; matrix products, arithmetic and copies ran while one was open for 0% -> 0% of each run, Pallas kernels for 14% -> 17%
where the time goes in v4:
time: 58.3 us; the launch traced here: 58 us
  starting transfers between devices  24.9 us (43%)
  waiting for transfers between devices  15.5 us (27%)
  Pallas kernels  12.2 us (21%)
  local copies, waits for them, and re-layouts  4.41 us (8%)
  between operations  0.84 us (1%)
    ppermute x25, starting transfers between devices, swap(): lax.ppermute(array, axis, [(i, i ^ mask) for i in range(lax.axis_size(axi...  24.9 us
    ppermute x25, waiting for transfers between devices, swap(): lax.ppermute(array, axis, [(i, i ^ mask) for i in range(lax.axis_size(axi...  15.5 us
    pallas_call x14, Pallas kernels, call(): pl.pallas_call(body, out_shape=outs, in_specs=specs, out_specs=[VMEM] * l...  12.2 us
    unnamed x12, local copies, waits for them, and re-layouts  4.41 us
  transfers between devices with their start and end apart: 25, of which 13 were waited for; matrix products, arithmetic and copies ran while one was open for 0% of the time, Pallas kernels for 17%

profile of v4, /device:TPU:0, one launch (start us, length us, event | category | flops | bytes accessed | tf_op | source)
XLA Modules:
  0.0 58.0 jit_solution(1275539267814665371)
XLA Ops:
  0.6 4.1 %collective-permute-start.4 = (bf16[512,128]{1,0:T(8,128)(2,1)}, bf16[512,128]{1,0:T(8,128)(2,1)S(1)}, u32[]{:S(2)}, u32[]{:S(2)}) collective-permute-start(bf16[512,128]{1,0:T(8,128)(2,1)} %feats.1), channel_id=1, source_target_pairs={{0,4},{1,5},{2,6},{3,7},{4,0},{5,1},{6,2},{7,3},{8,12},{9,13},{10,... | collective-permute-start | bytes 393224 | tf_op jit(solution)/shard_map/ppermute | solution.py:196
  4.7 1.3 %collective-permute-start.5 = (bf16[512,128]{1,0:T(8,128)(2,1)}, bf16[512,128]{1,0:T(8,128)(2,1)S(1)}, u32[]{:S(2)}, u32[]{:S(2)}) collective-permute-start(bf16[512,128]{1,0:T(8,128)(2,1)} %feats.1), channel_id=1, source_target_pairs={{0,6},{1,7},{2,4},{3,5},{4,2},{5,3},{6,0},{7,1},{8,14},{9,15},{10,... | collective-permute-start | bytes 393224 | tf_op jit(solution)/shard_map/ppermute | solution.py:196
  6.3 0.9 %copy-done.1 = bf16[1024,128]{1,0:T(8,128)(2,1)S(1)} copy-done((bf16[1024,128]{1,0:T(8,128)(2,1)S(1)}, bf16[1024,128]{1,0:T(8,128)(2,1)}, u32[]{:S(2)}) %copy-start.1) | copy-done | bytes 262168
  7.3 0.9 %copy-done.2 = bf16[1024,128]{1,0:T(8,128)(2,1)S(1)} copy-done((bf16[1024,128]{1,0:T(8,128)(2,1)S(1)}, bf16[1024,128]{1,0:T(8,128)(2,1)}, u32[]{:S(2)}) %copy-start.2) | copy-done | bytes 262168
  8.2 0.9 %copy-done.3 = bf16[512,128]{1,0:T(8,128)(2,1)S(1)} copy-done((bf16[512,128]{1,0:T(8,128)(2,1)S(1)}, bf16[512,128]{1,0:T(8,128)(2,1)}, u32[]{:S(2)}) %copy-start.3) | copy-done | bytes 131096
  9.2 4.2 %shard_map.94.adj.refs_3_ = bf16[512,2048]{1,0:T(8,128)(2,1)} custom-call(s32[4]{0:T(128)} %all_counts.1, s32[80]{0:T(128)} %all_cols.1, bf16[80,128,128]{2,1,0:T(8,128)(2,1)} %vals.1), custom_call_target="tpu_custom_call" | custom-call | flops 4194304 | bytes 4718928 | tf_op jit(solution)/shard_map/pallas_call | solution.py:28
  13.5 1.5 %collective-permute-done.4.refs_4_ = bf16[512,128]{1,0:T(8,128)(2,1)S(1)} collective-permute-done((bf16[512,128]{1,0:T(8,128)(2,1)}, bf16[512,128]{1,0:T(8,128)(2,1)S(1)}, u32[]{:S(2)}, u32[]{:S(2)}) %collective-permute-start.4) | collective-permute-done | bytes 131104 | tf_op jit(solution)/shard_map/ppermute | solution.py:196
  17.7 1.6 %collective-permute-start.10 = (bf16[512,128]{1,0:T(8,128)(2,1)S(1)}, bf16[512,128]{1,0:T(8,128)(2,1)S(1)}, u32[]{:S(2)}, u32[]{:S(2)}) collective-permute-start(bf16[512,128]{1,0:T(8,128)(2,1)S(1)} %get-tuple-element.53.hidden), channel_id=1, source_target_pairs={{0,8},{8,0},{16,24},{24,16},{1,9},{9,1},{17,25},{25,17},{2,10},{10... | collective-permute-start | bytes 393224 | tf_op jit(solution)/shard_map/ppermute | solution.py:196
  19.4 1.5 %collective-permute-start.11 = (bf16[512,128]{1,0:T(8,128)(2,1)S(1)}, bf16[512,128]{1,0:T(8,128)(2,1)S(1)}, u32[]{:S(2)}, u32[]{:S(2)}) collective-permute-start(bf16[512,128]{1,0:T(8,128)(2,1)S(1)} %get-tuple-element.53.hidden), channel_id=1, source_target_pairs={{0,16},{8,24},{16,0},{24,8},{1,17},{9,25},{17,1},{25,9},{2,18},{10... | collective-permute-start | bytes 393224 | tf_op jit(solution)/shard_map/ppermute | solution.py:196
  21.3 1.6 %copy-done = bf16[512,2048]{1,0:T(8,128)(2,1)S(1)} copy-done((bf16[512,2048]{1,0:T(8,128)(2,1)S(1)}, bf16[512,2048]{1,0:T(8,128)(2,1)}, u32[]{:S(2)}) %copy-start) | copy-done | bytes 2097176
  22.9 1.4 %shard_map.95.refs_4_.adj_t = bf16[2048,512]{1,0:T(8,128)(2,1)S(1)} custom-call(bf16[512,2048]{1,0:T(8,128)(2,1)S(1)} %copy-done), custom_call_target="tpu_custom_call" | custom-call | bytes 4194304 | tf_op jit(solution)/shard_map/pallas_call | solution.py:28
  24.7 2.8 %collective-permute-done.11.refs_1_ = bf16[512,128]{1,0:T(8,128)(2,1)S(1)} collective-permute-done((bf16[512,128]{1,0:T(8,128)(2,1)S(1)}, bf16[512,128]{1,0:T(8,128)(2,1)S(1)}, u32[]{:S(2)}, u32[]{:S(2)}) %collective-permute-start.11) | collective-permute-done | bytes 131104 | tf_op jit(solution)/shard_map/ppermute | solution.py:196
  27.5 1.8 %shard_map.99 = (bf16[512,128]{1,0:T(8,128)(2,1)S(1)}, bf16[512,128]{1,0:T(8,128)(2,1)S(1)}, bf16[512,128]{1,0:T(8,128)(2,1)S(1)}, bf16[512,128]{1,0:T(8,128)(2,1)S(1)}) custom-call(bf16[512,128]{1,0:T(8,128)(2,1)S(1)} %collective-permute-done.10.refs_0_, bf16[512,128]{1,0:T(8,128)(2,1)S(1)} %collective-permute-done.11.refs_1_, ...), custom_call_target="tpu_custom_call" | custom-call | flops 536870912 | bytes 5505024 | tf_op jit(solution)/shard_map/pallas_call | solution.py:28
  29.3 1.3 %collective-permute-start.13 = (bf16[512,128]{1,0:T(8,128)(2,1)S(1)}, bf16[512,128]{1,0:T(8,128)(2,1)S(1)}, u32[]{:S(2)}, u32[]{:S(2)}) collective-permute-start(bf16[512,128]{1,0:T(8,128)(2,1)S(1)} %get-tuple-element.57), channel_id=1, source_target_pairs={{0,8},{8,0},{16,24},{24,16},{1,9},{9,1},{17,25},{25,17},{2,10},{10... | collective-permute-start | bytes 393224 | tf_op jit(solution)/shard_map/ppermute | solution.py:196
  30.6 0.8 %collective-permute-start.14 = (bf16[512,128]{1,0:T(8,128)(2,1)S(1)}, bf16[512,128]{1,0:T(8,128)(2,1)S(1)}, u32[]{:S(2)}, u32[]{:S(2)}) collective-permute-start(bf16[512,128]{1,0:T(8,128)(2,1)S(1)} %get-tuple-element.58), channel_id=1, source_target_pairs={{0,16},{8,24},{16,0},{24,8},{1,17},{9,25},{17,1},{25,9},{2,18},{10... | collective-permute-start | bytes 393224 | tf_op jit(solution)/shard_map/ppermute | solution.py:196
  31.4 1.4 %collective-permute-start.15 = (bf16[512,128]{1,0:T(8,128)(2,1)S(1)}, bf16[512,128]{1,0:T(8,128)(2,1)S(1)}, u32[]{:S(2)}, u32[]{:S(2)}) collective-permute-start(bf16[512,128]{1,0:T(8,128)(2,1)S(1)} %get-tuple-element.59), channel_id=1, source_target_pairs={{0,24},{8,16},{16,8},{24,0},{1,25},{9,17},{17,9},{25,1},{2,26},{10... | collective-permute-start | bytes 393224 | tf_op jit(solution)/shard_map/ppermute | solution.py:196
  33.8 1.3 %collective-permute-start.21 = (bf16[512,128]{1,0:T(8,128)(2,1)S(1)}, bf16[512,128]{1,0:T(8,128)(2,1)S(1)}, u32[]{:S(2)}, u32[]{:S(2)}) collective-permute-start(bf16[512,128]{1,0:T(8,128)(2,1)S(1)} %get-tuple-element.67.refs_4_), channel_id=1, source_target_pairs={{0,8},{8,0},{16,24},{24,16},{1,9},{9,1},{17,25},{25,17},{2,10},{10... | collective-permute-start | bytes 393224 | tf_op jit(solution)/shard_map/ppermute | solution.py:196
  35.1 0.8 %collective-permute-start.22 = (bf16[512,128]{1,0:T(8,128)(2,1)S(1)}, bf16[512,128]{1,0:T(8,128)(2,1)S(1)}, u32[]{:S(2)}, u32[]{:S(2)}) collective-permute-start(bf16[512,128]{1,0:T(8,128)(2,1)S(1)} %get-tuple-element.68.refs_5_), channel_id=1, source_target_pairs={{0,16},{8,24},{16,0},{24,8},{1,17},{9,25},{17,1},{25,9},{2,18},{10... | collective-permute-start | bytes 393224 | tf_op jit(solution)/shard_map/ppermute | solution.py:196
  35.9 1.5 %collective-permute-done.14.refs_2_ = bf16[512,128]{1,0:T(8,128)(2,1)S(1)} collective-permute-done((bf16[512,128]{1,0:T(8,128)(2,1)S(1)}, bf16[512,128]{1,0:T(8,128)(2,1)S(1)}, u32[]{:S(2)}, u32[]{:S(2)}) %collective-permute-start.14) | collective-permute-done | bytes 131104 | tf_op jit(solution)/shard_map/ppermute | solution.py:196
  37.4 1.8 %collective-permute-done.15.refs_3_ = bf16[512,128]{1,0:T(8,128)(2,1)S(1)} collective-permute-done((bf16[512,128]{1,0:T(8,128)(2,1)S(1)}, bf16[512,128]{1,0:T(8,128)(2,1)S(1)}, u32[]{:S(2)}, u32[]{:S(2)}) %collective-permute-start.15) | collective-permute-done | bytes 131104 | tf_op jit(solution)/shard_map/ppermute | solution.py:196
  40.0 0.7 %collective-permute-done.22.refs_7_ = bf16[512,128]{1,0:T(8,128)(2,1)S(1)} collective-permute-done((bf16[512,128]{1,0:T(8,128)(2,1)S(1)}, bf16[512,128]{1,0:T(8,128)(2,1)S(1)}, u32[]{:S(2)}, u32[]{:S(2)}) %collective-permute-start.22) | collective-permute-done | bytes 131104 | tf_op jit(solution)/shard_map/ppermute | solution.py:196
  40.7 1.2 %collective-permute-start.23 = (bf16[512,128]{1,0:T(8,128)(2,1)S(1)}, bf16[512,128]{1,0:T(8,128)(2,1)S(1)}, u32[]{:S(2)}, u32[]{:S(2)}) collective-permute-start(bf16[512,128]{1,0:T(8,128)(2,1)S(1)} %get-tuple-element.69.refs_0_), channel_id=1, source_target_pairs={{0,8},{8,0},{16,24},{24,16},{1,9},{9,1},{17,25},{25,17},{2,10},{10... | collective-permute-start | bytes 393224 | tf_op jit(solution)/shard_map/ppermute | solution.py:196
  41.9 0.9 %collective-permute-start.24 = (bf16[512,128]{1,0:T(8,128)(2,1)S(1)}, bf16[512,128]{1,0:T(8,128)(2,1)S(1)}, u32[]{:S(2)}, u32[]{:S(2)}) collective-permute-start(bf16[512,128]{1,0:T(8,128)(2,1)S(1)} %get-tuple-element.70.refs_1_), channel_id=1, source_target_pairs={{0,16},{8,24},{16,0},{24,8},{1,17},{9,25},{17,1},{25,9},{2,18},{10... | collective-permute-start | bytes 393224 | tf_op jit(solution)/shard_map/ppermute | solution.py:196
  42.9 0.7 %shard_map.103 = (f32[512,128]{1,0:T(8,128)S(1)}, bf16[512,128]{1,0:T(8,128)(2,1)S(1)}, bf16[512,128]{1,0:T(8,128)(2,1)S(1)}, bf16[512,128]{1,0:T(8,128)(2,1)S(1)}) custom-call(bf16[512,128]{1,0:T(8,128)(2,1)S(1)} %shard_map.102.hidden.grads, bf16[512,128]{1,0:T(8,128)(2,1)S(1)} %get-tuple-element.55.grad_pre.pre, ...), custom_call_target="tpu_custom_call" | custom-call | flops 268435456 | bytes 1703936 | tf_op jit(solution)/shard_map/pallas_call | solution.py:28
  43.6 4.1 %collective-permute-start.18 = (bf16[512,128]{1,0:T(8,128)(2,1)S(1)}, bf16[512,128]{1,0:T(8,128)(2,1)S(1)}, u32[]{:S(2)}, u32[]{:S(2)}) collective-permute-start(bf16[512,128]{1,0:T(8,128)(2,1)S(1)} %get-tuple-element.62), channel_id=1, source_target_pairs={{0,4},{1,5},{2,6},{3,7},{4,0},{5,1},{6,2},{7,3},{8,12},{9,13},{10,... | collective-permute-start | bytes 393224 | tf_op jit(solution)/shard_map/ppermute | solution.py:196
  48.5 8.6 %conditional.1 = ((f32[1024,128]{1,0:T(8,128)}, f32[1024,128]{1,0:T(8,128)})) conditional(s32[]{:T(128)} %bitcast, () %tuple.22, (bf16[512,256]{1,0:T(8,128)(2,1)S(1)}, bf16[512,256]{1,0:T(8,128)(2,1)S(1)}) %shard_map.105), branch_computations={%region_0.0_spmd, %region_1.0_spmd} | conditional | bytes 4194392 | solution.py:318
  48.6 1.2 %collective-permute-start = (bf16[512,256]{1,0:T(8,128)(2,1)S(1)}, bf16[512,256]{1,0:T(8,128)(2,1)S(1)}, u32[]{:S(2)}, u32[]{:S(2)}) collective-permute-start(bf16[512,256]{1,0:T(8,128)(2,1)S(1)} %get-tuple-element.4.top), channel_id=1, source_target_pairs={{0,16},{8,24},{16,0},{24,8},{1,17},{9,25},{17,1},{25,9},{2,18},{10... | collective-permute-start | bytes 786440 | tf_op jit(solution)/shard_map/cond/branch_1_fun/ppermute | solution.py:196
  49.7 0.8 %collective-permute-start.1 = (bf16[512,256]{1,0:T(8,128)(2,1)S(1)}, bf16[512,256]{1,0:T(8,128)(2,1)S(1)}, u32[]{:S(2)}, u32[]{:S(2)}) collective-permute-start(bf16[512,256]{1,0:T(8,128)(2,1)S(1)} %get-tuple-element.5.bottom), channel_id=1, source_target_pairs={{0,8},{8,0},{16,24},{24,16},{1,9},{9,1},{17,25},{25,17},{2,10},{10... | collective-permute-start | bytes 786440 | tf_op jit(solution)/shard_map/cond/branch_1_fun/ppermute | solution.py:196
  50.5 4.6 %collective-permute-done.top_2 = bf16[512,256]{1,0:T(8,128)(2,1)S(1)} collective-permute-done((bf16[512,256]{1,0:T(8,128)(2,1)S(1)}, bf16[512,256]{1,0:T(8,128)(2,1)S(1)}, u32[]{:S(2)}, u32[]{:S(2)}) %collective-permute-start) | collective-permute-done | bytes 262176 | tf_op jit(solution)/shard_map/cond/branch_1_fun/ppermute | solution.py:196
  55.2 0.9 %collective-permute-done.1.bottom_2 = bf16[512,256]{1,0:T(8,128)(2,1)S(1)} collective-permute-done((bf16[512,256]{1,0:T(8,128)(2,1)S(1)}, bf16[512,256]{1,0:T(8,128)(2,1)S(1)}, u32[]{:S(2)}, u32[]{:S(2)}) %collective-permute-start.1) | collective-permute-done | bytes 262176 | tf_op jit(solution)/shard_map/cond/branch_1_fun/ppermute | solution.py:196
  56.1 1.1 %branch_1_fun.1 = (f32[1024,128]{1,0:T(8,128)}, f32[1024,128]{1,0:T(8,128)}) custom-call(bf16[512,256]{1,0:T(8,128)(2,1)S(1)} %get-tuple-element.4.top, bf16[512,256]{1,0:T(8,128)(2,1)S(1)} %collective-permute-done.top_2, bf16[512,256]{1,0:T(8,128)(2,1)S(1)} %get-tuple-element.5.bottom, bf16[512,256]{1,0:T(8,128)(2,1)S(1)} %collective-permute-done.1.bottom_2), custom_call_target="tpu_custom_call" | custom-call | bytes 2097152 | tf_op jit(solution)/shard_map/cond/branch_1_fun/pallas_call | solution.py:28
  57.3 0.7 %shard_map.106 = bf16[512,128]{1,0:T(8,128)(2,1)} custom-call(f32[512,128]{1,0:T(8,128)S(1)} %get-tuple-element.75.refs_0_, bf16[512,128]{1,0:T(8,128)(2,1)S(1)} %collective-permute-done.18.refs_1_, bf16[512,128]{1,0:T(8,128)(2,1)S(1)} %collective-permute-done.19.refs_2_, bf16[512,128]{1,0:T(8,128)(2,1)S(1)} %collective-permute-done.20.refs_3_), custom_call_target="tpu_custom_call" | custom-call | bytes 786432 | tf_op jit(solution)/shard_map/pallas_call | solution.py:28
  (45 shorter events, 6.5 us)
Async XLA Ops:
  0.6 14.3 %collective-permute-start.4 = (bf16[512,128]{1,0:T(8,128)(2,1)}, bf16[512,128]{1,0:T(8,128)(2,1)S(1)}, u32[]{:S(2)}, u32[]{:S(2)}) collective-permute-start(bf16[512,128]{1,0:T(8,128)(2,1)} %feats.1), channel_id=1, source_target_pairs={{0,4},{1,5},{2,6},{3,7},{4,0},{5,1},{6,2},{7,3},{8,12},{9,13},{10,... | collective-permute-start | bytes 393224 | tf_op jit(solution)/shard_map/ppermute | solution.py:196
  4.7 10.2 %collective-permute-start.5 = (bf16[512,128]{1,0:T(8,128)(2,1)}, bf16[512,128]{1,0:T(8,128)(2,1)S(1)}, u32[]{:S(2)}, u32[]{:S(2)}) collective-permute-start(bf16[512,128]{1,0:T(8,128)(2,1)} %feats.1), channel_id=1, source_target_pairs={{0,6},{1,7},{2,4},{3,5},{4,2},{5,3},{6,0},{7,1},{8,14},{9,15},{10,... | collective-permute-start | bytes 393224 | tf_op jit(solution)/shard_map/ppermute | solution.py:196
  6.1 9.4 %collective-permute-start.6 = (bf16[512,128]{1,0:T(8,128)(2,1)}, bf16[512,128]{1,0:T(8,128)(2,1)S(1)}, u32[]{:S(2)}, u32[]{:S(2)}) collective-permute-start(bf16[512,128]{1,0:T(8,128)(2,1)} %feats.1), channel_id=1, source_target_pairs={{0,2},{1,3},{2,0},{3,1},{4,6},{5,7},{6,4},{7,5},{8,10},{9,11},{10,... | collective-permute-start | bytes 393224 | tf_op jit(solution)/shard_map/ppermute | solution.py:196
  6.3 0.9 %copy-start.1 = (bf16[1024,128]{1,0:T(8,128)(2,1)S(1)}, bf16[1024,128]{1,0:T(8,128)(2,1)}, u32[]{:S(2)}) copy-start(bf16[1024,128]{1,0:T(8,128)(2,1)} %weight.1) | copy-start | bytes 786436
  7.3 0.9 %copy-start.2 = (bf16[1024,128]{1,0:T(8,128)(2,1)S(1)}, bf16[1024,128]{1,0:T(8,128)(2,1)}, u32[]{:S(2)}) copy-start(bf16[1024,128]{1,0:T(8,128)(2,1)} %root.1) | copy-start | bytes 786436
  8.2 0.9 %copy-start.3 = (bf16[512,128]{1,0:T(8,128)(2,1)S(1)}, bf16[512,128]{1,0:T(8,128)(2,1)}, u32[]{:S(2)}) copy-start(bf16[512,128]{1,0:T(8,128)(2,1)} %feats.1) | copy-start | bytes 393220
  9.2 7.3 %collective-permute-start.3 = (bf16[512,128]{1,0:T(8,128)(2,1)S(1)}, bf16[512,128]{1,0:T(8,128)(2,1)S(1)}, u32[]{:S(2)}, u32[]{:S(2)}) collective-permute-start(bf16[512,128]{1,0:T(8,128)(2,1)S(1)} %get-tuple-element.47.refs_0_), channel_id=1, source_target_pairs={{0,1},{1,0},{2,3},{3,2},{4,5},{5,4},{6,7},{7,6},{8,9},{9,8},{10,11... | collective-permute-start | bytes 393224 | tf_op jit(solution)/shard_map/ppermute | solution.py:196
  15.4 1.3 %collective-permute-start.9 = (bf16[512,128]{1,0:T(8,128)(2,1)S(1)}, bf16[512,128]{1,0:T(8,128)(2,1)S(1)}, u32[]{:S(2)}, u32[]{:S(2)}) collective-permute-start(bf16[512,128]{1,0:T(8,128)(2,1)S(1)} %collective-permute-done.5.refs_6_), channel_id=1, source_target_pairs={{0,1},{1,0},{2,3},{3,2},{4,5},{5,4},{6,7},{7,6},{8,9},{9,8},{10,11... | collective-permute-start | bytes 393224 | tf_op jit(solution)/shard_map/ppermute | solution.py:196
  15.4 1.5 %collective-permute-start.7 = (bf16[512,128]{1,0:T(8,128)(2,1)S(1)}, bf16[512,128]{1,0:T(8,128)(2,1)S(1)}, u32[]{:S(2)}, u32[]{:S(2)}) collective-permute-start(bf16[512,128]{1,0:T(8,128)(2,1)S(1)} %collective-permute-done.6.refs_2_), channel_id=1, source_target_pairs={{0,1},{1,0},{2,3},{3,2},{4,5},{5,4},{6,7},{7,6},{8,9},{9,8},{10,11... | collective-permute-start | bytes 393224 | tf_op jit(solution)/shard_map/ppermute | solution.py:196
  16.0 1.3 %collective-permute-start.8 = (bf16[512,128]{1,0:T(8,128)(2,1)S(1)}, bf16[512,128]{1,0:T(8,128)(2,1)S(1)}, u32[]{:S(2)}, u32[]{:S(2)}) collective-permute-start(bf16[512,128]{1,0:T(8,128)(2,1)S(1)} %collective-permute-done.4.refs_4_), channel_id=1, source_target_pairs={{0,1},{1,0},{2,3},{3,2},{4,5},{5,4},{6,7},{7,6},{8,9},{9,8},{10,11... | collective-permute-start | bytes 393224 | tf_op jit(solution)/shard_map/ppermute | solution.py:196
  16.0 8.4 %collective-permute-start.2 = (bf16[2,512,128]{2,1,0:T(8,128)(2,1)S(1)}, bf16[2,512,128]{2,1,0:T(8,128)(2,1)S(1)}, u32[]{:S(2)}, u32[]{:S(2)}) collective-permute-start(bf16[2,512,128]{2,1,0:T(8,128)(2,1)S(1)} %get-tuple-element.45.refs_9_), channel_id=1, source_target_pairs={{0,1},{1,0},{2,3},{3,2},{4,5},{5,4},{6,7},{7,6},{8,9},{9,8},{10,11... | collective-permute-start | bytes 786440 | tf_op jit(solution)/shard_map/ppermute | solution.py:196
  17.7 6.9 %collective-permute-start.10 = (bf16[512,128]{1,0:T(8,128)(2,1)S(1)}, bf16[512,128]{1,0:T(8,128)(2,1)S(1)}, u32[]{:S(2)}, u32[]{:S(2)}) collective-permute-start(bf16[512,128]{1,0:T(8,128)(2,1)S(1)} %get-tuple-element.53.hidden), channel_id=1, source_target_pairs={{0,8},{8,0},{16,24},{24,16},{1,9},{9,1},{17,25},{25,17},{2,10},{10... | collective-permute-start | bytes 393224 | tf_op jit(solution)/shard_map/ppermute | solution.py:196
  19.4 8.1 %collective-permute-start.11 = (bf16[512,128]{1,0:T(8,128)(2,1)S(1)}, bf16[512,128]{1,0:T(8,128)(2,1)S(1)}, u32[]{:S(2)}, u32[]{:S(2)}) collective-permute-start(bf16[512,128]{1,0:T(8,128)(2,1)S(1)} %get-tuple-element.53.hidden), channel_id=1, source_target_pairs={{0,16},{8,24},{16,0},{24,8},{1,17},{9,25},{17,1},{25,9},{2,18},{10... | collective-permute-start | bytes 393224 | tf_op jit(solution)/shard_map/ppermute | solution.py:196
  20.9 6.6 %collective-permute-start.12 = (bf16[512,128]{1,0:T(8,128)(2,1)S(1)}, bf16[512,128]{1,0:T(8,128)(2,1)S(1)}, u32[]{:S(2)}, u32[]{:S(2)}) collective-permute-start(bf16[512,128]{1,0:T(8,128)(2,1)S(1)} %get-tuple-element.53.hidden), channel_id=1, source_target_pairs={{0,24},{8,16},{16,8},{24,0},{1,25},{9,17},{17,9},{25,1},{2,26},{10... | collective-permute-start | bytes 393224 | tf_op jit(solution)/shard_map/ppermute | solution.py:196
  21.3 1.6 %copy-start = (bf16[512,2048]{1,0:T(8,128)(2,1)S(1)}, bf16[512,2048]{1,0:T(8,128)(2,1)}, u32[]{:S(2)}) copy-start(bf16[512,2048]{1,0:T(8,128)(2,1)} %shard_map.94.adj.refs_3_) | copy-start | bytes 6291460
  24.3 3.1 %copy-start.4 = (bf16[512,128]{1,0:T(8,128)(2,1)S(1)}, bf16[512,128]{1,0:T(8,128)(2,1)}, u32[]{:S(2)}) copy-start(bf16[512,128]{1,0:T(8,128)(2,1)} %refs_6_.1) | copy-start | bytes 393220
  29.3 6.6 %collective-permute-start.13 = (bf16[512,128]{1,0:T(8,128)(2,1)S(1)}, bf16[512,128]{1,0:T(8,128)(2,1)S(1)}, u32[]{:S(2)}, u32[]{:S(2)}) collective-permute-start(bf16[512,128]{1,0:T(8,128)(2,1)S(1)} %get-tuple-element.57), channel_id=1, source_target_pairs={{0,8},{8,0},{16,24},{24,16},{1,9},{9,1},{17,25},{25,17},{2,10},{10... | collective-permute-start | bytes 393224 | tf_op jit(solution)/shard_map/ppermute | solution.py:196
  30.6 6.8 %collective-permute-start.14 = (bf16[512,128]{1,0:T(8,128)(2,1)S(1)}, bf16[512,128]{1,0:T(8,128)(2,1)S(1)}, u32[]{:S(2)}, u32[]{:S(2)}) collective-permute-start(bf16[512,128]{1,0:T(8,128)(2,1)S(1)} %get-tuple-element.58), channel_id=1, source_target_pairs={{0,16},{8,24},{16,0},{24,8},{1,17},{9,25},{17,1},{25,9},{2,18},{10... | collective-permute-start | bytes 393224 | tf_op jit(solution)/shard_map/ppermute | solution.py:196
  31.4 7.8 %collective-permute-start.15 = (bf16[512,128]{1,0:T(8,128)(2,1)S(1)}, bf16[512,128]{1,0:T(8,128)(2,1)S(1)}, u32[]{:S(2)}, u32[]{:S(2)}) collective-permute-start(bf16[512,128]{1,0:T(8,128)(2,1)S(1)} %get-tuple-element.59), channel_id=1, source_target_pairs={{0,24},{8,16},{16,8},{24,0},{1,25},{9,17},{17,9},{25,1},{2,26},{10... | collective-permute-start | bytes 393224 | tf_op jit(solution)/shard_map/ppermute | solution.py:196
  33.8 14.6 %copy-start.5 = (s32[4]{0:T(128)S(1)}, s32[4]{0:T(128)}, u32[]{:S(2)}) copy-start(s32[4]{0:T(128)} %all_counts.1) | copy-start | bytes 52
  33.8 6.2 %collective-permute-start.21 = (bf16[512,128]{1,0:T(8,128)(2,1)S(1)}, bf16[512,128]{1,0:T(8,128)(2,1)S(1)}, u32[]{:S(2)}, u32[]{:S(2)}) collective-permute-start(bf16[512,128]{1,0:T(8,128)(2,1)S(1)} %get-tuple-element.67.refs_4_), channel_id=1, source_target_pairs={{0,8},{8,0},{16,24},{24,16},{1,9},{9,1},{17,25},{25,17},{2,10},{10... | collective-permute-start | bytes 393224 | tf_op jit(solution)/shard_map/ppermute | solution.py:196
  35.1 5.6 %collective-permute-start.22 = (bf16[512,128]{1,0:T(8,128)(2,1)S(1)}, bf16[512,128]{1,0:T(8,128)(2,1)S(1)}, u32[]{:S(2)}, u32[]{:S(2)}) collective-permute-start(bf16[512,128]{1,0:T(8,128)(2,1)S(1)} %get-tuple-element.68.refs_5_), channel_id=1, source_target_pairs={{0,16},{8,24},{16,0},{24,8},{1,17},{9,25},{17,1},{25,9},{2,18},{10... | collective-permute-start | bytes 393224 | tf_op jit(solution)/shard_map/ppermute | solution.py:196
  35.9 6.9 %collective-permute-start.17 = (bf16[512,128]{1,0:T(8,128)(2,1)S(1)}, bf16[512,128]{1,0:T(8,128)(2,1)S(1)}, u32[]{:S(2)}, u32[]{:S(2)}) collective-permute-start(bf16[512,128]{1,0:T(8,128)(2,1)S(1)} %get-tuple-element.55.grad_pre.pre), channel_id=1, source_target_pairs={{0,1},{1,0},{2,3},{3,2},{4,5},{5,4},{6,7},{7,6},{8,9},{9,8},{10,11... | collective-permute-start | bytes 393224 | tf_op jit(solution)/shard_map/ppermute | solution.py:196
  39.2 3.6 %collective-permute-start.16 = (bf16[512,128]{1,0:T(8,128)(2,1)S(1)}, bf16[512,128]{1,0:T(8,128)(2,1)S(1)}, u32[]{:S(2)}, u32[]{:S(2)}) collective-permute-start(bf16[512,128]{1,0:T(8,128)(2,1)S(1)} %shard_map.102.hidden.grads), channel_id=1, source_target_pairs={{0,1},{1,0},{2,3},{3,2},{4,5},{5,4},{6,7},{7,6},{8,9},{9,8},{10,11... | collective-permute-start | bytes 393224 | tf_op jit(solution)/shard_map/ppermute | solution.py:196
  40.7 7.7 %collective-permute-start.23 = (bf16[512,128]{1,0:T(8,128)(2,1)S(1)}, bf16[512,128]{1,0:T(8,128)(2,1)S(1)}, u32[]{:S(2)}, u32[]{:S(2)}) collective-permute-start(bf16[512,128]{1,0:T(8,128)(2,1)S(1)} %get-tuple-element.69.refs_0_), channel_id=1, source_target_pairs={{0,8},{8,0},{16,24},{24,16},{1,9},{9,1},{17,25},{25,17},{2,10},{10... | collective-permute-start | bytes 393224 | tf_op jit(solution)/shard_map/ppermute | solution.py:196
  41.9 6.5 %collective-permute-start.24 = (bf16[512,128]{1,0:T(8,128)(2,1)S(1)}, bf16[512,128]{1,0:T(8,128)(2,1)S(1)}, u32[]{:S(2)}, u32[]{:S(2)}) collective-permute-start(bf16[512,128]{1,0:T(8,128)(2,1)S(1)} %get-tuple-element.70.refs_1_), channel_id=1, source_target_pairs={{0,16},{8,24},{16,0},{24,8},{1,17},{9,25},{17,1},{25,9},{2,18},{10... | collective-permute-start | bytes 393224 | tf_op jit(solution)/shard_map/ppermute | solution.py:196
  43.6 13.6 %collective-permute-start.18 = (bf16[512,128]{1,0:T(8,128)(2,1)S(1)}, bf16[512,128]{1,0:T(8,128)(2,1)S(1)}, u32[]{:S(2)}, u32[]{:S(2)}) collective-permute-start(bf16[512,128]{1,0:T(8,128)(2,1)S(1)} %get-tuple-element.62), channel_id=1, source_target_pairs={{0,4},{1,5},{2,6},{3,7},{4,0},{5,1},{6,2},{7,3},{8,12},{9,13},{10,... | collective-permute-start | bytes 393224 | tf_op jit(solution)/shard_map/ppermute | solution.py:196
  47.7 9.5 %collective-permute-start.19 = (bf16[512,128]{1,0:T(8,128)(2,1)S(1)}, bf16[512,128]{1,0:T(8,128)(2,1)S(1)}, u32[]{:S(2)}, u32[]{:S(2)}) collective-permute-start(bf16[512,128]{1,0:T(8,128)(2,1)S(1)} %get-tuple-element.63), channel_id=1, source_target_pairs={{0,6},{1,7},{2,4},{3,5},{4,2},{5,3},{6,0},{7,1},{8,14},{9,15},{10,... | collective-permute-start | bytes 393224 | tf_op jit(solution)/shard_map/ppermute | solution.py:196
  48.2 9.0 %collective-permute-start.20 = (bf16[512,128]{1,0:T(8,128)(2,1)S(1)}, bf16[512,128]{1,0:T(8,128)(2,1)S(1)}, u32[]{:S(2)}, u32[]{:S(2)}) collective-permute-start(bf16[512,128]{1,0:T(8,128)(2,1)S(1)} %get-tuple-element.64), channel_id=1, source_target_pairs={{0,2},{1,3},{2,0},{3,1},{4,6},{5,7},{6,4},{7,5},{8,10},{9,11},{10,... | collective-permute-start | bytes 393224 | tf_op jit(solution)/shard_map/ppermute | solution.py:196
  48.6 6.6 %collective-permute-start = (bf16[512,256]{1,0:T(8,128)(2,1)S(1)}, bf16[512,256]{1,0:T(8,128)(2,1)S(1)}, u32[]{:S(2)}, u32[]{:S(2)}) collective-permute-start(bf16[512,256]{1,0:T(8,128)(2,1)S(1)} %get-tuple-element.4.top), channel_id=1, source_target_pairs={{0,16},{8,24},{16,0},{24,8},{1,17},{9,25},{17,1},{25,9},{2,18},{10... | collective-permute-start | bytes 786440 | tf_op jit(solution)/shard_map/cond/branch_1_fun/ppermute | solution.py:196
  49.7 6.4 %collective-permute-start.1 = (bf16[512,256]{1,0:T(8,128)(2,1)S(1)}, bf16[512,256]{1,0:T(8,128)(2,1)S(1)}, u32[]{:S(2)}, u32[]{:S(2)}) collective-permute-start(bf16[512,256]{1,0:T(8,128)(2,1)S(1)} %get-tuple-element.5.bottom), channel_id=1, source_target_pairs={{0,8},{8,0},{16,24},{24,16},{1,9},{9,1},{17,25},{25,17},{2,10},{10... | collective-permute-start | bytes 786440 | tf_op jit(solution)/shard_map/cond/branch_1_fun/ppermute | solution.py:196

commit v5 on v4

--- a/solution.py
+++ b/solution.py
@@ -164,25 +164,26 @@
 
 
 def join_kernel(*refs):
-    terms, outs = refs[:8], refs[8:]
+    terms, outs = refs[:6], refs[6:]
     for half, out in enumerate(outs):
-        weight = terms[half][...].astype(F32) + terms[half + 2][...].astype(F32)
-        root = terms[half + 4][...].astype(F32) + terms[half + 6][...].astype(F32)
-        out[...] = jnp.concatenate([weight, root], 1).astype(BF)
+        width = out.shape[1] // 2
+        out[:, :width] = terms[half][...]
+        root = terms[half + 2][...].astype(F32) + terms[half + 4][...].astype(F32)
+        out[:, width:] = root.astype(BF)
 
 
 def pair_sum_kernel(top, top_2, bottom, bottom_2, top_sum, bottom_sum):
     for out, terms in ((top_sum, (top, top_2)), (bottom_sum, (bottom, bottom_2))):
-        total = terms[0][...].astype(F32) + terms[1][...].astype(F32)
+        width = out.shape[1]
+        total = terms[0][:, :width].astype(F32) + terms[1][:, :width].astype(F32)
         out[...] = total.astype(BF)
 
 
-def place_kernel(top, top_2, bottom, bottom_2, weight, root):
-    half, width = top.shape[0], weight.shape[1]
+def place_kernel(top, top_2, bottom, bottom_2, out):
+    half, width = top.shape[0], out.shape[1]
     for at, terms in ((0, (top, top_2)), (half, (bottom, bottom_2))):
         total = terms[0][...].astype(F32) + terms[1][...].astype(F32)
-        weight[at : at + half, :] = total[:, :width]
-        root[at : at + half, :] = total[:, width:]
+        out[at : at + half, :] = total[:, -width:]
 
 
 def on_device(node_feats, weight, root_weight, grad_out, block_counts, tile_cols, tile_vals):
@@ -208,7 +209,7 @@
             pltpu.VMEM((rows, nodes), F32),
             pltpu.SemaphoreType.DMA((3,)),
         ],
-        limit=58 * 1024 * 1024,
+        limit=48 * 1024 * 1024,
     )
     mine, near, far = call(
         functools.partial(prepare_kernel, nf),
@@ -220,15 +221,24 @@
         functools.partial(flip_kernel, tile_vals.shape[1]), [sds((nodes, rows), BF)], [VMEM], (adj,)
     )
     ranks = sorted(range(1, nz), key=lambda k: (k < nz // 2, k))
-    moved = {0: node_feats} | {2 * k: swap(node_feats, "feat", 2 * k) for k in ranks}
-    order = [2 * k for k in ranks]
-    moved |= dict(zip(order, lax.optimization_barrier((*[moved[m] for m in order], adj))))
+    masks = [1 << bit for bit in range(1, nf.bit_length() - 1)]
+    moved = {0: node_feats}
+    for mask in reversed(masks[1:]):
+        moved |= {m | mask: swap(piece, "feat", mask) for m, piece in moved.items()}
+    moved[masks[0]] = swap(node_feats, "feat", masks[0])
+    beside = {0: swap(node_feats, "feat", 1)}
+    order = sorted((m for m in moved if m), reverse=True)
+    *early, near, beside[0] = lax.optimization_barrier((*[moved[m] for m in order], near, beside[0]))
+    moved |= dict(zip(order, early))
+    ahead = {m: swap(moved[m], "feat", 1) for m in order}
+    last = [m | masks[0] for m in order if m != masks[0]]
+    moved |= {m: swap(moved[m ^ masks[0]], "feat", masks[0]) for m in last}
+    held = lax.optimization_barrier((*[moved[m] for m in last], *[ahead[m] for m in order]))
+    moved |= dict(zip(last, held))
+    beside |= dict(zip(order, held[len(last) :]))
+    beside |= {m: swap(moved[m], "feat", 1) for m in last}
     moved[0] = mine
-    late = [m for m in moved if m == 2 * nz - 2]
-    moved |= dict(zip(late, lax.optimization_barrier((*[moved[m] for m in late], near))))
-    pieces = []
-    for m in sorted(moved):
-        pieces += [moved[m], swap(moved[m], "feat", 1)]
+    pieces = [piece for m in sorted(moved) for piece in (moved[m], beside[m])]
     near_2 = swap(far, "feat", 1)
     hidden, own = call(
         functools.partial(forward_kernel, nf),
@@ -288,34 +298,34 @@
         flops=2 * rows * depth * width,
     )
     steps = [1 << bit for bit in range(nr.bit_length() - 1)]
-    first, *between, final = zip(steps, reversed(steps))
+    first, *between = zip(steps, reversed(steps))
+    final = between[-1]
     root_got = [swap(part, "rows", mask) for part, mask in zip(root_part, first)]
     *weight_part, root_got[0], root_got[1] = lax.optimization_barrier((*weight_part, *root_got))
-    weight_got = [swap(part, "rows", mask) for part, mask in zip(weight_part, first)]
     sums_f = [parts[0]] + [swap(parts[k], "feat", 2 * k) for k in ranks]
     joined = [sds((depth // 2, 2 * width), BF)] * 2
-    grads = call(
-        join_kernel, joined, [VMEM] * 8, (*weight_part, *weight_got, *root_part, *root_got)
-    )
+    grads = call(join_kernel, joined, [VMEM] * 6, (*weight_part, *root_part, *root_got))
     for masks in between:
         got = [swap(part, "rows", mask) for part, mask in zip(grads, masks)]
-        grads = call(pair_sum_kernel, joined, [VMEM] * 4, (grads[0], got[0], grads[1], got[1]))
-
-    def finish(grads):
-        got = [swap(part, "rows", mask) for part, mask in zip(grads, final)]
-        return tuple(
-            call(
-                place_kernel,
-                [sds((depth, width), F32)] * 2,
-                [VMEM] * 4,
-                (grads[0], got[0], grads[1], got[1]),
-            )
-        )
-
-    def skip(grads):
+        pairs = grads[0], got[0], grads[1], got[1]
+        last = masks == final
+        shapes = [sds((depth // 2, width), BF)] * 2 if last else joined
+        grads = call(pair_sum_kernel, shapes, [VMEM] * 4, pairs)
+
+    def place(top, top_2, bottom, bottom_2):
+        arrays = top, top_2, bottom, bottom_2
+        return call(place_kernel, [sds((depth, width), F32)], [VMEM] * 4, arrays)[0]
+
+    def finish(operands):
+        grads, pairs = operands
+        got = [swap(part, "rows", mask) for part, mask in zip(grads, first)]
+        return place(grads[0], got[0], grads[1], got[1]), place(*pairs)
+
+    def skip(operands):
         return (jnp.zeros((depth, width), F32),) * 2
 
-    grad_weight, grad_root = lax.cond(block_counts[0] > 0, finish, skip, tuple(grads))
+    operands = tuple(grads), tuple(pairs)
+    grad_weight, grad_root = lax.cond(block_counts[0] > 0, finish, skip, operands)
     *sums_f, grad_weight, grad_root = lax.optimization_barrier((*sums_f, grad_weight, grad_root))
     (grad_feats,) = call(
         functools.partial(sum_kernel, len(sums_f)),

time: 58.3 us -> 57.5 us (0.986)
  Pallas kernels: 12.2 us -> 8.38 us
  waiting for transfers between devices: 15.5 us -> 17.3 us
  starting transfers between devices: 24.9 us -> 26.2 us
    pallas_call x14 -> x16, Pallas kernels: 12.2 us -> 8.38 us  [call(): pl.pallas_call(body, out_shape=outs, in_specs=specs, out_specs=[VMEM] * l...]
    ppermute x25, waiting for transfers between devices: 15.5 us -> 17.3 us  [swap(): lax.ppermute(array, axis, [(i, i ^ mask) for i in range(lax.axis_size(axi...]
    ppermute x25, starting transfers between devices: 24.9 us -> 26.2 us  [swap(): lax.ppermute(array, axis, [(i, i ^ mask) for i in range(lax.axis_size(axi...]
    unnamed x12 -> x18, local copies, waits for them, and re-layouts: 4.41 us -> 4.57 us
  transfers between devices with their start and end apart: 25 -> 25, of which waited for: 13 -> 14; matrix products, arithmetic and copies ran while one was open for 0% -> 0% of each run, Pallas kernels for 17% -> 10%
where the time goes in v5:
time: 57.5 us; the launch traced here: 57.3 us
  starting transfers between devices  26.2 us (46%)
  waiting for transfers between devices  17.3 us (30%)
  Pallas kernels  8.38 us (15%)
  local copies, waits for them, and re-layouts  4.57 us (8%)
  between operations  0.84 us (1%)
    ppermute x25, starting transfers between devices, swap(): lax.ppermute(array, axis, [(i, i ^ mask) for i in range(lax.axis_size(axi...  26.2 us
    ppermute x25, waiting for transfers between devices, swap(): lax.ppermute(array, axis, [(i, i ^ mask) for i in range(lax.axis_size(axi...  17.3 us
    pallas_call x16, Pallas kernels, call(): pl.pallas_call(body, out_shape=outs, in_specs=specs, out_specs=[VMEM] * l...  8.38 us
    unnamed x18, local copies, waits for them, and re-layouts  4.57 us
  transfers between devices with their start and end apart: 25, of which 14 were waited for; matrix products, arithmetic and copies ran while one was open for 0% of the time, Pallas kernels for 10%

profile of v5, /device:TPU:0, one launch (start us, length us, event | category | flops | bytes accessed | tf_op | source)
XLA Modules:
  0.0 57.3 jit_solution(7973305360499738356)
XLA Ops:
  0.6 4.1 %collective-permute-start.3 = (bf16[512,128]{1,0:T(8,128)(2,1)}, bf16[512,128]{1,0:T(8,128)(2,1)S(1)}, u32[]{:S(2)}, u32[]{:S(2)}) collective-permute-start(bf16[512,128]{1,0:T(8,128)(2,1)} %feats.1), channel_id=1, source_target_pairs={{0,4},{1,5},{2,6},{3,7},{4,0},{5,1},{6,2},{7,3},{8,12},{9,13},{10,... | collective-permute-start | bytes 393224 | tf_op jit(solution)/shard_map/ppermute | solution.py:197
  4.7 1.6 %collective-permute-start.4 = (bf16[512,128]{1,0:T(8,128)(2,1)}, bf16[512,128]{1,0:T(8,128)(2,1)S(1)}, u32[]{:S(2)}, u32[]{:S(2)}) collective-permute-start(bf16[512,128]{1,0:T(8,128)(2,1)} %feats.1), channel_id=1, source_target_pairs={{0,2},{1,3},{2,0},{3,1},{4,6},{5,7},{6,4},{7,5},{8,10},{9,11},{10,... | collective-permute-start | bytes 393224 | tf_op jit(solution)/shard_map/ppermute | solution.py:197
  6.3 0.9 %copy-done.1 = bf16[1024,128]{1,0:T(8,128)(2,1)S(1)} copy-done((bf16[1024,128]{1,0:T(8,128)(2,1)S(1)}, bf16[1024,128]{1,0:T(8,128)(2,1)}, u32[]{:S(2)}) %copy-start.1) | copy-done | bytes 262168
  7.3 0.9 %copy-done.2 = bf16[1024,128]{1,0:T(8,128)(2,1)S(1)} copy-done((bf16[1024,128]{1,0:T(8,128)(2,1)S(1)}, bf16[1024,128]{1,0:T(8,128)(2,1)}, u32[]{:S(2)}) %copy-start.2) | copy-done | bytes 262168
  8.2 0.9 %copy-done.3 = bf16[512,128]{1,0:T(8,128)(2,1)S(1)} copy-done((bf16[512,128]{1,0:T(8,128)(2,1)S(1)}, bf16[512,128]{1,0:T(8,128)(2,1)}, u32[]{:S(2)}) %copy-start.3) | copy-done | bytes 131096
  9.2 2.2 %collective-permute-done.3.refs_4_ = bf16[512,128]{1,0:T(8,128)(2,1)S(1)} collective-permute-done((bf16[512,128]{1,0:T(8,128)(2,1)}, bf16[512,128]{1,0:T(8,128)(2,1)S(1)}, u32[]{:S(2)}, u32[]{:S(2)}) %collective-permute-start.3) | collective-permute-done | bytes 131104 | tf_op jit(solution)/shard_map/ppermute | solution.py:197
  11.6 1.4 %collective-permute-start.6 = (bf16[512,128]{1,0:T(8,128)(2,1)S(1)}, bf16[512,128]{1,0:T(8,128)(2,1)S(1)}, u32[]{:S(2)}, u32[]{:S(2)}) collective-permute-start(bf16[512,128]{1,0:T(8,128)(2,1)S(1)} %collective-permute-done.3.refs_4_), channel_id=1, source_target_pairs={{0,2},{1,3},{2,0},{3,1},{4,6},{5,7},{6,4},{7,5},{8,10},{9,11},{10,... | collective-permute-start | bytes 393224 | tf_op jit(solution)/shard_map/ppermute | solution.py:197
  13.5 3.0 %collective-permute-done.6.refs_6_ = bf16[512,128]{1,0:T(8,128)(2,1)S(1)} collective-permute-done((bf16[512,128]{1,0:T(8,128)(2,1)S(1)}, bf16[512,128]{1,0:T(8,128)(2,1)S(1)}, u32[]{:S(2)}, u32[]{:S(2)}) %collective-permute-start.6) | collective-permute-done | bytes 131104 | tf_op jit(solution)/shard_map/ppermute | solution.py:197
  17.1 0.8 %collective-permute-done.9.refs_7_ = bf16[512,128]{1,0:T(8,128)(2,1)S(1)} collective-permute-done((bf16[512,128]{1,0:T(8,128)(2,1)S(1)}, bf16[512,128]{1,0:T(8,128)(2,1)S(1)}, u32[]{:S(2)}, u32[]{:S(2)}) %collective-permute-start.9) | collective-permute-done | bytes 131104 | tf_op jit(solution)/shard_map/ppermute | solution.py:197
  18.3 1.6 %collective-permute-start.10 = (bf16[512,128]{1,0:T(8,128)(2,1)S(1)}, bf16[512,128]{1,0:T(8,128)(2,1)S(1)}, u32[]{:S(2)}, u32[]{:S(2)}) collective-permute-start(bf16[512,128]{1,0:T(8,128)(2,1)S(1)} %get-tuple-element.75.hidden), channel_id=1, source_target_pairs={{0,8},{8,0},{16,24},{24,16},{1,9},{9,1},{17,25},{25,17},{2,10},{10... | collective-permute-start | bytes 393224 | tf_op jit(solution)/shard_map/ppermute | solution.py:197
  19.9 1.5 %collective-permute-start.11 = (bf16[512,128]{1,0:T(8,128)(2,1)S(1)}, bf16[512,128]{1,0:T(8,128)(2,1)S(1)}, u32[]{:S(2)}, u32[]{:S(2)}) collective-permute-start(bf16[512,128]{1,0:T(8,128)(2,1)S(1)} %get-tuple-element.75.hidden), channel_id=1, source_target_pairs={{0,16},{8,24},{16,0},{24,8},{1,17},{9,25},{17,1},{25,9},{2,18},{10... | collective-permute-start | bytes 393224 | tf_op jit(solution)/shard_map/ppermute | solution.py:197
  21.9 1.7 %copy-done = bf16[80,128,128]{2,1,0:T(8,128)(2,1)S(1)} copy-done((bf16[80,128,128]{2,1,0:T(8,128)(2,1)S(1)}, bf16[80,128,128]{2,1,0:T(8,128)(2,1)}, u32[]{:S(2)}) %copy-start) | copy-done | bytes 2621464
  23.6 1.3 %shard_map.94.adj.refs_3_ = bf16[512,2048]{1,0:T(8,128)(2,1)S(1)} custom-call(s32[4]{0:T(128)S(1)} %copy-done.6, s32[80]{0:T(128)S(1)} %copy-done.5, bf16[80,128,128]{2,1,0:T(8,128)(2,1)S(1)} %copy-done), custom_call_target="tpu_custom_call" | custom-call | flops 4194304 | bytes 4718928 | tf_op jit(solution)/shard_map/pallas_call | solution.py:28
  24.9 1.4 %shard_map.95.refs_4_.adj_t = bf16[2048,512]{1,0:T(8,128)(2,1)S(1)} custom-call(bf16[512,2048]{1,0:T(8,128)(2,1)S(1)} %shard_map.94.adj.refs_3_), custom_call_target="tpu_custom_call" | custom-call | bytes 4194304 | tf_op jit(solution)/shard_map/pallas_call | solution.py:28
  27.0 1.0 %collective-permute-done.11.refs_1_ = bf16[512,128]{1,0:T(8,128)(2,1)S(1)} collective-permute-done((bf16[512,128]{1,0:T(8,128)(2,1)S(1)}, bf16[512,128]{1,0:T(8,128)(2,1)S(1)}, u32[]{:S(2)}, u32[]{:S(2)}) %collective-permute-start.11) | collective-permute-done | bytes 131104 | tf_op jit(solution)/shard_map/ppermute | solution.py:197
  28.0 1.8 %shard_map.99 = (bf16[512,128]{1,0:T(8,128)(2,1)S(1)}, bf16[512,128]{1,0:T(8,128)(2,1)S(1)}, bf16[512,128]{1,0:T(8,128)(2,1)S(1)}, bf16[512,128]{1,0:T(8,128)(2,1)S(1)}) custom-call(bf16[512,128]{1,0:T(8,128)(2,1)S(1)} %collective-permute-done.10.refs_0_, bf16[512,128]{1,0:T(8,128)(2,1)S(1)} %collective-permute-done.11.refs_1_, ...), custom_call_target="tpu_custom_call" | custom-call | flops 536870912 | bytes 5505024 | tf_op jit(solution)/shard_map/pallas_call | solution.py:28
  29.9 1.3 %collective-permute-start.13 = (bf16[512,128]{1,0:T(8,128)(2,1)S(1)}, bf16[512,128]{1,0:T(8,128)(2,1)S(1)}, u32[]{:S(2)}, u32[]{:S(2)}) collective-permute-start(bf16[512,128]{1,0:T(8,128)(2,1)S(1)} %get-tuple-element.79), channel_id=1, source_target_pairs={{0,8},{8,0},{16,24},{24,16},{1,9},{9,1},{17,25},{25,17},{2,10},{10... | collective-permute-start | bytes 393224 | tf_op jit(solution)/shard_map/ppermute | solution.py:197
  31.2 1.4 %collective-permute-start.14 = (bf16[512,128]{1,0:T(8,128)(2,1)S(1)}, bf16[512,128]{1,0:T(8,128)(2,1)S(1)}, u32[]{:S(2)}, u32[]{:S(2)}) collective-permute-start(bf16[512,128]{1,0:T(8,128)(2,1)S(1)} %get-tuple-element.80), channel_id=1, source_target_pairs={{0,16},{8,24},{16,0},{24,8},{1,17},{9,25},{17,1},{25,9},{2,18},{10... | collective-permute-start | bytes 393224 | tf_op jit(solution)/shard_map/ppermute | solution.py:197
  32.6 0.9 %collective-permute-start.15 = (bf16[512,128]{1,0:T(8,128)(2,1)S(1)}, bf16[512,128]{1,0:T(8,128)(2,1)S(1)}, u32[]{:S(2)}, u32[]{:S(2)}) collective-permute-start(bf16[512,128]{1,0:T(8,128)(2,1)S(1)} %get-tuple-element.81), channel_id=1, source_target_pairs={{0,24},{8,16},{16,8},{24,0},{1,25},{9,17},{17,9},{25,1},{2,26},{10... | collective-permute-start | bytes 393224 | tf_op jit(solution)/shard_map/ppermute | solution.py:197
  34.0 1.3 %collective-permute-start.21 = (bf16[512,128]{1,0:T(8,128)(2,1)S(1)}, bf16[512,128]{1,0:T(8,128)(2,1)S(1)}, u32[]{:S(2)}, u32[]{:S(2)}) collective-permute-start(bf16[512,128]{1,0:T(8,128)(2,1)S(1)} %get-tuple-element.89.refs_2_), channel_id=1, source_target_pairs={{0,8},{8,0},{16,24},{24,16},{1,9},{9,1},{17,25},{25,17},{2,10},{10... | collective-permute-start | bytes 393224 | tf_op jit(solution)/shard_map/ppermute | solution.py:197
  35.3 1.4 %collective-permute-start.22 = (bf16[512,128]{1,0:T(8,128)(2,1)S(1)}, bf16[512,128]{1,0:T(8,128)(2,1)S(1)}, u32[]{:S(2)}, u32[]{:S(2)}) collective-permute-start(bf16[512,128]{1,0:T(8,128)(2,1)S(1)} %get-tuple-element.90.refs_3_), channel_id=1, source_target_pairs={{0,16},{8,24},{16,0},{24,8},{1,17},{9,25},{17,1},{25,9},{2,18},{10... | collective-permute-start | bytes 393224 | tf_op jit(solution)/shard_map/ppermute | solution.py:197
  36.7 2.6 %collective-permute-done.14.refs_2_ = bf16[512,128]{1,0:T(8,128)(2,1)S(1)} collective-permute-done((bf16[512,128]{1,0:T(8,128)(2,1)S(1)}, bf16[512,128]{1,0:T(8,128)(2,1)S(1)}, u32[]{:S(2)}, u32[]{:S(2)}) %collective-permute-start.14) | collective-permute-done | bytes 131104 | tf_op jit(solution)/shard_map/ppermute | solution.py:197
  40.5 1.2 %collective-permute-done.22.refs_5_ = bf16[512,128]{1,0:T(8,128)(2,1)S(1)} collective-permute-done((bf16[512,128]{1,0:T(8,128)(2,1)S(1)}, bf16[512,128]{1,0:T(8,128)(2,1)S(1)}, u32[]{:S(2)}, u32[]{:S(2)}) %collective-permute-start.22) | collective-permute-done | bytes 131104 | tf_op jit(solution)/shard_map/ppermute | solution.py:197
  41.8 1.1 %collective-permute-start.23 = (bf16[512,256]{1,0:T(8,128)(2,1)S(1)}, bf16[512,256]{1,0:T(8,128)(2,1)S(1)}, u32[]{:S(2)}, u32[]{:S(2)}) collective-permute-start(bf16[512,256]{1,0:T(8,128)(2,1)S(1)} %get-tuple-element.95.top), channel_id=1, source_target_pairs={{0,16},{8,24},{16,0},{24,8},{1,17},{9,25},{17,1},{25,9},{2,18},{10... | collective-permute-start | bytes 786440 | tf_op jit(solution)/shard_map/ppermute | solution.py:197
  42.9 0.8 %collective-permute-start.24 = (bf16[512,256]{1,0:T(8,128)(2,1)S(1)}, bf16[512,256]{1,0:T(8,128)(2,1)S(1)}, u32[]{:S(2)}, u32[]{:S(2)}) collective-permute-start(bf16[512,256]{1,0:T(8,128)(2,1)S(1)} %get-tuple-element.96.bottom), channel_id=1, source_target_pairs={{0,8},{8,0},{16,24},{24,16},{1,9},{9,1},{17,25},{25,17},{2,10},{10... | collective-permute-start | bytes 786440 | tf_op jit(solution)/shard_map/ppermute | solution.py:197
  44.5 2.5 %collective-permute-start.18 = (bf16[512,128]{1,0:T(8,128)(2,1)S(1)}, bf16[512,128]{1,0:T(8,128)(2,1)S(1)}, u32[]{:S(2)}, u32[]{:S(2)}) collective-permute-start(bf16[512,128]{1,0:T(8,128)(2,1)S(1)} %get-tuple-element.84), channel_id=1, source_target_pairs={{0,4},{1,5},{2,6},{3,7},{4,0},{5,1},{6,2},{7,3},{8,12},{9,13},{10,... | collective-permute-start | bytes 393224 | tf_op jit(solution)/shard_map/ppermute | solution.py:197
  47.0 1.3 %collective-permute-start.19 = (bf16[512,128]{1,0:T(8,128)(2,1)S(1)}, bf16[512,128]{1,0:T(8,128)(2,1)S(1)}, u32[]{:S(2)}, u32[]{:S(2)}) collective-permute-start(bf16[512,128]{1,0:T(8,128)(2,1)S(1)} %get-tuple-element.85), channel_id=1, source_target_pairs={{0,6},{1,7},{2,4},{3,5},{4,2},{5,3},{6,0},{7,1},{8,14},{9,15},{10,... | collective-permute-start | bytes 393224 | tf_op jit(solution)/shard_map/ppermute | solution.py:197
  48.8 0.8 %collective-permute-done.23.top_2 = bf16[512,256]{1,0:T(8,128)(2,1)S(1)} collective-permute-done((bf16[512,256]{1,0:T(8,128)(2,1)S(1)}, bf16[512,256]{1,0:T(8,128)(2,1)S(1)}, u32[]{:S(2)}, u32[]{:S(2)}) %collective-permute-start.23) | collective-permute-done | bytes 262176 | tf_op jit(solution)/shard_map/ppermute | solution.py:197
  50.3 5.8 %conditional.1 = (f32[1024,128]{1,0:T(8,128)S(1)}, f32[1024,128]{1,0:T(8,128)S(1)}) conditional(s32[]{:T(128)} %bitcast, () %tuple.24, (bf16[512,128]{1,0:T(8,128)(2,1)S(1)}, bf16[512,128]{1,0:T(8,128)(2,1)S(1)}, bf16[512,256]{1,0:T(8,128)(2,1)S(1)}, bf16[512,256]{1,0:T(8,128)(2,1)S(1)}, bf16[512,256]{1,0:T(8,128)(2,1)S(1)}, ...), branch_computations={%region_0.0_spmd, %region_1.0_spmd} | conditional | bytes 3670112 | solution.py:328
  50.3 0.8 %collective-permute-start = (bf16[512,128]{1,0:T(8,128)(2,1)S(1)}, bf16[512,128]{1,0:T(8,128)(2,1)S(1)}, u32[]{:S(2)}, u32[]{:S(2)}) collective-permute-start(bf16[512,128]{1,0:T(8,128)(2,1)S(1)} %get-tuple-element.12.top), channel_id=1, source_target_pairs={{0,8},{8,0},{16,24},{24,16},{1,9},{9,1},{17,25},{25,17},{2,10},{10... | collective-permute-start | bytes 393224 | tf_op jit(solution)/shard_map/cond/branch_1_fun/ppermute | solution.py:197
  51.1 1.2 %collective-permute-start.1 = (bf16[512,128]{1,0:T(8,128)(2,1)S(1)}, bf16[512,128]{1,0:T(8,128)(2,1)S(1)}, u32[]{:S(2)}, u32[]{:S(2)}) collective-permute-start(bf16[512,128]{1,0:T(8,128)(2,1)S(1)} %get-tuple-element.13.bottom), channel_id=1, source_target_pairs={{0,16},{8,24},{16,0},{24,8},{1,17},{9,25},{17,1},{25,9},{2,18},{10... | collective-permute-start | bytes 393224 | tf_op jit(solution)/shard_map/cond/branch_1_fun/ppermute | solution.py:197
  52.4 3.0 %collective-permute-done.top_2 = bf16[512,128]{1,0:T(8,128)(2,1)S(1)} collective-permute-done((bf16[512,128]{1,0:T(8,128)(2,1)S(1)}, bf16[512,128]{1,0:T(8,128)(2,1)S(1)}, u32[]{:S(2)}, u32[]{:S(2)}) %collective-permute-start) | collective-permute-done | bytes 131104 | tf_op jit(solution)/shard_map/cond/branch_1_fun/ppermute | solution.py:197
  (53 shorter events, 8.5 us)
Async XLA Ops:
  0.6 10.7 %collective-permute-start.3 = (bf16[512,128]{1,0:T(8,128)(2,1)}, bf16[512,128]{1,0:T(8,128)(2,1)S(1)}, u32[]{:S(2)}, u32[]{:S(2)}) collective-permute-start(bf16[512,128]{1,0:T(8,128)(2,1)} %feats.1), channel_id=1, source_target_pairs={{0,4},{1,5},{2,6},{3,7},{4,0},{5,1},{6,2},{7,3},{8,12},{9,13},{10,... | collective-permute-start | bytes 393224 | tf_op jit(solution)/shard_map/ppermute | solution.py:197
  4.7 6.8 %collective-permute-start.4 = (bf16[512,128]{1,0:T(8,128)(2,1)}, bf16[512,128]{1,0:T(8,128)(2,1)S(1)}, u32[]{:S(2)}, u32[]{:S(2)}) collective-permute-start(bf16[512,128]{1,0:T(8,128)(2,1)} %feats.1), channel_id=1, source_target_pairs={{0,2},{1,3},{2,0},{3,1},{4,6},{5,7},{6,4},{7,5},{8,10},{9,11},{10,... | collective-permute-start | bytes 393224 | tf_op jit(solution)/shard_map/ppermute | solution.py:197
  6.3 5.3 %collective-permute-start.5 = (bf16[512,128]{1,0:T(8,128)(2,1)}, bf16[512,128]{1,0:T(8,128)(2,1)S(1)}, u32[]{:S(2)}, u32[]{:S(2)}) collective-permute-start(bf16[512,128]{1,0:T(8,128)(2,1)} %feats.1), channel_id=1, source_target_pairs={{0,1},{1,0},{2,3},{3,2},{4,5},{5,4},{6,7},{7,6},{8,9},{9,8},{10,11... | collective-permute-start | bytes 393224 | tf_op jit(solution)/shard_map/ppermute | solution.py:197
  6.3 1.0 %copy-start.1 = (bf16[1024,128]{1,0:T(8,128)(2,1)S(1)}, bf16[1024,128]{1,0:T(8,128)(2,1)}, u32[]{:S(2)}) copy-start(bf16[1024,128]{1,0:T(8,128)(2,1)} %weight.1) | copy-start | bytes 786436
  9.1 12.8 %copy-start.5 = (s32[80]{0:T(128)S(1)}, s32[80]{0:T(128)}, u32[]{:S(2)}) copy-start(s32[80]{0:T(128)} %all_cols.1) | copy-start | bytes 964
  9.1 12.8 %copy-start.6 = (s32[4]{0:T(128)S(1)}, s32[4]{0:T(128)}, u32[]{:S(2)}) copy-start(s32[4]{0:T(128)} %all_counts.1) | copy-start | bytes 52
  11.6 5.0 %collective-permute-start.6 = (bf16[512,128]{1,0:T(8,128)(2,1)S(1)}, bf16[512,128]{1,0:T(8,128)(2,1)S(1)}, u32[]{:S(2)}, u32[]{:S(2)}) collective-permute-start(bf16[512,128]{1,0:T(8,128)(2,1)S(1)} %collective-permute-done.3.refs_4_), channel_id=1, source_target_pairs={{0,2},{1,3},{2,0},{3,1},{4,6},{5,7},{6,4},{7,5},{8,10},{9,11},{10,... | collective-permute-start | bytes 393224 | tf_op jit(solution)/shard_map/ppermute | solution.py:197
  13.0 3.5 %collective-permute-start.7 = (bf16[512,128]{1,0:T(8,128)(2,1)S(1)}, bf16[512,128]{1,0:T(8,128)(2,1)S(1)}, u32[]{:S(2)}, u32[]{:S(2)}) collective-permute-start(bf16[512,128]{1,0:T(8,128)(2,1)S(1)} %collective-permute-done.3.refs_4_), channel_id=1, source_target_pairs={{0,1},{1,0},{2,3},{3,2},{4,5},{5,4},{6,7},{7,6},{8,9},{9,8},{10,11... | collective-permute-start | bytes 393224 | tf_op jit(solution)/shard_map/ppermute | solution.py:197
  13.0 3.5 %collective-permute-start.8 = (bf16[512,128]{1,0:T(8,128)(2,1)S(1)}, bf16[512,128]{1,0:T(8,128)(2,1)S(1)}, u32[]{:S(2)}, u32[]{:S(2)}) collective-permute-start(bf16[512,128]{1,0:T(8,128)(2,1)S(1)} %collective-permute-done.4.refs_2_), channel_id=1, source_target_pairs={{0,1},{1,0},{2,3},{3,2},{4,5},{5,4},{6,7},{7,6},{8,9},{9,8},{10,11... | collective-permute-start | bytes 393224 | tf_op jit(solution)/shard_map/ppermute | solution.py:197
  16.5 1.4 %collective-permute-start.9 = (bf16[512,128]{1,0:T(8,128)(2,1)S(1)}, bf16[512,128]{1,0:T(8,128)(2,1)S(1)}, u32[]{:S(2)}, u32[]{:S(2)}) collective-permute-start(bf16[512,128]{1,0:T(8,128)(2,1)S(1)} %collective-permute-done.6.refs_6_), channel_id=1, source_target_pairs={{0,1},{1,0},{2,3},{3,2},{4,5},{5,4},{6,7},{7,6},{8,9},{9,8},{10,11... | collective-permute-start | bytes 393224 | tf_op jit(solution)/shard_map/ppermute | solution.py:197
  16.5 9.8 %collective-permute-start.2 = (bf16[2,512,128]{2,1,0:T(8,128)(2,1)S(1)}, bf16[2,512,128]{2,1,0:T(8,128)(2,1)S(1)}, u32[]{:S(2)}, u32[]{:S(2)}) collective-permute-start(bf16[2,512,128]{2,1,0:T(8,128)(2,1)S(1)} %get-tuple-element.64.refs_9_), channel_id=1, source_target_pairs={{0,1},{1,0},{2,3},{3,2},{4,5},{5,4},{6,7},{7,6},{8,9},{9,8},{10,11... | collective-permute-start | bytes 786440 | tf_op jit(solution)/shard_map/ppermute | solution.py:197
  18.3 8.7 %collective-permute-start.10 = (bf16[512,128]{1,0:T(8,128)(2,1)S(1)}, bf16[512,128]{1,0:T(8,128)(2,1)S(1)}, u32[]{:S(2)}, u32[]{:S(2)}) collective-permute-start(bf16[512,128]{1,0:T(8,128)(2,1)S(1)} %get-tuple-element.75.hidden), channel_id=1, source_target_pairs={{0,8},{8,0},{16,24},{24,16},{1,9},{9,1},{17,25},{25,17},{2,10},{10... | collective-permute-start | bytes 393224 | tf_op jit(solution)/shard_map/ppermute | solution.py:197
  19.9 8.1 %collective-permute-start.11 = (bf16[512,128]{1,0:T(8,128)(2,1)S(1)}, bf16[512,128]{1,0:T(8,128)(2,1)S(1)}, u32[]{:S(2)}, u32[]{:S(2)}) collective-permute-start(bf16[512,128]{1,0:T(8,128)(2,1)S(1)} %get-tuple-element.75.hidden), channel_id=1, source_target_pairs={{0,16},{8,24},{16,0},{24,8},{1,17},{9,25},{17,1},{25,9},{2,18},{10... | collective-permute-start | bytes 393224 | tf_op jit(solution)/shard_map/ppermute | solution.py:197
  21.5 6.6 %collective-permute-start.12 = (bf16[512,128]{1,0:T(8,128)(2,1)S(1)}, bf16[512,128]{1,0:T(8,128)(2,1)S(1)}, u32[]{:S(2)}, u32[]{:S(2)}) collective-permute-start(bf16[512,128]{1,0:T(8,128)(2,1)S(1)} %get-tuple-element.75.hidden), channel_id=1, source_target_pairs={{0,24},{8,16},{16,8},{24,0},{1,25},{9,17},{17,9},{25,1},{2,26},{10... | collective-permute-start | bytes 393224 | tf_op jit(solution)/shard_map/ppermute | solution.py:197
  21.9 1.7 %copy-start = (bf16[80,128,128]{2,1,0:T(8,128)(2,1)S(1)}, bf16[80,128,128]{2,1,0:T(8,128)(2,1)}, u32[]{:S(2)}) copy-start(bf16[80,128,128]{2,1,0:T(8,128)(2,1)} %vals.1) | copy-start | bytes 7864324
  26.3 1.7 %copy-start.4 = (bf16[512,128]{1,0:T(8,128)(2,1)S(1)}, bf16[512,128]{1,0:T(8,128)(2,1)}, u32[]{:S(2)}) copy-start(bf16[512,128]{1,0:T(8,128)(2,1)} %refs_6_.1) | copy-start | bytes 393220
  29.9 6.8 %collective-permute-start.13 = (bf16[512,128]{1,0:T(8,128)(2,1)S(1)}, bf16[512,128]{1,0:T(8,128)(2,1)S(1)}, u32[]{:S(2)}, u32[]{:S(2)}) collective-permute-start(bf16[512,128]{1,0:T(8,128)(2,1)S(1)} %get-tuple-element.79), channel_id=1, source_target_pairs={{0,8},{8,0},{16,24},{24,16},{1,9},{9,1},{17,25},{25,17},{2,10},{10... | collective-permute-start | bytes 393224 | tf_op jit(solution)/shard_map/ppermute | solution.py:197
  31.2 8.1 %collective-permute-start.14 = (bf16[512,128]{1,0:T(8,128)(2,1)S(1)}, bf16[512,128]{1,0:T(8,128)(2,1)S(1)}, u32[]{:S(2)}, u32[]{:S(2)}) collective-permute-start(bf16[512,128]{1,0:T(8,128)(2,1)S(1)} %get-tuple-element.80), channel_id=1, source_target_pairs={{0,16},{8,24},{16,0},{24,8},{1,17},{9,25},{17,1},{25,9},{2,18},{10... | collective-permute-start | bytes 393224 | tf_op jit(solution)/shard_map/ppermute | solution.py:197
  32.6 7.3 %collective-permute-start.15 = (bf16[512,128]{1,0:T(8,128)(2,1)S(1)}, bf16[512,128]{1,0:T(8,128)(2,1)S(1)}, u32[]{:S(2)}, u32[]{:S(2)}) collective-permute-start(bf16[512,128]{1,0:T(8,128)(2,1)S(1)} %get-tuple-element.81), channel_id=1, source_target_pairs={{0,24},{8,16},{16,8},{24,0},{1,25},{9,17},{17,9},{25,1},{2,26},{10... | collective-permute-start | bytes 393224 | tf_op jit(solution)/shard_map/ppermute | solution.py:197
  34.0 6.5 %collective-permute-start.21 = (bf16[512,128]{1,0:T(8,128)(2,1)S(1)}, bf16[512,128]{1,0:T(8,128)(2,1)S(1)}, u32[]{:S(2)}, u32[]{:S(2)}) collective-permute-start(bf16[512,128]{1,0:T(8,128)(2,1)S(1)} %get-tuple-element.89.refs_2_), channel_id=1, source_target_pairs={{0,8},{8,0},{16,24},{24,16},{1,9},{9,1},{17,25},{25,17},{2,10},{10... | collective-permute-start | bytes 393224 | tf_op jit(solution)/shard_map/ppermute | solution.py:197
  35.3 6.5 %collective-permute-start.22 = (bf16[512,128]{1,0:T(8,128)(2,1)S(1)}, bf16[512,128]{1,0:T(8,128)(2,1)S(1)}, u32[]{:S(2)}, u32[]{:S(2)}) collective-permute-start(bf16[512,128]{1,0:T(8,128)(2,1)S(1)} %get-tuple-element.90.refs_3_), channel_id=1, source_target_pairs={{0,16},{8,24},{16,0},{24,8},{1,17},{9,25},{17,1},{25,9},{2,18},{10... | collective-permute-start | bytes 393224 | tf_op jit(solution)/shard_map/ppermute | solution.py:197
  36.7 7.0 %collective-permute-start.17 = (bf16[512,128]{1,0:T(8,128)(2,1)S(1)}, bf16[512,128]{1,0:T(8,128)(2,1)S(1)}, u32[]{:S(2)}, u32[]{:S(2)}) collective-permute-start(bf16[512,128]{1,0:T(8,128)(2,1)S(1)} %get-tuple-element.77.grad_pre.pre), channel_id=1, source_target_pairs={{0,1},{1,0},{2,3},{3,2},{4,5},{5,4},{6,7},{7,6},{8,9},{9,8},{10,11... | collective-permute-start | bytes 393224 | tf_op jit(solution)/shard_map/ppermute | solution.py:197
  39.9 3.8 %collective-permute-start.16 = (bf16[512,128]{1,0:T(8,128)(2,1)S(1)}, bf16[512,128]{1,0:T(8,128)(2,1)S(1)}, u32[]{:S(2)}, u32[]{:S(2)}) collective-permute-start(bf16[512,128]{1,0:T(8,128)(2,1)S(1)} %shard_map.102.hidden.grads), channel_id=1, source_target_pairs={{0,1},{1,0},{2,3},{3,2},{4,5},{5,4},{6,7},{7,6},{8,9},{9,8},{10,11... | collective-permute-start | bytes 393224 | tf_op jit(solution)/shard_map/ppermute | solution.py:197
  41.8 7.7 %collective-permute-start.23 = (bf16[512,256]{1,0:T(8,128)(2,1)S(1)}, bf16[512,256]{1,0:T(8,128)(2,1)S(1)}, u32[]{:S(2)}, u32[]{:S(2)}) collective-permute-start(bf16[512,256]{1,0:T(8,128)(2,1)S(1)} %get-tuple-element.95.top), channel_id=1, source_target_pairs={{0,16},{8,24},{16,0},{24,8},{1,17},{9,25},{17,1},{25,9},{2,18},{10... | collective-permute-start | bytes 786440 | tf_op jit(solution)/shard_map/ppermute | solution.py:197
  42.9 7.3 %collective-permute-start.24 = (bf16[512,256]{1,0:T(8,128)(2,1)S(1)}, bf16[512,256]{1,0:T(8,128)(2,1)S(1)}, u32[]{:S(2)}, u32[]{:S(2)}) collective-permute-start(bf16[512,256]{1,0:T(8,128)(2,1)S(1)} %get-tuple-element.96.bottom), channel_id=1, source_target_pairs={{0,8},{8,0},{16,24},{24,16},{1,9},{9,1},{17,25},{25,17},{2,10},{10... | collective-permute-start | bytes 786440 | tf_op jit(solution)/shard_map/ppermute | solution.py:197
  44.5 11.9 %collective-permute-start.18 = (bf16[512,128]{1,0:T(8,128)(2,1)S(1)}, bf16[512,128]{1,0:T(8,128)(2,1)S(1)}, u32[]{:S(2)}, u32[]{:S(2)}) collective-permute-start(bf16[512,128]{1,0:T(8,128)(2,1)S(1)} %get-tuple-element.84), channel_id=1, source_target_pairs={{0,4},{1,5},{2,6},{3,7},{4,0},{5,1},{6,2},{7,3},{8,12},{9,13},{10,... | collective-permute-start | bytes 393224 | tf_op jit(solution)/shard_map/ppermute | solution.py:197
  47.0 9.4 %collective-permute-start.19 = (bf16[512,128]{1,0:T(8,128)(2,1)S(1)}, bf16[512,128]{1,0:T(8,128)(2,1)S(1)}, u32[]{:S(2)}, u32[]{:S(2)}) collective-permute-start(bf16[512,128]{1,0:T(8,128)(2,1)S(1)} %get-tuple-element.85), channel_id=1, source_target_pairs={{0,6},{1,7},{2,4},{3,5},{4,2},{5,3},{6,0},{7,1},{8,14},{9,15},{10,... | collective-permute-start | bytes 393224 | tf_op jit(solution)/shard_map/ppermute | solution.py:197
  48.3 8.3 %collective-permute-start.20 = (bf16[512,128]{1,0:T(8,128)(2,1)S(1)}, bf16[512,128]{1,0:T(8,128)(2,1)S(1)}, u32[]{:S(2)}, u32[]{:S(2)}) collective-permute-start(bf16[512,128]{1,0:T(8,128)(2,1)S(1)} %get-tuple-element.86), channel_id=1, source_target_pairs={{0,2},{1,3},{2,0},{3,1},{4,6},{5,7},{6,4},{7,5},{8,10},{9,11},{10,... | collective-permute-start | bytes 393224 | tf_op jit(solution)/shard_map/ppermute | solution.py:197
  50.3 5.0 %collective-permute-start = (bf16[512,128]{1,0:T(8,128)(2,1)S(1)}, bf16[512,128]{1,0:T(8,128)(2,1)S(1)}, u32[]{:S(2)}, u32[]{:S(2)}) collective-permute-start(bf16[512,128]{1,0:T(8,128)(2,1)S(1)} %get-tuple-element.12.top), channel_id=1, source_target_pairs={{0,8},{8,0},{16,24},{24,16},{1,9},{9,1},{17,25},{25,17},{2,10},{10... | collective-permute-start | bytes 393224 | tf_op jit(solution)/shard_map/cond/branch_1_fun/ppermute | solution.py:197
  51.1 5.0 %collective-permute-start.1 = (bf16[512,128]{1,0:T(8,128)(2,1)S(1)}, bf16[512,128]{1,0:T(8,128)(2,1)S(1)}, u32[]{:S(2)}, u32[]{:S(2)}) collective-permute-start(bf16[512,128]{1,0:T(8,128)(2,1)S(1)} %get-tuple-element.13.bottom), channel_id=1, source_target_pairs={{0,16},{8,24},{16,0},{24,8},{1,17},{9,25},{17,1},{25,9},{2,18},{10... | collective-permute-start | bytes 393224 | tf_op jit(solution)/shard_map/cond/branch_1_fun/ppermute | solution.py:197
  56.1 1.2 %copy-start.7 = (f32[1024,128]{1,0:T(8,128)}, f32[1024,128]{1,0:T(8,128)S(1)}, u32[]{:S(2)}) copy-start(f32[1024,128]{1,0:T(8,128)S(1)} %get-tuple-element.62) | copy-start | bytes 1572868
  56.1 1.1 %copy-start.8 = (f32[1024,128]{1,0:T(8,128)}, f32[1024,128]{1,0:T(8,128)S(1)}, u32[]{:S(2)}) copy-start(f32[1024,128]{1,0:T(8,128)S(1)} %get-tuple-element.63) | copy-start | bytes 1572868
  (2 other events, 1.9 us)

commit v6 on v5

--- a/solution.py
+++ b/solution.py
@@ -74,7 +74,7 @@
     lax.fori_loop(0, adj.shape[1] // tile, flip, 0)
 
 
-def prepare_kernel(nf, feats, weight, root, mine, near, far):
+def prepare_kernel(nf, feats, weight, root, mine, near, far, right):
     width = weight.shape[1]
     me = lax.axis_index("feat")
     mine[...] = feats[...]
@@ -84,21 +84,20 @@
             rows = pl.ds(pl.multiple_of((me ^ (2 * k + flip)) * width, width), width)
             out[0, place, :] = weight[rows, :]
             out[1, place, :] = root[rows, :]
+            into = slice((2 * k + flip) * width, (2 * k + flip + 1) * width)
+            right[into, :] = jnp.concatenate([weight[rows, :], root[rows, :]], 1)
 
 
 def forward_kernel(nf, *refs):
-    pieces, (near, far, hidden, own) = refs[:nf], refs[nf:]
-    width = hidden.shape[1]
-    total = None
-    for k in range(nf // 2):
-        place = slice(k * width, (k + 1) * width)
-        left = jnp.concatenate([pieces[2 * k][...], pieces[2 * k + 1][...]], 1)
-        top = jnp.concatenate([near[0, place, :], near[1, place, :]], 1)
-        bottom = jnp.concatenate([far[0, place, :], far[1, place, :]], 1)
-        part = dot(left, jnp.concatenate([top, bottom], 0))
-        total = part if total is None else total + part
-    hidden[...] = total[:, :width].astype(BF)
-    own[...] = total[:, width:]
+    pieces, (right, hidden, own) = refs[:nf], refs[nf:]
+    rows, width = hidden.shape
+    half = rows // 2
+    for at in (0, half):
+        part = slice(at, at + half)
+        left = jnp.concatenate([piece[part, :] for piece in pieces], 1)
+        total = dot(left, right[...])
+        hidden[part, :] = total[:, :width].astype(BF)
+        own[part, :] = total[:, width:]
 
 
 def transpose_kernel(nf, *refs):
@@ -122,23 +121,24 @@
     sent = refs[nr + 4 :]
     me = lax.axis_index("rows")
     rows = begun.shape[0]
-    pre = begun[...]
-    for j in range(1, nr):
-        place = pl.ds(pl.multiple_of((me ^ j) * rows, rows), rows)
-        pre = pre + dot(adj[:, place], hidden[j - 1][...])
-    sig = jax.nn.sigmoid(pre)
-    grad = (grad_out[...].astype(F32) * sig * (1.0 + pre * (1.0 - sig))).astype(BF)
-    grad_pre[...] = grad
-    for j in range(1, nr):
-        place = pl.ds(pl.multiple_of((me ^ j) * rows, rows), rows)
-        sent[j - 1][...] = dot(adj_t[place, :], grad).astype(BF)
-
-
-def keep_kernel(adj_t, grad_pre, feats_t, kept, top, bottom):
+    places = [pl.ds(pl.multiple_of((me ^ j) * rows, rows), rows) for j in range(1, nr)]
+    half = rows // 2
+    for at in (0, half):
+        part = slice(at, at + half)
+        pre = begun[part, :]
+        for j in range(nr - 1):
+            pre = pre + dot(adj[part, places[j]], hidden[j][...])
+        sig = jax.nn.sigmoid(pre)
+        grad = grad_out[part, :].astype(F32) * sig * (1.0 + pre * (1.0 - sig))
+        grad_pre[part, :] = grad.astype(BF)
+    for j in range(nr - 1):
+        sent[j][...] = dot(adj_t[places[j], :], grad_pre[...]).astype(BF)
+
+
+def keep_kernel(adj_t, grad_pre, kept):
     rows = kept.shape[0]
     place = pl.ds(pl.multiple_of(lax.axis_index("rows") * rows, rows), rows)
     kept[...] = dot(adj_t[place, :], grad_pre[...])
-    weights_kernel(feats_t, grad_pre, top, bottom)
 
 
 def sum_kernel(n, *refs):
@@ -148,19 +148,32 @@
     refs[n][...] = total.astype(refs[n].dtype)
 
 
-def feats_kernel(nz, hidden, pre, hidden_2, pre_2, near, near_2, *out):
-    width = hidden.shape[1]
-    left = jnp.concatenate([hidden[...], pre[...], hidden_2[...], pre_2[...]], 1)
+def back_kernel(nz, near, near_2, back):
+    width = near.shape[2]
     for k in range(nz):
         place = slice(k * width, (k + 1) * width)
-        right = [near[0, place, :], near[1, place, :], near_2[0, place, :], near_2[1, place, :]]
-        out[k][...] = dot_nt(left, jnp.concatenate(right, 1)).astype(out[k].dtype)
+        rows = [near[0, place, :], near[1, place, :], near_2[0, place, :], near_2[1, place, :]]
+        back[:, place] = jnp.concatenate(rows, 1).T
+
+
+def feats_kernel(nz, hidden, pre, hidden_2, pre_2, back, *out):
+    rows, width = hidden.shape
+    half = rows // 2
+    for at in (0, half):
+        part = slice(at, at + half)
+        arrays = hidden, pre, hidden_2, pre_2
+        total = dot(jnp.concatenate([array[part, :] for array in arrays], 1), back[...])
+        for k in range(nz):
+            out[k][part, :] = total[:, k * width : (k + 1) * width].astype(out[k].dtype)
 
 
 def weights_kernel(feats_t, grads, top, bottom):
     half = top.shape[0]
-    top[...] = dot(feats_t[:half, :], grads[...]).astype(BF)
-    bottom[...] = dot(feats_t[half:, :], grads[...]).astype(BF)
+    step = half // 2
+    for at in range(0, 2 * half, step):
+        out = top if at < half else bottom
+        place = slice(at % half, at % half + step)
+        out[place, :] = dot(feats_t[at : at + step, :], grads[...]).astype(BF)
 
 
 def join_kernel(*refs):
@@ -211,9 +224,11 @@
         ],
         limit=48 * 1024 * 1024,
     )
-    mine, near, far = call(
+    mine, near, far, right = call(
         functools.partial(prepare_kernel, nf),
-        [sds((rows, width), BF)] + [sds((2, depth // 2, width), BF)] * 2,
+        [sds((rows, width), BF)]
+        + [sds((2, depth // 2, width), BF)] * 2
+        + [sds((depth, 2 * width), BF)],
         [VMEM] * 3,
         (node_feats, weight, root_weight),
     )
@@ -243,8 +258,8 @@
     hidden, own = call(
         functools.partial(forward_kernel, nf),
         [sds((rows, width), BF), sds((rows, width), F32)],
-        [VMEM] * (nf + 2),
-        (*pieces, near, far),
+        [VMEM] * (nf + 1),
+        (*pieces, right),
         flops=4 * rows * depth * width,
     )
     gathered = [hidden] + [swap(hidden, "rows", j) for j in range(1, nr)]
@@ -254,7 +269,13 @@
         [VMEM] * nf,
         pieces,
     )
-    adj_t, near_2 = lax.optimization_barrier((adj_t, near_2))
+    (back,) = call(
+        functools.partial(back_kernel, nz),
+        [sds((4 * width, depth // 2), BF)],
+        [VMEM] * 2,
+        (near, near_2),
+    )
+    adj_t, back, feats_t = lax.optimization_barrier((adj_t, back, feats_t))
     (begun,) = call(
         begin_kernel,
         [sds((rows, width), F32)],
@@ -270,12 +291,19 @@
         flops=4 * rows * nodes * width,
         limit=max(32 * 1024 * 1024, 10 * rows * nodes),
     )
-    kept, *root_part = call(
+    root_part = call(
+        weights_kernel,
+        [sds((depth // 2, width), BF)] * 2,
+        [VMEM] * 2,
+        (feats_t, grad_pre),
+        flops=2 * rows * depth * width,
+    )
+    (kept,) = call(
         keep_kernel,
-        [sds((rows, width), F32)] + [sds((depth // 2, width), BF)] * 2,
-        [VMEM] * 3,
-        (adj_t, grad_pre, feats_t),
-        flops=4 * rows * depth * width,
+        [sds((rows, width), F32)],
+        [VMEM] * 2,
+        (adj_t, grad_pre),
+        flops=2 * rows * rows * width,
     )
     pre_2 = swap(grad_pre, "feat", 1)
     sums = [kept] + [swap(part, "rows", j + 1) for j, part in enumerate(sent)]
@@ -286,8 +314,8 @@
     parts = call(
         functools.partial(feats_kernel, nz),
         [sds((rows, width), BF if k else F32) for k in range(nz)],
-        [VMEM] * 6,
-        (grad_hidden, grad_pre, hidden_2, pre_2, near, near_2),
+        [VMEM] * 5,
+        (grad_hidden, grad_pre, hidden_2, pre_2, back),
         flops=4 * rows * depth * width,
     )
     weight_part = call(

time: 57.5 us -> 57 us (level)
  waiting for transfers between devices: 17.3 us -> 15.7 us
  starting transfers between devices: 26.2 us -> 27.1 us
    ppermute x25, waiting for transfers between devices: 17.3 us -> 15.7 us  [swap(): lax.ppermute(array, axis, [(i, i ^ mask) for i in range(lax.axis_size(axi...]
    ppermute x25, starting transfers between devices: 26.2 us -> 27.1 us  [swap(): lax.ppermute(array, axis, [(i, i ^ mask) for i in range(lax.axis_size(axi...]
    pallas_call x16 -> x18, Pallas kernels: 8.38 us -> 8.4 us  [call(): pl.pallas_call(body, out_shape=outs, in_specs=specs, out_specs=[VMEM] * l...]
  transfers between devices with their start and end apart: 25 -> 25, of which waited for: 14 -> 13; matrix products, arithmetic and copies ran while one was open for 0% -> 0% of each run, Pallas kernels for 10% -> 11%
where the time goes in v6:
time: 57 us; the launch traced here: 56.7 us
  starting transfers between devices  27.1 us (48%)
  waiting for transfers between devices  15.7 us (28%)
  Pallas kernels  8.4 us (15%)
  local copies, waits for them, and re-layouts  4.57 us (8%)
  between operations  0.88 us (2%)
    ppermute x25, starting transfers between devices, swap(): lax.ppermute(array, axis, [(i, i ^ mask) for i in range(lax.axis_size(axi...  27.1 us
    ppermute x25, waiting for transfers between devices, swap(): lax.ppermute(array, axis, [(i, i ^ mask) for i in range(lax.axis_size(axi...  15.7 us
    pallas_call x18, Pallas kernels, call(): pl.pallas_call(body, out_shape=outs, in_specs=specs, out_specs=[VMEM] * l...  8.4 us
    unnamed x18, local copies, waits for them, and re-layouts  4.57 us
  transfers between devices with their start and end apart: 25, of which 13 were waited for; matrix products, arithmetic and copies ran while one was open for 0% of the time, Pallas kernels for 11%

profile of v6, /device:TPU:0, one launch (start us, length us, event | category | flops | bytes accessed | tf_op | source)
XLA Modules:
  0.0 56.7 jit_solution(15581172222665346591)
XLA Ops:
  0.6 4.1 %collective-permute-start.2 = (bf16[512,128]{1,0:T(8,128)(2,1)}, bf16[512,128]{1,0:T(8,128)(2,1)S(1)}, u32[]{:S(2)}, u32[]{:S(2)}) collective-permute-start(bf16[512,128]{1,0:T(8,128)(2,1)} %feats.1), channel_id=1, source_target_pairs={{0,4},{1,5},{2,6},{3,7},{4,0},{5,1},{6,2},{7,3},{8,12},{9,13},{10,... | collective-permute-start | bytes 393224 | tf_op jit(solution)/shard_map/ppermute | solution.py:210
  4.7 1.6 %collective-permute-start.3 = (bf16[512,128]{1,0:T(8,128)(2,1)}, bf16[512,128]{1,0:T(8,128)(2,1)S(1)}, u32[]{:S(2)}, u32[]{:S(2)}) collective-permute-start(bf16[512,128]{1,0:T(8,128)(2,1)} %feats.1), channel_id=1, source_target_pairs={{0,2},{1,3},{2,0},{3,1},{4,6},{5,7},{6,4},{7,5},{8,10},{9,11},{10,... | collective-permute-start | bytes 393224 | tf_op jit(solution)/shard_map/ppermute | solution.py:210
  6.3 0.9 %copy-done.1 = bf16[1024,128]{1,0:T(8,128)(2,1)S(1)} copy-done((bf16[1024,128]{1,0:T(8,128)(2,1)S(1)}, bf16[1024,128]{1,0:T(8,128)(2,1)}, u32[]{:S(2)}) %copy-start.1) | copy-done | bytes 262168
  7.3 0.9 %copy-done.2 = bf16[1024,128]{1,0:T(8,128)(2,1)S(1)} copy-done((bf16[1024,128]{1,0:T(8,128)(2,1)S(1)}, bf16[1024,128]{1,0:T(8,128)(2,1)}, u32[]{:S(2)}) %copy-start.2) | copy-done | bytes 262168
  8.2 0.9 %copy-done.3 = bf16[512,128]{1,0:T(8,128)(2,1)S(1)} copy-done((bf16[512,128]{1,0:T(8,128)(2,1)S(1)}, bf16[512,128]{1,0:T(8,128)(2,1)}, u32[]{:S(2)}) %copy-start.3) | copy-done | bytes 131096
  9.2 2.1 %collective-permute-done.2.refs_4_ = bf16[512,128]{1,0:T(8,128)(2,1)S(1)} collective-permute-done((bf16[512,128]{1,0:T(8,128)(2,1)}, bf16[512,128]{1,0:T(8,128)(2,1)S(1)}, u32[]{:S(2)}, u32[]{:S(2)}) %collective-permute-start.2) | collective-permute-done | bytes 131104 | tf_op jit(solution)/shard_map/ppermute | solution.py:210
  11.6 1.4 %collective-permute-start.6 = (bf16[512,128]{1,0:T(8,128)(2,1)S(1)}, bf16[512,128]{1,0:T(8,128)(2,1)S(1)}, u32[]{:S(2)}, u32[]{:S(2)}) collective-permute-start(bf16[512,128]{1,0:T(8,128)(2,1)S(1)} %collective-permute-done.2.refs_4_), channel_id=1, source_target_pairs={{0,2},{1,3},{2,0},{3,1},{4,6},{5,7},{6,4},{7,5},{8,10},{9,11},{10,... | collective-permute-start | bytes 393224 | tf_op jit(solution)/shard_map/ppermute | solution.py:210
  13.0 0.5 collective-permute-start.8
  13.5 3.0 %collective-permute-done.6.refs_6_ = bf16[512,128]{1,0:T(8,128)(2,1)S(1)} collective-permute-done((bf16[512,128]{1,0:T(8,128)(2,1)S(1)}, bf16[512,128]{1,0:T(8,128)(2,1)S(1)}, u32[]{:S(2)}, u32[]{:S(2)}) %collective-permute-start.6) | collective-permute-done | bytes 131104 | tf_op jit(solution)/shard_map/ppermute | solution.py:210
  17.1 0.8 %collective-permute-done.9.refs_7_ = bf16[512,128]{1,0:T(8,128)(2,1)S(1)} collective-permute-done((bf16[512,128]{1,0:T(8,128)(2,1)S(1)}, bf16[512,128]{1,0:T(8,128)(2,1)S(1)}, u32[]{:S(2)}, u32[]{:S(2)}) %collective-permute-start.9) | collective-permute-done | bytes 131104 | tf_op jit(solution)/shard_map/ppermute | solution.py:210
  18.3 1.6 %collective-permute-start.10 = (bf16[512,128]{1,0:T(8,128)(2,1)S(1)}, bf16[512,128]{1,0:T(8,128)(2,1)S(1)}, u32[]{:S(2)}, u32[]{:S(2)}) collective-permute-start(bf16[512,128]{1,0:T(8,128)(2,1)S(1)} %get-tuple-element.77.hidden), channel_id=1, source_target_pairs={{0,8},{8,0},{16,24},{24,16},{1,9},{9,1},{17,25},{25,17},{2,10},{10... | collective-permute-start | bytes 393224 | tf_op jit(solution)/shard_map/ppermute | solution.py:210
  19.9 1.5 %collective-permute-start.11 = (bf16[512,128]{1,0:T(8,128)(2,1)S(1)}, bf16[512,128]{1,0:T(8,128)(2,1)S(1)}, u32[]{:S(2)}, u32[]{:S(2)}) collective-permute-start(bf16[512,128]{1,0:T(8,128)(2,1)S(1)} %get-tuple-element.77.hidden), channel_id=1, source_target_pairs={{0,16},{8,24},{16,0},{24,8},{1,17},{9,25},{17,1},{25,9},{2,18},{10... | collective-permute-start | bytes 393224 | tf_op jit(solution)/shard_map/ppermute | solution.py:210
  21.9 1.7 %copy-done = bf16[80,128,128]{2,1,0:T(8,128)(2,1)S(1)} copy-done((bf16[80,128,128]{2,1,0:T(8,128)(2,1)S(1)}, bf16[80,128,128]{2,1,0:T(8,128)(2,1)}, u32[]{:S(2)}) %copy-start) | copy-done | bytes 2621464
  23.6 1.7 %shard_map.94.adj.refs_3_ = bf16[512,2048]{1,0:T(8,128)(2,1)S(1)} custom-call(s32[4]{0:T(128)S(1)} %copy-done.6, s32[80]{0:T(128)S(1)} %copy-done.5, bf16[80,128,128]{2,1,0:T(8,128)(2,1)S(1)} %copy-done), custom_call_target="tpu_custom_call" | custom-call | flops 4194304 | bytes 4718928 | tf_op jit(solution)/shard_map/pallas_call | solution.py:28
  25.4 1.4 %shard_map.95.refs_4_.adj_t = bf16[2048,512]{1,0:T(8,128)(2,1)S(1)} custom-call(bf16[512,2048]{1,0:T(8,128)(2,1)S(1)} %shard_map.94.adj.refs_3_), custom_call_target="tpu_custom_call" | custom-call | bytes 4194304 | tf_op jit(solution)/shard_map/pallas_call | solution.py:28
  28.0 1.1 %shard_map.101 = (bf16[512,128]{1,0:T(8,128)(2,1)S(1)}, bf16[512,128]{1,0:T(8,128)(2,1)S(1)}, bf16[512,128]{1,0:T(8,128)(2,1)S(1)}, bf16[512,128]{1,0:T(8,128)(2,1)S(1)}) custom-call(bf16[512,128]{1,0:T(8,128)(2,1)S(1)} %collective-permute-done.10.refs_0_, bf16[512,128]{1,0:T(8,128)(2,1)S(1)} %collective-permute-done.11.refs_1_, ...), custom_call_target="tpu_custom_call" | custom-call | flops 536870912 | bytes 5505024 | tf_op jit(solution)/shard_map/pallas_call | solution.py:28
  29.2 1.3 %collective-permute-start.13 = (bf16[512,128]{1,0:T(8,128)(2,1)S(1)}, bf16[512,128]{1,0:T(8,128)(2,1)S(1)}, u32[]{:S(2)}, u32[]{:S(2)}) collective-permute-start(bf16[512,128]{1,0:T(8,128)(2,1)S(1)} %get-tuple-element.80), channel_id=1, source_target_pairs={{0,8},{8,0},{16,24},{24,16},{1,9},{9,1},{17,25},{25,17},{2,10},{10... | collective-permute-start | bytes 393224 | tf_op jit(solution)/shard_map/ppermute | solution.py:210
  30.5 2.0 %collective-permute-start.14 = (bf16[512,128]{1,0:T(8,128)(2,1)S(1)}, bf16[512,128]{1,0:T(8,128)(2,1)S(1)}, u32[]{:S(2)}, u32[]{:S(2)}) collective-permute-start(bf16[512,128]{1,0:T(8,128)(2,1)S(1)} %get-tuple-element.81), channel_id=1, source_target_pairs={{0,16},{8,24},{16,0},{24,8},{1,17},{9,25},{17,1},{25,9},{2,18},{10... | collective-permute-start | bytes 393224 | tf_op jit(solution)/shard_map/ppermute | solution.py:210
  33.1 1.3 %collective-permute-start.21 = (bf16[512,128]{1,0:T(8,128)(2,1)S(1)}, bf16[512,128]{1,0:T(8,128)(2,1)S(1)}, u32[]{:S(2)}, u32[]{:S(2)}) collective-permute-start(bf16[512,128]{1,0:T(8,128)(2,1)S(1)} %get-tuple-element.91.refs_2_), channel_id=1, source_target_pairs={{0,8},{8,0},{16,24},{24,16},{1,9},{9,1},{17,25},{25,17},{2,10},{10... | collective-permute-start | bytes 393224 | tf_op jit(solution)/shard_map/ppermute | solution.py:210
  34.4 2.0 %collective-permute-start.22 = (bf16[512,128]{1,0:T(8,128)(2,1)S(1)}, bf16[512,128]{1,0:T(8,128)(2,1)S(1)}, u32[]{:S(2)}, u32[]{:S(2)}) collective-permute-start(bf16[512,128]{1,0:T(8,128)(2,1)S(1)} %get-tuple-element.92.refs_3_), channel_id=1, source_target_pairs={{0,16},{8,24},{16,0},{24,8},{1,17},{9,25},{17,1},{25,9},{2,18},{10... | collective-permute-start | bytes 393224 | tf_op jit(solution)/shard_map/ppermute | solution.py:210
  36.9 1.6 %collective-permute-done.14.refs_2_ = bf16[512,128]{1,0:T(8,128)(2,1)S(1)} collective-permute-done((bf16[512,128]{1,0:T(8,128)(2,1)S(1)}, bf16[512,128]{1,0:T(8,128)(2,1)S(1)}, u32[]{:S(2)}, u32[]{:S(2)}) %collective-permute-start.14) | collective-permute-done | bytes 131104 | tf_op jit(solution)/shard_map/ppermute | solution.py:210
  38.4 1.0 %collective-permute-done.15.refs_3_ = bf16[512,128]{1,0:T(8,128)(2,1)S(1)} collective-permute-done((bf16[512,128]{1,0:T(8,128)(2,1)S(1)}, bf16[512,128]{1,0:T(8,128)(2,1)S(1)}, u32[]{:S(2)}, u32[]{:S(2)}) %collective-permute-start.15) | collective-permute-done | bytes 131104 | tf_op jit(solution)/shard_map/ppermute | solution.py:210
  40.0 1.1 %collective-permute-done.22.refs_5_ = bf16[512,128]{1,0:T(8,128)(2,1)S(1)} collective-permute-done((bf16[512,128]{1,0:T(8,128)(2,1)S(1)}, bf16[512,128]{1,0:T(8,128)(2,1)S(1)}, u32[]{:S(2)}, u32[]{:S(2)}) %collective-permute-start.22) | collective-permute-done | bytes 131104 | tf_op jit(solution)/shard_map/ppermute | solution.py:210
  41.2 1.5 %collective-permute-start.23 = (bf16[512,256]{1,0:T(8,128)(2,1)S(1)}, bf16[512,256]{1,0:T(8,128)(2,1)S(1)}, u32[]{:S(2)}, u32[]{:S(2)}) collective-permute-start(bf16[512,256]{1,0:T(8,128)(2,1)S(1)} %get-tuple-element.97.top), channel_id=1, source_target_pairs={{0,16},{8,24},{16,0},{24,8},{1,17},{9,25},{17,1},{25,9},{2,18},{10... | collective-permute-start | bytes 786440 | tf_op jit(solution)/shard_map/ppermute | solution.py:210
  43.6 2.5 %collective-permute-start.18 = (bf16[512,128]{1,0:T(8,128)(2,1)S(1)}, bf16[512,128]{1,0:T(8,128)(2,1)S(1)}, u32[]{:S(2)}, u32[]{:S(2)}) collective-permute-start(bf16[512,128]{1,0:T(8,128)(2,1)S(1)} %get-tuple-element.85), channel_id=1, source_target_pairs={{0,4},{1,5},{2,6},{3,7},{4,0},{5,1},{6,2},{7,3},{8,12},{9,13},{10,... | collective-permute-start | bytes 393224 | tf_op jit(solution)/shard_map/ppermute | solution.py:210
  46.1 1.3 %collective-permute-start.19 = (bf16[512,128]{1,0:T(8,128)(2,1)S(1)}, bf16[512,128]{1,0:T(8,128)(2,1)S(1)}, u32[]{:S(2)}, u32[]{:S(2)}) collective-permute-start(bf16[512,128]{1,0:T(8,128)(2,1)S(1)} %get-tuple-element.86), channel_id=1, source_target_pairs={{0,6},{1,7},{2,4},{3,5},{4,2},{5,3},{6,0},{7,1},{8,14},{9,15},{10,... | collective-permute-start | bytes 393224 | tf_op jit(solution)/shard_map/ppermute | solution.py:210
  47.9 1.0 %collective-permute-done.23.top_2 = bf16[512,256]{1,0:T(8,128)(2,1)S(1)} collective-permute-done((bf16[512,256]{1,0:T(8,128)(2,1)S(1)}, bf16[512,256]{1,0:T(8,128)(2,1)S(1)}, u32[]{:S(2)}, u32[]{:S(2)}) %collective-permute-start.23) | collective-permute-done | bytes 262176 | tf_op jit(solution)/shard_map/ppermute | solution.py:210
  48.9 1.2 %collective-permute-done.24.bottom_2 = bf16[512,256]{1,0:T(8,128)(2,1)S(1)} collective-permute-done((bf16[512,256]{1,0:T(8,128)(2,1)S(1)}, bf16[512,256]{1,0:T(8,128)(2,1)S(1)}, u32[]{:S(2)}, u32[]{:S(2)}) %collective-permute-start.24) | collective-permute-done | bytes 262176 | tf_op jit(solution)/shard_map/ppermute | solution.py:210
  50.2 5.5 %conditional.1 = (f32[1024,128]{1,0:T(8,128)S(1)}, f32[1024,128]{1,0:T(8,128)S(1)}) conditional(s32[]{:T(128)} %bitcast, () %tuple.24, (bf16[512,128]{1,0:T(8,128)(2,1)S(1)}, bf16[512,128]{1,0:T(8,128)(2,1)S(1)}, bf16[512,256]{1,0:T(8,128)(2,1)S(1)}, bf16[512,256]{1,0:T(8,128)(2,1)S(1)}, bf16[512,256]{1,0:T(8,128)(2,1)S(1)}, ...), branch_computations={%region_0.0_spmd, %region_1.0_spmd} | conditional | bytes 3670112 | solution.py:356
  50.7 1.7 %collective-permute-start.1 = (bf16[512,128]{1,0:T(8,128)(2,1)S(1)}, bf16[512,128]{1,0:T(8,128)(2,1)S(1)}, u32[]{:S(2)}, u32[]{:S(2)}) collective-permute-start(bf16[512,128]{1,0:T(8,128)(2,1)S(1)} %get-tuple-element.13.bottom), channel_id=1, source_target_pairs={{0,16},{8,24},{16,0},{24,8},{1,17},{9,25},{17,1},{25,9},{2,18},{10... | collective-permute-start | bytes 393224 | tf_op jit(solution)/shard_map/cond/branch_1_fun/ppermute | solution.py:210
  52.4 2.8 %collective-permute-done.top_2 = bf16[512,128]{1,0:T(8,128)(2,1)S(1)} collective-permute-done((bf16[512,128]{1,0:T(8,128)(2,1)S(1)}, bf16[512,128]{1,0:T(8,128)(2,1)S(1)}, u32[]{:S(2)}, u32[]{:S(2)}) %collective-permute-start) | collective-permute-done | bytes 131104 | tf_op jit(solution)/shard_map/cond/branch_1_fun/ppermute | solution.py:210
  55.9 0.8 %shard_map.109 = bf16[512,128]{1,0:T(8,128)(2,1)} custom-call(f32[512,128]{1,0:T(8,128)S(1)} %get-tuple-element.103.refs_0_, bf16[512,128]{1,0:T(8,128)(2,1)S(1)} %collective-permute-done.18.refs_1_, bf16[512,128]{1,0:T(8,128)(2,1)S(1)} %collective-permute-done.19.refs_2_, bf16[512,128]{1,0:T(8,128)(2,1)S(1)} %collective-permute-done.20.refs_3_), custom_call_target="tpu_custom_call" | custom-call | bytes 786432 | tf_op jit(solution)/shard_map/pallas_call | solution.py:28
  (55 shorter events, 7.0 us)
Async XLA Ops:
  0.6 10.7 %collective-permute-start.2 = (bf16[512,128]{1,0:T(8,128)(2,1)}, bf16[512,128]{1,0:T(8,128)(2,1)S(1)}, u32[]{:S(2)}, u32[]{:S(2)}) collective-permute-start(bf16[512,128]{1,0:T(8,128)(2,1)} %feats.1), channel_id=1, source_target_pairs={{0,4},{1,5},{2,6},{3,7},{4,0},{5,1},{6,2},{7,3},{8,12},{9,13},{10,... | collective-permute-start | bytes 393224 | tf_op jit(solution)/shard_map/ppermute | solution.py:210
  4.7 6.8 %collective-permute-start.3 = (bf16[512,128]{1,0:T(8,128)(2,1)}, bf16[512,128]{1,0:T(8,128)(2,1)S(1)}, u32[]{:S(2)}, u32[]{:S(2)}) collective-permute-start(bf16[512,128]{1,0:T(8,128)(2,1)} %feats.1), channel_id=1, source_target_pairs={{0,2},{1,3},{2,0},{3,1},{4,6},{5,7},{6,4},{7,5},{8,10},{9,11},{10,... | collective-permute-start | bytes 393224 | tf_op jit(solution)/shard_map/ppermute | solution.py:210
  6.3 5.3 %collective-permute-start.4 = (bf16[512,128]{1,0:T(8,128)(2,1)}, bf16[512,128]{1,0:T(8,128)(2,1)S(1)}, u32[]{:S(2)}, u32[]{:S(2)}) collective-permute-start(bf16[512,128]{1,0:T(8,128)(2,1)} %feats.1), channel_id=1, source_target_pairs={{0,1},{1,0},{2,3},{3,2},{4,5},{5,4},{6,7},{7,6},{8,9},{9,8},{10,11... | collective-permute-start | bytes 393224 | tf_op jit(solution)/shard_map/ppermute | solution.py:210
  6.3 1.0 %copy-start.1 = (bf16[1024,128]{1,0:T(8,128)(2,1)S(1)}, bf16[1024,128]{1,0:T(8,128)(2,1)}, u32[]{:S(2)}) copy-start(bf16[1024,128]{1,0:T(8,128)(2,1)} %weight.1) | copy-start | bytes 786436
  9.1 12.8 %copy-start.5 = (s32[80]{0:T(128)S(1)}, s32[80]{0:T(128)}, u32[]{:S(2)}) copy-start(s32[80]{0:T(128)} %all_cols.1) | copy-start | bytes 964
  9.1 12.8 %copy-start.6 = (s32[4]{0:T(128)S(1)}, s32[4]{0:T(128)}, u32[]{:S(2)}) copy-start(s32[4]{0:T(128)} %all_counts.1) | copy-start | bytes 52
  11.6 5.0 %collective-permute-start.6 = (bf16[512,128]{1,0:T(8,128)(2,1)S(1)}, bf16[512,128]{1,0:T(8,128)(2,1)S(1)}, u32[]{:S(2)}, u32[]{:S(2)}) collective-permute-start(bf16[512,128]{1,0:T(8,128)(2,1)S(1)} %collective-permute-done.2.refs_4_), channel_id=1, source_target_pairs={{0,2},{1,3},{2,0},{3,1},{4,6},{5,7},{6,4},{7,5},{8,10},{9,11},{10,... | collective-permute-start | bytes 393224 | tf_op jit(solution)/shard_map/ppermute | solution.py:210
  13.0 3.5 %collective-permute-start.7 = (bf16[512,128]{1,0:T(8,128)(2,1)S(1)}, bf16[512,128]{1,0:T(8,128)(2,1)S(1)}, u32[]{:S(2)}, u32[]{:S(2)}) collective-permute-start(bf16[512,128]{1,0:T(8,128)(2,1)S(1)} %collective-permute-done.2.refs_4_), channel_id=1, source_target_pairs={{0,1},{1,0},{2,3},{3,2},{4,5},{5,4},{6,7},{7,6},{8,9},{9,8},{10,11... | collective-permute-start | bytes 393224 | tf_op jit(solution)/shard_map/ppermute | solution.py:210
  13.0 3.5 %collective-permute-start.8 = (bf16[512,128]{1,0:T(8,128)(2,1)S(1)}, bf16[512,128]{1,0:T(8,128)(2,1)S(1)}, u32[]{:S(2)}, u32[]{:S(2)}) collective-permute-start(bf16[512,128]{1,0:T(8,128)(2,1)S(1)} %collective-permute-done.3.refs_2_), channel_id=1, source_target_pairs={{0,1},{1,0},{2,3},{3,2},{4,5},{5,4},{6,7},{7,6},{8,9},{9,8},{10,11... | collective-permute-start | bytes 393224 | tf_op jit(solution)/shard_map/ppermute | solution.py:210
  16.5 1.4 %collective-permute-start.9 = (bf16[512,128]{1,0:T(8,128)(2,1)S(1)}, bf16[512,128]{1,0:T(8,128)(2,1)S(1)}, u32[]{:S(2)}, u32[]{:S(2)}) collective-permute-start(bf16[512,128]{1,0:T(8,128)(2,1)S(1)} %collective-permute-done.6.refs_6_), channel_id=1, source_target_pairs={{0,1},{1,0},{2,3},{3,2},{4,5},{5,4},{6,7},{7,6},{8,9},{9,8},{10,11... | collective-permute-start | bytes 393224 | tf_op jit(solution)/shard_map/ppermute | solution.py:210
  16.5 10.3 %collective-permute-start.5 = (bf16[2,512,128]{2,1,0:T(8,128)(2,1)S(1)}, bf16[2,512,128]{2,1,0:T(8,128)(2,1)S(1)}, u32[]{:S(2)}, u32[]{:S(2)}) collective-permute-start(bf16[2,512,128]{2,1,0:T(8,128)(2,1)S(1)} %get-tuple-element.67), channel_id=1, source_target_pairs={{0,1},{1,0},{2,3},{3,2},{4,5},{5,4},{6,7},{7,6},{8,9},{9,8},{10,11... | collective-permute-start | bytes 786440 | tf_op jit(solution)/shard_map/ppermute | solution.py:210
  18.3 9.3 %collective-permute-start.10 = (bf16[512,128]{1,0:T(8,128)(2,1)S(1)}, bf16[512,128]{1,0:T(8,128)(2,1)S(1)}, u32[]{:S(2)}, u32[]{:S(2)}) collective-permute-start(bf16[512,128]{1,0:T(8,128)(2,1)S(1)} %get-tuple-element.77.hidden), channel_id=1, source_target_pairs={{0,8},{8,0},{16,24},{24,16},{1,9},{9,1},{17,25},{25,17},{2,10},{10... | collective-permute-start | bytes 393224 | tf_op jit(solution)/shard_map/ppermute | solution.py:210
  19.9 8.1 %collective-permute-start.11 = (bf16[512,128]{1,0:T(8,128)(2,1)S(1)}, bf16[512,128]{1,0:T(8,128)(2,1)S(1)}, u32[]{:S(2)}, u32[]{:S(2)}) collective-permute-start(bf16[512,128]{1,0:T(8,128)(2,1)S(1)} %get-tuple-element.77.hidden), channel_id=1, source_target_pairs={{0,16},{8,24},{16,0},{24,8},{1,17},{9,25},{17,1},{25,9},{2,18},{10... | collective-permute-start | bytes 393224 | tf_op jit(solution)/shard_map/ppermute | solution.py:210
  21.5 6.6 %collective-permute-start.12 = (bf16[512,128]{1,0:T(8,128)(2,1)S(1)}, bf16[512,128]{1,0:T(8,128)(2,1)S(1)}, u32[]{:S(2)}, u32[]{:S(2)}) collective-permute-start(bf16[512,128]{1,0:T(8,128)(2,1)S(1)} %get-tuple-element.77.hidden), channel_id=1, source_target_pairs={{0,24},{8,16},{16,8},{24,0},{1,25},{9,17},{17,9},{25,1},{2,26},{10... | collective-permute-start | bytes 393224 | tf_op jit(solution)/shard_map/ppermute | solution.py:210
  21.9 1.7 %copy-start = (bf16[80,128,128]{2,1,0:T(8,128)(2,1)S(1)}, bf16[80,128,128]{2,1,0:T(8,128)(2,1)}, u32[]{:S(2)}) copy-start(bf16[80,128,128]{2,1,0:T(8,128)(2,1)} %vals.1) | copy-start | bytes 7864324
  27.0 1.0 %copy-start.4 = (bf16[512,128]{1,0:T(8,128)(2,1)S(1)}, bf16[512,128]{1,0:T(8,128)(2,1)}, u32[]{:S(2)}) copy-start(bf16[512,128]{1,0:T(8,128)(2,1)} %refs_6_.1) | copy-start | bytes 393220
  29.2 7.6 %collective-permute-start.13 = (bf16[512,128]{1,0:T(8,128)(2,1)S(1)}, bf16[512,128]{1,0:T(8,128)(2,1)S(1)}, u32[]{:S(2)}, u32[]{:S(2)}) collective-permute-start(bf16[512,128]{1,0:T(8,128)(2,1)S(1)} %get-tuple-element.80), channel_id=1, source_target_pairs={{0,8},{8,0},{16,24},{24,16},{1,9},{9,1},{17,25},{25,17},{2,10},{10... | collective-permute-start | bytes 393224 | tf_op jit(solution)/shard_map/ppermute | solution.py:210
  30.5 8.0 %collective-permute-start.14 = (bf16[512,128]{1,0:T(8,128)(2,1)S(1)}, bf16[512,128]{1,0:T(8,128)(2,1)S(1)}, u32[]{:S(2)}, u32[]{:S(2)}) collective-permute-start(bf16[512,128]{1,0:T(8,128)(2,1)S(1)} %get-tuple-element.81), channel_id=1, source_target_pairs={{0,16},{8,24},{16,0},{24,8},{1,17},{9,25},{17,1},{25,9},{2,18},{10... | collective-permute-start | bytes 393224 | tf_op jit(solution)/shard_map/ppermute | solution.py:210
  32.5 6.9 %collective-permute-start.15 = (bf16[512,128]{1,0:T(8,128)(2,1)S(1)}, bf16[512,128]{1,0:T(8,128)(2,1)S(1)}, u32[]{:S(2)}, u32[]{:S(2)}) collective-permute-start(bf16[512,128]{1,0:T(8,128)(2,1)S(1)} %get-tuple-element.82), channel_id=1, source_target_pairs={{0,24},{8,16},{16,8},{24,0},{1,25},{9,17},{17,9},{25,1},{2,26},{10... | collective-permute-start | bytes 393224 | tf_op jit(solution)/shard_map/ppermute | solution.py:210
  33.1 6.8 %collective-permute-start.21 = (bf16[512,128]{1,0:T(8,128)(2,1)S(1)}, bf16[512,128]{1,0:T(8,128)(2,1)S(1)}, u32[]{:S(2)}, u32[]{:S(2)}) collective-permute-start(bf16[512,128]{1,0:T(8,128)(2,1)S(1)} %get-tuple-element.91.refs_2_), channel_id=1, source_target_pairs={{0,8},{8,0},{16,24},{24,16},{1,9},{9,1},{17,25},{25,17},{2,10},{10... | collective-permute-start | bytes 393224 | tf_op jit(solution)/shard_map/ppermute | solution.py:210
  34.4 6.6 %collective-permute-start.22 = (bf16[512,128]{1,0:T(8,128)(2,1)S(1)}, bf16[512,128]{1,0:T(8,128)(2,1)S(1)}, u32[]{:S(2)}, u32[]{:S(2)}) collective-permute-start(bf16[512,128]{1,0:T(8,128)(2,1)S(1)} %get-tuple-element.92.refs_3_), channel_id=1, source_target_pairs={{0,16},{8,24},{16,0},{24,8},{1,17},{9,25},{17,1},{25,9},{2,18},{10... | collective-permute-start | bytes 393224 | tf_op jit(solution)/shard_map/ppermute | solution.py:210
  36.8 6.4 %collective-permute-start.17 = (bf16[512,128]{1,0:T(8,128)(2,1)S(1)}, bf16[512,128]{1,0:T(8,128)(2,1)S(1)}, u32[]{:S(2)}, u32[]{:S(2)}) collective-permute-start(bf16[512,128]{1,0:T(8,128)(2,1)S(1)} %get-tuple-element.79.grad_pre.pre.grads), channel_id=1, source_target_pairs={{0,1},{1,0},{2,3},{3,2},{4,5},{5,4},{6,7},{7,6},{8,9},{9,8},{10,11... | collective-permute-start | bytes 393224 | tf_op jit(solution)/shard_map/ppermute | solution.py:210
  39.5 3.7 %collective-permute-start.16 = (bf16[512,128]{1,0:T(8,128)(2,1)S(1)}, bf16[512,128]{1,0:T(8,128)(2,1)S(1)}, u32[]{:S(2)}, u32[]{:S(2)}) collective-permute-start(bf16[512,128]{1,0:T(8,128)(2,1)S(1)} %shard_map.103.hidden.grads), channel_id=1, source_target_pairs={{0,1},{1,0},{2,3},{3,2},{4,5},{5,4},{6,7},{7,6},{8,9},{9,8},{10,11... | collective-permute-start | bytes 393224 | tf_op jit(solution)/shard_map/ppermute | solution.py:210
  41.2 7.7 %collective-permute-start.23 = (bf16[512,256]{1,0:T(8,128)(2,1)S(1)}, bf16[512,256]{1,0:T(8,128)(2,1)S(1)}, u32[]{:S(2)}, u32[]{:S(2)}) collective-permute-start(bf16[512,256]{1,0:T(8,128)(2,1)S(1)} %get-tuple-element.97.top), channel_id=1, source_target_pairs={{0,16},{8,24},{16,0},{24,8},{1,17},{9,25},{17,1},{25,9},{2,18},{10... | collective-permute-start | bytes 786440 | tf_op jit(solution)/shard_map/ppermute | solution.py:210
  42.7 7.4 %collective-permute-start.24 = (bf16[512,256]{1,0:T(8,128)(2,1)S(1)}, bf16[512,256]{1,0:T(8,128)(2,1)S(1)}, u32[]{:S(2)}, u32[]{:S(2)}) collective-permute-start(bf16[512,256]{1,0:T(8,128)(2,1)S(1)} %get-tuple-element.98.bottom), channel_id=1, source_target_pairs={{0,8},{8,0},{16,24},{24,16},{1,9},{9,1},{17,25},{25,17},{2,10},{10... | collective-permute-start | bytes 786440 | tf_op jit(solution)/shard_map/ppermute | solution.py:210
  43.6 12.1 %collective-permute-start.18 = (bf16[512,128]{1,0:T(8,128)(2,1)S(1)}, bf16[512,128]{1,0:T(8,128)(2,1)S(1)}, u32[]{:S(2)}, u32[]{:S(2)}) collective-permute-start(bf16[512,128]{1,0:T(8,128)(2,1)S(1)} %get-tuple-element.85), channel_id=1, source_target_pairs={{0,4},{1,5},{2,6},{3,7},{4,0},{5,1},{6,2},{7,3},{8,12},{9,13},{10,... | collective-permute-start | bytes 393224 | tf_op jit(solution)/shard_map/ppermute | solution.py:210
  46.1 9.6 %collective-permute-start.19 = (bf16[512,128]{1,0:T(8,128)(2,1)S(1)}, bf16[512,128]{1,0:T(8,128)(2,1)S(1)}, u32[]{:S(2)}, u32[]{:S(2)}) collective-permute-start(bf16[512,128]{1,0:T(8,128)(2,1)S(1)} %get-tuple-element.86), channel_id=1, source_target_pairs={{0,6},{1,7},{2,4},{3,5},{4,2},{5,3},{6,0},{7,1},{8,14},{9,15},{10,... | collective-permute-start | bytes 393224 | tf_op jit(solution)/shard_map/ppermute | solution.py:210
  47.4 8.4 %collective-permute-start.20 = (bf16[512,128]{1,0:T(8,128)(2,1)S(1)}, bf16[512,128]{1,0:T(8,128)(2,1)S(1)}, u32[]{:S(2)}, u32[]{:S(2)}) collective-permute-start(bf16[512,128]{1,0:T(8,128)(2,1)S(1)} %get-tuple-element.87), channel_id=1, source_target_pairs={{0,2},{1,3},{2,0},{3,1},{4,6},{5,7},{6,4},{7,5},{8,10},{9,11},{10,... | collective-permute-start | bytes 393224 | tf_op jit(solution)/shard_map/ppermute | solution.py:210
  50.2 5.0 %collective-permute-start = (bf16[512,128]{1,0:T(8,128)(2,1)S(1)}, bf16[512,128]{1,0:T(8,128)(2,1)S(1)}, u32[]{:S(2)}, u32[]{:S(2)}) collective-permute-start(bf16[512,128]{1,0:T(8,128)(2,1)S(1)} %get-tuple-element.12.top), channel_id=1, source_target_pairs={{0,8},{8,0},{16,24},{24,16},{1,9},{9,1},{17,25},{25,17},{2,10},{10... | collective-permute-start | bytes 393224 | tf_op jit(solution)/shard_map/cond/branch_1_fun/ppermute | solution.py:210
  50.7 5.0 %collective-permute-start.1 = (bf16[512,128]{1,0:T(8,128)(2,1)S(1)}, bf16[512,128]{1,0:T(8,128)(2,1)S(1)}, u32[]{:S(2)}, u32[]{:S(2)}) collective-permute-start(bf16[512,128]{1,0:T(8,128)(2,1)S(1)} %get-tuple-element.13.bottom), channel_id=1, source_target_pairs={{0,16},{8,24},{16,0},{24,8},{1,17},{9,25},{17,1},{25,9},{2,18},{10... | collective-permute-start | bytes 393224 | tf_op jit(solution)/shard_map/cond/branch_1_fun/ppermute | solution.py:210
  55.7 1.0 %copy-start.7 = (f32[1024,128]{1,0:T(8,128)}, f32[1024,128]{1,0:T(8,128)S(1)}, u32[]{:S(2)}) copy-start(f32[1024,128]{1,0:T(8,128)S(1)} %get-tuple-element.63) | copy-start | bytes 1572868
  55.7 1.0 %copy-start.8 = (f32[1024,128]{1,0:T(8,128)}, f32[1024,128]{1,0:T(8,128)S(1)}, u32[]{:S(2)}) copy-start(f32[1024,128]{1,0:T(8,128)S(1)} %get-tuple-element.64) | copy-start | bytes 1572868
  (2 other events, 1.9 us)

commit v7 on v6

--- a/solution.py
+++ b/solution.py
@@ -109,16 +109,23 @@
         out[rows, :] = pieces[m][...].T
 
 
-def begin_kernel(adj, hidden, own, pre):
+def begin_kernel(adj, hidden, hidden_1, own, pre):
     rows = own.shape[0]
-    place = pl.ds(pl.multiple_of(lax.axis_index("rows") * rows, rows), rows)
-    pre[...] = own[...] + dot(adj[:, place], hidden[...])
+    me = lax.axis_index("rows")
+    half = rows // 2
+    for at in (0, half):
+        part = slice(at, at + half)
+        total = own[part, :]
+        for j, block in enumerate((hidden, hidden_1)):
+            place = pl.ds(pl.multiple_of((me ^ j) * rows, rows), rows)
+            total = total + dot(adj[part, place], block[...])
+        pre[part, :] = total
 
 
 def aggregate_kernel(nr, *refs):
-    hidden = refs[: nr - 1]
-    adj, adj_t, begun, grad_out, grad_pre = refs[nr - 1 : nr + 4]
-    sent = refs[nr + 4 :]
+    hidden = refs[: nr - 2]
+    adj, adj_t, begun, grad_out, grad_pre = refs[nr - 2 : nr + 3]
+    sent = refs[nr + 3 :]
     me = lax.axis_index("rows")
     rows = begun.shape[0]
     places = [pl.ds(pl.multiple_of((me ^ j) * rows, rows), rows) for j in range(1, nr)]
@@ -126,13 +133,15 @@
     for at in (0, half):
         part = slice(at, at + half)
         pre = begun[part, :]
-        for j in range(nr - 1):
-            pre = pre + dot(adj[part, places[j]], hidden[j][...])
+        for j in range(1, nr - 1):
+            pre = pre + dot(adj[part, places[j]], hidden[j - 1][...])
         sig = jax.nn.sigmoid(pre)
         grad = grad_out[part, :].astype(F32) * sig * (1.0 + pre * (1.0 - sig))
         grad_pre[part, :] = grad.astype(BF)
     for j in range(nr - 1):
-        sent[j][...] = dot(adj_t[places[j], :], grad_pre[...]).astype(BF)
+        for at in (0, half):
+            place = pl.ds(pl.multiple_of((me ^ (j + 1)) * rows + at, half), half)
+            sent[j][at : at + half, :] = dot(adj_t[place, :], grad_pre[...]).astype(BF)
 
 
 def keep_kernel(adj_t, grad_pre, kept):
@@ -176,13 +185,10 @@
         out[place, :] = dot(feats_t[at : at + step, :], grads[...]).astype(BF)
 
 
-def join_kernel(*refs):
-    terms, outs = refs[:6], refs[6:]
-    for half, out in enumerate(outs):
-        width = out.shape[1] // 2
-        out[:, :width] = terms[half][...]
-        root = terms[half + 2][...].astype(F32) + terms[half + 4][...].astype(F32)
-        out[:, width:] = root.astype(BF)
+def join_kernel(weight, root, root_2, out):
+    width = weight.shape[1]
+    out[:, :width] = weight[...]
+    out[:, width:] = (root[...].astype(F32) + root_2[...].astype(F32)).astype(BF)
 
 
 def pair_sum_kernel(top, top_2, bottom, bottom_2, top_sum, bottom_sum):
@@ -279,15 +285,15 @@
     (begun,) = call(
         begin_kernel,
         [sds((rows, width), F32)],
-        [VMEM] * 3,
-        (adj, hidden, own),
+        [VMEM] * 4,
+        (adj, hidden, gathered[1], own),
         flops=2 * rows * rows * width,
     )
     grad_pre, *sent = call(
         functools.partial(aggregate_kernel, nr),
         [sds((rows, width), BF)] * nr,
-        [VMEM] * (nr + 3),
-        (*gathered[1:], adj, adj_t, begun, grad_out),
+        [VMEM] * (nr + 2),
+        (*gathered[2:], adj, adj_t, begun, grad_out),
         flops=4 * rows * nodes * width,
         limit=max(32 * 1024 * 1024, 10 * rows * nodes),
     )
@@ -326,13 +332,15 @@
         flops=2 * rows * depth * width,
     )
     steps = [1 << bit for bit in range(nr.bit_length() - 1)]
-    first, *between = zip(steps, reversed(steps))
+    first, *between = zip(reversed(steps), steps)
     final = between[-1]
     root_got = [swap(part, "rows", mask) for part, mask in zip(root_part, first)]
-    *weight_part, root_got[0], root_got[1] = lax.optimization_barrier((*weight_part, *root_got))
     sums_f = [parts[0]] + [swap(parts[k], "feat", 2 * k) for k in ranks]
     joined = [sds((depth // 2, 2 * width), BF)] * 2
-    grads = call(join_kernel, joined, [VMEM] * 6, (*weight_part, *root_part, *root_got))
+    grads = [
+        call(join_kernel, joined[:1], [VMEM] * 3, arrays)[0]
+        for arrays in zip(weight_part, root_part, root_got)
+    ]
     for masks in between:
         got = [swap(part, "rows", mask) for part, mask in zip(grads, masks)]
         pairs = grads[0], got[0], grads[1], got[1]

time: 57 us -> 57.1 us (level)
  starting transfers between devices: 27.1 us -> 28.1 us
  waiting for transfers between devices: 15.7 us -> 14.7 us
    ppermute x25, waiting for transfers between devices: 15.7 us -> 14.7 us  [swap(): lax.ppermute(array, axis, [(i, i ^ mask) for i in range(lax.axis_size(axi...]
    ppermute x25, starting transfers between devices: 27.1 us -> 28.1 us  [swap(): lax.ppermute(array, axis, [(i, i ^ mask) for i in range(lax.axis_size(axi...]
    pallas_call x18 -> x19, Pallas kernels: 8.4 us -> 8.39 us  [call(): pl.pallas_call(body, out_shape=outs, in_specs=specs, out_specs=[VMEM] * l...]
  transfers between devices with their start and end apart: 25 -> 25, of which waited for: 13 -> 11; matrix products, arithmetic and copies ran while one was open for 0% -> 0% of each run, Pallas kernels for 11% -> 12%
where the time goes in v7:
time: 57.1 us; the launch traced here: 56.8 us
  starting transfers between devices  28.1 us (49%)
  waiting for transfers between devices  14.7 us (26%)
  Pallas kernels  8.39 us (15%)
  local copies, waits for them, and re-layouts  4.67 us (8%)
  between operations  0.89 us (2%)
    ppermute x25, starting transfers between devices, swap(): lax.ppermute(array, axis, [(i, i ^ mask) for i in range(lax.axis_size(axi...  28.1 us
    ppermute x25, waiting for transfers between devices, swap(): lax.ppermute(array, axis, [(i, i ^ mask) for i in range(lax.axis_size(axi...  14.7 us
    pallas_call x19, Pallas kernels, call(): pl.pallas_call(body, out_shape=outs, in_specs=specs, out_specs=[VMEM] * l...  8.39 us
    unnamed x18, local copies, waits for them, and re-layouts  4.67 us
  transfers between devices with their start and end apart: 25, of which 11 were waited for; matrix products, arithmetic and copies ran while one was open for 0% of the time, Pallas kernels for 12%

profile of v7, /device:TPU:0, one launch (start us, length us, event | category | flops | bytes accessed | tf_op | source)
XLA Modules:
  0.0 56.8 jit_solution(5518104465582906060)
XLA Ops:
  0.6 4.1 %collective-permute-start.2 = (bf16[512,128]{1,0:T(8,128)(2,1)}, bf16[512,128]{1,0:T(8,128)(2,1)S(1)}, u32[]{:S(2)}, u32[]{:S(2)}) collective-permute-start(bf16[512,128]{1,0:T(8,128)(2,1)} %feats.1), channel_id=1, source_target_pairs={{0,4},{1,5},{2,6},{3,7},{4,0},{5,1},{6,2},{7,3},{8,12},{9,13},{10,... | collective-permute-start | bytes 393224 | tf_op jit(solution)/shard_map/ppermute | solution.py:216
  4.7 1.6 %collective-permute-start.3 = (bf16[512,128]{1,0:T(8,128)(2,1)}, bf16[512,128]{1,0:T(8,128)(2,1)S(1)}, u32[]{:S(2)}, u32[]{:S(2)}) collective-permute-start(bf16[512,128]{1,0:T(8,128)(2,1)} %feats.1), channel_id=1, source_target_pairs={{0,2},{1,3},{2,0},{3,1},{4,6},{5,7},{6,4},{7,5},{8,10},{9,11},{10,... | collective-permute-start | bytes 393224 | tf_op jit(solution)/shard_map/ppermute | solution.py:216
  6.3 0.9 %copy-done.1 = bf16[1024,128]{1,0:T(8,128)(2,1)S(1)} copy-done((bf16[1024,128]{1,0:T(8,128)(2,1)S(1)}, bf16[1024,128]{1,0:T(8,128)(2,1)}, u32[]{:S(2)}) %copy-start.1) | copy-done | bytes 262168
  7.3 0.9 %copy-done.2 = bf16[1024,128]{1,0:T(8,128)(2,1)S(1)} copy-done((bf16[1024,128]{1,0:T(8,128)(2,1)S(1)}, bf16[1024,128]{1,0:T(8,128)(2,1)}, u32[]{:S(2)}) %copy-start.2) | copy-done | bytes 262168
  8.2 0.9 %copy-done.3 = bf16[512,128]{1,0:T(8,128)(2,1)S(1)} copy-done((bf16[512,128]{1,0:T(8,128)(2,1)S(1)}, bf16[512,128]{1,0:T(8,128)(2,1)}, u32[]{:S(2)}) %copy-start.3) | copy-done | bytes 131096
  9.2 2.1 %collective-permute-done.2.refs_4_ = bf16[512,128]{1,0:T(8,128)(2,1)S(1)} collective-permute-done((bf16[512,128]{1,0:T(8,128)(2,1)}, bf16[512,128]{1,0:T(8,128)(2,1)S(1)}, u32[]{:S(2)}, u32[]{:S(2)}) %collective-permute-start.2) | collective-permute-done | bytes 131104 | tf_op jit(solution)/shard_map/ppermute | solution.py:216
  11.6 1.4 %collective-permute-start.6 = (bf16[512,128]{1,0:T(8,128)(2,1)S(1)}, bf16[512,128]{1,0:T(8,128)(2,1)S(1)}, u32[]{:S(2)}, u32[]{:S(2)}) collective-permute-start(bf16[512,128]{1,0:T(8,128)(2,1)S(1)} %collective-permute-done.2.refs_4_), channel_id=1, source_target_pairs={{0,2},{1,3},{2,0},{3,1},{4,6},{5,7},{6,4},{7,5},{8,10},{9,11},{10,... | collective-permute-start | bytes 393224 | tf_op jit(solution)/shard_map/ppermute | solution.py:216
  13.5 3.0 %collective-permute-done.6.refs_6_ = bf16[512,128]{1,0:T(8,128)(2,1)S(1)} collective-permute-done((bf16[512,128]{1,0:T(8,128)(2,1)S(1)}, bf16[512,128]{1,0:T(8,128)(2,1)S(1)}, u32[]{:S(2)}, u32[]{:S(2)}) %collective-permute-start.6) | collective-permute-done | bytes 131104 | tf_op jit(solution)/shard_map/ppermute | solution.py:216
  17.1 0.8 %collective-permute-done.9.refs_7_ = bf16[512,128]{1,0:T(8,128)(2,1)S(1)} collective-permute-done((bf16[512,128]{1,0:T(8,128)(2,1)S(1)}, bf16[512,128]{1,0:T(8,128)(2,1)S(1)}, u32[]{:S(2)}, u32[]{:S(2)}) %collective-permute-start.9) | collective-permute-done | bytes 131104 | tf_op jit(solution)/shard_map/ppermute | solution.py:216
  18.3 1.6 %collective-permute-start.12 = (bf16[512,128]{1,0:T(8,128)(2,1)S(1)}, bf16[512,128]{1,0:T(8,128)(2,1)S(1)}, u32[]{:S(2)}, u32[]{:S(2)}) collective-permute-start(bf16[512,128]{1,0:T(8,128)(2,1)S(1)} %get-tuple-element.71.hidden), channel_id=1, source_target_pairs={{0,8},{8,0},{16,24},{24,16},{1,9},{9,1},{17,25},{25,17},{2,10},{10... | collective-permute-start | bytes 393224 | tf_op jit(solution)/shard_map/ppermute | solution.py:216
  19.9 1.5 %collective-permute-start.10 = (bf16[512,128]{1,0:T(8,128)(2,1)S(1)}, bf16[512,128]{1,0:T(8,128)(2,1)S(1)}, u32[]{:S(2)}, u32[]{:S(2)}) collective-permute-start(bf16[512,128]{1,0:T(8,128)(2,1)S(1)} %get-tuple-element.71.hidden), channel_id=1, source_target_pairs={{0,16},{8,24},{16,0},{24,8},{1,17},{9,25},{17,1},{25,9},{2,18},{10... | collective-permute-start | bytes 393224 | tf_op jit(solution)/shard_map/ppermute | solution.py:216
  21.9 1.7 %copy-done = bf16[80,128,128]{2,1,0:T(8,128)(2,1)S(1)} copy-done((bf16[80,128,128]{2,1,0:T(8,128)(2,1)S(1)}, bf16[80,128,128]{2,1,0:T(8,128)(2,1)}, u32[]{:S(2)}) %copy-start) | copy-done | bytes 2621464
  23.6 1.7 %shard_map.94.adj.refs_2_ = bf16[512,2048]{1,0:T(8,128)(2,1)S(1)} custom-call(s32[4]{0:T(128)S(1)} %copy-done.6, s32[80]{0:T(128)S(1)} %copy-done.5, bf16[80,128,128]{2,1,0:T(8,128)(2,1)S(1)} %copy-done), custom_call_target="tpu_custom_call" | custom-call | flops 4194304 | bytes 4718928 | tf_op jit(solution)/shard_map/pallas_call | solution.py:28
  25.3 1.4 %shard_map.95.refs_3_.adj_t = bf16[2048,512]{1,0:T(8,128)(2,1)S(1)} custom-call(bf16[512,2048]{1,0:T(8,128)(2,1)S(1)} %shard_map.94.adj.refs_2_), custom_call_target="tpu_custom_call" | custom-call | bytes 4194304 | tf_op jit(solution)/shard_map/pallas_call | solution.py:28
  28.0 1.0 %shard_map.101 = (bf16[512,128]{1,0:T(8,128)(2,1)S(1)}, bf16[512,128]{1,0:T(8,128)(2,1)S(1)}, bf16[512,128]{1,0:T(8,128)(2,1)S(1)}, bf16[512,128]{1,0:T(8,128)(2,1)S(1)}) custom-call(bf16[512,128]{1,0:T(8,128)(2,1)S(1)} %collective-permute-done.10.refs_0_, bf16[512,128]{1,0:T(8,128)(2,1)S(1)} %collective-permute-done.11.refs_1_, ...), custom_call_target="tpu_custom_call" | custom-call | flops 536870912 | bytes 5373952 | tf_op jit(solution)/shard_map/pallas_call | solution.py:28
  29.0 1.3 %collective-permute-start.13 = (bf16[512,128]{1,0:T(8,128)(2,1)S(1)}, bf16[512,128]{1,0:T(8,128)(2,1)S(1)}, u32[]{:S(2)}, u32[]{:S(2)}) collective-permute-start(bf16[512,128]{1,0:T(8,128)(2,1)S(1)} %get-tuple-element.74), channel_id=1, source_target_pairs={{0,8},{8,0},{16,24},{24,16},{1,9},{9,1},{17,25},{25,17},{2,10},{10... | collective-permute-start | bytes 393224 | tf_op jit(solution)/shard_map/ppermute | solution.py:216
  30.3 2.0 %collective-permute-start.14 = (bf16[512,128]{1,0:T(8,128)(2,1)S(1)}, bf16[512,128]{1,0:T(8,128)(2,1)S(1)}, u32[]{:S(2)}, u32[]{:S(2)}) collective-permute-start(bf16[512,128]{1,0:T(8,128)(2,1)S(1)} %get-tuple-element.75), channel_id=1, source_target_pairs={{0,16},{8,24},{16,0},{24,8},{1,17},{9,25},{17,1},{25,9},{2,18},{10... | collective-permute-start | bytes 393224 | tf_op jit(solution)/shard_map/ppermute | solution.py:216
  33.0 1.3 %collective-permute-start.23 = (bf16[512,128]{1,0:T(8,128)(2,1)S(1)}, bf16[512,128]{1,0:T(8,128)(2,1)S(1)}, u32[]{:S(2)}, u32[]{:S(2)}) collective-permute-start(bf16[512,128]{1,0:T(8,128)(2,1)S(1)} %get-tuple-element.86.root), channel_id=1, source_target_pairs={{0,8},{8,0},{16,24},{24,16},{1,9},{9,1},{17,25},{25,17},{2,10},{10... | collective-permute-start | bytes 393224 | tf_op jit(solution)/shard_map/ppermute | solution.py:216
  34.3 2.0 %collective-permute-start.21 = (bf16[512,128]{1,0:T(8,128)(2,1)S(1)}, bf16[512,128]{1,0:T(8,128)(2,1)S(1)}, u32[]{:S(2)}, u32[]{:S(2)}) collective-permute-start(bf16[512,128]{1,0:T(8,128)(2,1)S(1)} %get-tuple-element.84.root), channel_id=1, source_target_pairs={{0,16},{8,24},{16,0},{24,8},{1,17},{9,25},{17,1},{25,9},{2,18},{10... | collective-permute-start | bytes 393224 | tf_op jit(solution)/shard_map/ppermute | solution.py:216
  36.7 1.6 %collective-permute-done.14.refs_2_ = bf16[512,128]{1,0:T(8,128)(2,1)S(1)} collective-permute-done((bf16[512,128]{1,0:T(8,128)(2,1)S(1)}, bf16[512,128]{1,0:T(8,128)(2,1)S(1)}, u32[]{:S(2)}, u32[]{:S(2)}) %collective-permute-start.14) | collective-permute-done | bytes 131104 | tf_op jit(solution)/shard_map/ppermute | solution.py:216
  38.3 1.0 %collective-permute-done.15.refs_3_ = bf16[512,128]{1,0:T(8,128)(2,1)S(1)} collective-permute-done((bf16[512,128]{1,0:T(8,128)(2,1)S(1)}, bf16[512,128]{1,0:T(8,128)(2,1)S(1)}, u32[]{:S(2)}, u32[]{:S(2)}) %collective-permute-start.15) | collective-permute-done | bytes 131104 | tf_op jit(solution)/shard_map/ppermute | solution.py:216
  39.9 1.6 %collective-permute-start.24 = (bf16[512,256]{1,0:T(8,128)(2,1)S(1)}, bf16[512,256]{1,0:T(8,128)(2,1)S(1)}, u32[]{:S(2)}, u32[]{:S(2)}) collective-permute-start(bf16[512,256]{1,0:T(8,128)(2,1)S(1)} %shard_map.108.bottom), channel_id=1, source_target_pairs={{0,16},{8,24},{16,0},{24,8},{1,17},{9,25},{17,1},{25,9},{2,18},{10... | collective-permute-start | bytes 786440 | tf_op jit(solution)/shard_map/ppermute | solution.py:216
  41.6 1.4 %collective-permute-start.22 = (bf16[512,256]{1,0:T(8,128)(2,1)S(1)}, bf16[512,256]{1,0:T(8,128)(2,1)S(1)}, u32[]{:S(2)}, u32[]{:S(2)}) collective-permute-start(bf16[512,256]{1,0:T(8,128)(2,1)S(1)} %shard_map.107.top), channel_id=1, source_target_pairs={{0,8},{8,0},{16,24},{24,16},{1,9},{9,1},{17,25},{25,17},{2,10},{10... | collective-permute-start | bytes 786440 | tf_op jit(solution)/shard_map/ppermute | solution.py:216
  43.4 2.5 %collective-permute-start.18 = (bf16[512,128]{1,0:T(8,128)(2,1)S(1)}, bf16[512,128]{1,0:T(8,128)(2,1)S(1)}, u32[]{:S(2)}, u32[]{:S(2)}) collective-permute-start(bf16[512,128]{1,0:T(8,128)(2,1)S(1)} %get-tuple-element.79), channel_id=1, source_target_pairs={{0,4},{1,5},{2,6},{3,7},{4,0},{5,1},{6,2},{7,3},{8,12},{9,13},{10,... | collective-permute-start | bytes 393224 | tf_op jit(solution)/shard_map/ppermute | solution.py:216
  45.9 1.3 %collective-permute-start.19 = (bf16[512,128]{1,0:T(8,128)(2,1)S(1)}, bf16[512,128]{1,0:T(8,128)(2,1)S(1)}, u32[]{:S(2)}, u32[]{:S(2)}) collective-permute-start(bf16[512,128]{1,0:T(8,128)(2,1)S(1)} %get-tuple-element.80), channel_id=1, source_target_pairs={{0,6},{1,7},{2,4},{3,5},{4,2},{5,3},{6,0},{7,1},{8,14},{9,15},{10,... | collective-permute-start | bytes 393224 | tf_op jit(solution)/shard_map/ppermute | solution.py:216
  47.7 1.0 %collective-permute-done.24.bottom_2 = bf16[512,256]{1,0:T(8,128)(2,1)S(1)} collective-permute-done((bf16[512,256]{1,0:T(8,128)(2,1)S(1)}, bf16[512,256]{1,0:T(8,128)(2,1)S(1)}, u32[]{:S(2)}, u32[]{:S(2)}) %collective-permute-start.24) | collective-permute-done | bytes 262176 | tf_op jit(solution)/shard_map/ppermute | solution.py:216
  48.7 1.4 %collective-permute-done.22.top_2 = bf16[512,256]{1,0:T(8,128)(2,1)S(1)} collective-permute-done((bf16[512,256]{1,0:T(8,128)(2,1)S(1)}, bf16[512,256]{1,0:T(8,128)(2,1)S(1)}, u32[]{:S(2)}, u32[]{:S(2)}) %collective-permute-start.22) | collective-permute-done | bytes 262176 | tf_op jit(solution)/shard_map/ppermute | solution.py:216
  50.1 5.6 %conditional.1 = (f32[1024,128]{1,0:T(8,128)S(1)}, f32[1024,128]{1,0:T(8,128)S(1)}) conditional(s32[]{:T(128)} %bitcast, () %tuple.23, (bf16[512,128]{1,0:T(8,128)(2,1)S(1)}, bf16[512,128]{1,0:T(8,128)(2,1)S(1)}, bf16[512,256]{1,0:T(8,128)(2,1)S(1)}, bf16[512,256]{1,0:T(8,128)(2,1)S(1)}, bf16[512,256]{1,0:T(8,128)(2,1)S(1)}, ...), branch_computations={%region_0.0_spmd, %region_1.0_spmd} | conditional | bytes 3670112 | solution.py:364
  50.1 0.6 %collective-permute-start = (bf16[512,128]{1,0:T(8,128)(2,1)S(1)}, bf16[512,128]{1,0:T(8,128)(2,1)S(1)}, u32[]{:S(2)}, u32[]{:S(2)}) collective-permute-start(bf16[512,128]{1,0:T(8,128)(2,1)S(1)} %get-tuple-element.12.top), channel_id=1, source_target_pairs={{0,16},{8,24},{16,0},{24,8},{1,17},{9,25},{17,1},{25,9},{2,18},{10... | collective-permute-start | bytes 393224 | tf_op jit(solution)/shard_map/cond/branch_1_fun/ppermute | solution.py:216
  50.7 1.5 %collective-permute-start.1 = (bf16[512,128]{1,0:T(8,128)(2,1)S(1)}, bf16[512,128]{1,0:T(8,128)(2,1)S(1)}, u32[]{:S(2)}, u32[]{:S(2)}) collective-permute-start(bf16[512,128]{1,0:T(8,128)(2,1)S(1)} %get-tuple-element.13.bottom), channel_id=1, source_target_pairs={{0,8},{8,0},{16,24},{24,16},{1,9},{9,1},{17,25},{25,17},{2,10},{10... | collective-permute-start | bytes 393224 | tf_op jit(solution)/shard_map/cond/branch_1_fun/ppermute | solution.py:216
  52.3 2.8 %collective-permute-done.top_2 = bf16[512,128]{1,0:T(8,128)(2,1)S(1)} collective-permute-done((bf16[512,128]{1,0:T(8,128)(2,1)S(1)}, bf16[512,128]{1,0:T(8,128)(2,1)S(1)}, u32[]{:S(2)}, u32[]{:S(2)}) %collective-permute-start) | collective-permute-done | bytes 131104 | tf_op jit(solution)/shard_map/cond/branch_1_fun/ppermute | solution.py:216
  55.8 0.8 %shard_map.110 = bf16[512,128]{1,0:T(8,128)(2,1)} custom-call(f32[512,128]{1,0:T(8,128)S(1)} %get-tuple-element.91.refs_0_, bf16[512,128]{1,0:T(8,128)(2,1)S(1)} %collective-permute-done.18.refs_1_, bf16[512,128]{1,0:T(8,128)(2,1)S(1)} %collective-permute-done.19.refs_2_, bf16[512,128]{1,0:T(8,128)(2,1)S(1)} %collective-permute-done.20.refs_3_), custom_call_target="tpu_custom_call" | custom-call | bytes 786432 | tf_op jit(solution)/shard_map/pallas_call | solution.py:28
  (56 shorter events, 6.8 us)
Async XLA Ops:
  0.6 10.7 %collective-permute-start.2 = (bf16[512,128]{1,0:T(8,128)(2,1)}, bf16[512,128]{1,0:T(8,128)(2,1)S(1)}, u32[]{:S(2)}, u32[]{:S(2)}) collective-permute-start(bf16[512,128]{1,0:T(8,128)(2,1)} %feats.1), channel_id=1, source_target_pairs={{0,4},{1,5},{2,6},{3,7},{4,0},{5,1},{6,2},{7,3},{8,12},{9,13},{10,... | collective-permute-start | bytes 393224 | tf_op jit(solution)/shard_map/ppermute | solution.py:216
  4.7 6.8 %collective-permute-start.3 = (bf16[512,128]{1,0:T(8,128)(2,1)}, bf16[512,128]{1,0:T(8,128)(2,1)S(1)}, u32[]{:S(2)}, u32[]{:S(2)}) collective-permute-start(bf16[512,128]{1,0:T(8,128)(2,1)} %feats.1), channel_id=1, source_target_pairs={{0,2},{1,3},{2,0},{3,1},{4,6},{5,7},{6,4},{7,5},{8,10},{9,11},{10,... | collective-permute-start | bytes 393224 | tf_op jit(solution)/shard_map/ppermute | solution.py:216
  6.3 5.3 %collective-permute-start.4 = (bf16[512,128]{1,0:T(8,128)(2,1)}, bf16[512,128]{1,0:T(8,128)(2,1)S(1)}, u32[]{:S(2)}, u32[]{:S(2)}) collective-permute-start(bf16[512,128]{1,0:T(8,128)(2,1)} %feats.1), channel_id=1, source_target_pairs={{0,1},{1,0},{2,3},{3,2},{4,5},{5,4},{6,7},{7,6},{8,9},{9,8},{10,11... | collective-permute-start | bytes 393224 | tf_op jit(solution)/shard_map/ppermute | solution.py:216
  6.3 1.0 %copy-start.1 = (bf16[1024,128]{1,0:T(8,128)(2,1)S(1)}, bf16[1024,128]{1,0:T(8,128)(2,1)}, u32[]{:S(2)}) copy-start(bf16[1024,128]{1,0:T(8,128)(2,1)} %weight.1) | copy-start | bytes 786436
  7.3 0.9 %copy-start.2 = (bf16[1024,128]{1,0:T(8,128)(2,1)S(1)}, bf16[1024,128]{1,0:T(8,128)(2,1)}, u32[]{:S(2)}) copy-start(bf16[1024,128]{1,0:T(8,128)(2,1)} %root.1) | copy-start | bytes 786436
  9.1 12.8 %copy-start.5 = (s32[80]{0:T(128)S(1)}, s32[80]{0:T(128)}, u32[]{:S(2)}) copy-start(s32[80]{0:T(128)} %all_cols.1) | copy-start | bytes 964
  9.1 12.8 %copy-start.6 = (s32[4]{0:T(128)S(1)}, s32[4]{0:T(128)}, u32[]{:S(2)}) copy-start(s32[4]{0:T(128)} %all_counts.1) | copy-start | bytes 52
  11.6 5.0 %collective-permute-start.6 = (bf16[512,128]{1,0:T(8,128)(2,1)S(1)}, bf16[512,128]{1,0:T(8,128)(2,1)S(1)}, u32[]{:S(2)}, u32[]{:S(2)}) collective-permute-start(bf16[512,128]{1,0:T(8,128)(2,1)S(1)} %collective-permute-done.2.refs_4_), channel_id=1, source_target_pairs={{0,2},{1,3},{2,0},{3,1},{4,6},{5,7},{6,4},{7,5},{8,10},{9,11},{10,... | collective-permute-start | bytes 393224 | tf_op jit(solution)/shard_map/ppermute | solution.py:216
  13.0 3.5 %collective-permute-start.7 = (bf16[512,128]{1,0:T(8,128)(2,1)S(1)}, bf16[512,128]{1,0:T(8,128)(2,1)S(1)}, u32[]{:S(2)}, u32[]{:S(2)}) collective-permute-start(bf16[512,128]{1,0:T(8,128)(2,1)S(1)} %collective-permute-done.2.refs_4_), channel_id=1, source_target_pairs={{0,1},{1,0},{2,3},{3,2},{4,5},{5,4},{6,7},{7,6},{8,9},{9,8},{10,11... | collective-permute-start | bytes 393224 | tf_op jit(solution)/shard_map/ppermute | solution.py:216
  13.0 3.5 %collective-permute-start.8 = (bf16[512,128]{1,0:T(8,128)(2,1)S(1)}, bf16[512,128]{1,0:T(8,128)(2,1)S(1)}, u32[]{:S(2)}, u32[]{:S(2)}) collective-permute-start(bf16[512,128]{1,0:T(8,128)(2,1)S(1)} %collective-permute-done.3.refs_2_), channel_id=1, source_target_pairs={{0,1},{1,0},{2,3},{3,2},{4,5},{5,4},{6,7},{7,6},{8,9},{9,8},{10,11... | collective-permute-start | bytes 393224 | tf_op jit(solution)/shard_map/ppermute | solution.py:216
  16.5 1.4 %collective-permute-start.9 = (bf16[512,128]{1,0:T(8,128)(2,1)S(1)}, bf16[512,128]{1,0:T(8,128)(2,1)S(1)}, u32[]{:S(2)}, u32[]{:S(2)}) collective-permute-start(bf16[512,128]{1,0:T(8,128)(2,1)S(1)} %collective-permute-done.6.refs_6_), channel_id=1, source_target_pairs={{0,1},{1,0},{2,3},{3,2},{4,5},{5,4},{6,7},{7,6},{8,9},{9,8},{10,11... | collective-permute-start | bytes 393224 | tf_op jit(solution)/shard_map/ppermute | solution.py:216
  16.5 10.2 %collective-permute-start.5 = (bf16[2,512,128]{2,1,0:T(8,128)(2,1)S(1)}, bf16[2,512,128]{2,1,0:T(8,128)(2,1)S(1)}, u32[]{:S(2)}, u32[]{:S(2)}) collective-permute-start(bf16[2,512,128]{2,1,0:T(8,128)(2,1)S(1)} %get-tuple-element.61), channel_id=1, source_target_pairs={{0,1},{1,0},{2,3},{3,2},{4,5},{5,4},{6,7},{7,6},{8,9},{9,8},{10,11... | collective-permute-start | bytes 786440 | tf_op jit(solution)/shard_map/ppermute | solution.py:216
  18.3 9.0 %collective-permute-start.12 = (bf16[512,128]{1,0:T(8,128)(2,1)S(1)}, bf16[512,128]{1,0:T(8,128)(2,1)S(1)}, u32[]{:S(2)}, u32[]{:S(2)}) collective-permute-start(bf16[512,128]{1,0:T(8,128)(2,1)S(1)} %get-tuple-element.71.hidden), channel_id=1, source_target_pairs={{0,8},{8,0},{16,24},{24,16},{1,9},{9,1},{17,25},{25,17},{2,10},{10... | collective-permute-start | bytes 393224 | tf_op jit(solution)/shard_map/ppermute | solution.py:216
  19.9 8.1 %collective-permute-start.10 = (bf16[512,128]{1,0:T(8,128)(2,1)S(1)}, bf16[512,128]{1,0:T(8,128)(2,1)S(1)}, u32[]{:S(2)}, u32[]{:S(2)}) collective-permute-start(bf16[512,128]{1,0:T(8,128)(2,1)S(1)} %get-tuple-element.71.hidden), channel_id=1, source_target_pairs={{0,16},{8,24},{16,0},{24,8},{1,17},{9,25},{17,1},{25,9},{2,18},{10... | collective-permute-start | bytes 393224 | tf_op jit(solution)/shard_map/ppermute | solution.py:216
  21.5 6.6 %collective-permute-start.11 = (bf16[512,128]{1,0:T(8,128)(2,1)S(1)}, bf16[512,128]{1,0:T(8,128)(2,1)S(1)}, u32[]{:S(2)}, u32[]{:S(2)}) collective-permute-start(bf16[512,128]{1,0:T(8,128)(2,1)S(1)} %get-tuple-element.71.hidden), channel_id=1, source_target_pairs={{0,24},{8,16},{16,8},{24,0},{1,25},{9,17},{17,9},{25,1},{2,26},{10... | collective-permute-start | bytes 393224 | tf_op jit(solution)/shard_map/ppermute | solution.py:216
  21.9 1.7 %copy-start = (bf16[80,128,128]{2,1,0:T(8,128)(2,1)S(1)}, bf16[80,128,128]{2,1,0:T(8,128)(2,1)}, u32[]{:S(2)}) copy-start(bf16[80,128,128]{2,1,0:T(8,128)(2,1)} %vals.1) | copy-start | bytes 7864324
  27.0 1.0 %copy-start.4 = (bf16[512,128]{1,0:T(8,128)(2,1)S(1)}, bf16[512,128]{1,0:T(8,128)(2,1)}, u32[]{:S(2)}) copy-start(bf16[512,128]{1,0:T(8,128)(2,1)} %refs_5_.1) | copy-start | bytes 393220
  29.0 7.6 %collective-permute-start.13 = (bf16[512,128]{1,0:T(8,128)(2,1)S(1)}, bf16[512,128]{1,0:T(8,128)(2,1)S(1)}, u32[]{:S(2)}, u32[]{:S(2)}) collective-permute-start(bf16[512,128]{1,0:T(8,128)(2,1)S(1)} %get-tuple-element.74), channel_id=1, source_target_pairs={{0,8},{8,0},{16,24},{24,16},{1,9},{9,1},{17,25},{25,17},{2,10},{10... | collective-permute-start | bytes 393224 | tf_op jit(solution)/shard_map/ppermute | solution.py:216
  30.3 7.9 %collective-permute-start.14 = (bf16[512,128]{1,0:T(8,128)(2,1)S(1)}, bf16[512,128]{1,0:T(8,128)(2,1)S(1)}, u32[]{:S(2)}, u32[]{:S(2)}) collective-permute-start(bf16[512,128]{1,0:T(8,128)(2,1)S(1)} %get-tuple-element.75), channel_id=1, source_target_pairs={{0,16},{8,24},{16,0},{24,8},{1,17},{9,25},{17,1},{25,9},{2,18},{10... | collective-permute-start | bytes 393224 | tf_op jit(solution)/shard_map/ppermute | solution.py:216
  32.4 6.9 %collective-permute-start.15 = (bf16[512,128]{1,0:T(8,128)(2,1)S(1)}, bf16[512,128]{1,0:T(8,128)(2,1)S(1)}, u32[]{:S(2)}, u32[]{:S(2)}) collective-permute-start(bf16[512,128]{1,0:T(8,128)(2,1)S(1)} %get-tuple-element.76), channel_id=1, source_target_pairs={{0,24},{8,16},{16,8},{24,0},{1,25},{9,17},{17,9},{25,1},{2,26},{10... | collective-permute-start | bytes 393224 | tf_op jit(solution)/shard_map/ppermute | solution.py:216
  33.0 6.8 %collective-permute-start.23 = (bf16[512,128]{1,0:T(8,128)(2,1)S(1)}, bf16[512,128]{1,0:T(8,128)(2,1)S(1)}, u32[]{:S(2)}, u32[]{:S(2)}) collective-permute-start(bf16[512,128]{1,0:T(8,128)(2,1)S(1)} %get-tuple-element.86.root), channel_id=1, source_target_pairs={{0,8},{8,0},{16,24},{24,16},{1,9},{9,1},{17,25},{25,17},{2,10},{10... | collective-permute-start | bytes 393224 | tf_op jit(solution)/shard_map/ppermute | solution.py:216
  34.3 7.2 %collective-permute-start.21 = (bf16[512,128]{1,0:T(8,128)(2,1)S(1)}, bf16[512,128]{1,0:T(8,128)(2,1)S(1)}, u32[]{:S(2)}, u32[]{:S(2)}) collective-permute-start(bf16[512,128]{1,0:T(8,128)(2,1)S(1)} %get-tuple-element.84.root), channel_id=1, source_target_pairs={{0,16},{8,24},{16,0},{24,8},{1,17},{9,25},{17,1},{25,9},{2,18},{10... | collective-permute-start | bytes 393224 | tf_op jit(solution)/shard_map/ppermute | solution.py:216
  36.6 6.3 %collective-permute-start.17 = (bf16[512,128]{1,0:T(8,128)(2,1)S(1)}, bf16[512,128]{1,0:T(8,128)(2,1)S(1)}, u32[]{:S(2)}, u32[]{:S(2)}) collective-permute-start(bf16[512,128]{1,0:T(8,128)(2,1)S(1)} %get-tuple-element.73.grad_pre.pre.grads), channel_id=1, source_target_pairs={{0,1},{1,0},{2,3},{3,2},{4,5},{5,4},{6,7},{7,6},{8,9},{9,8},{10,11... | collective-permute-start | bytes 393224 | tf_op jit(solution)/shard_map/ppermute | solution.py:216
  39.3 3.6 %collective-permute-start.16 = (bf16[512,128]{1,0:T(8,128)(2,1)S(1)}, bf16[512,128]{1,0:T(8,128)(2,1)S(1)}, u32[]{:S(2)}, u32[]{:S(2)}) collective-permute-start(bf16[512,128]{1,0:T(8,128)(2,1)S(1)} %shard_map.103.hidden.grads), channel_id=1, source_target_pairs={{0,1},{1,0},{2,3},{3,2},{4,5},{5,4},{6,7},{7,6},{8,9},{9,8},{10,11... | collective-permute-start | bytes 393224 | tf_op jit(solution)/shard_map/ppermute | solution.py:216
  39.9 8.8 %collective-permute-start.24 = (bf16[512,256]{1,0:T(8,128)(2,1)S(1)}, bf16[512,256]{1,0:T(8,128)(2,1)S(1)}, u32[]{:S(2)}, u32[]{:S(2)}) collective-permute-start(bf16[512,256]{1,0:T(8,128)(2,1)S(1)} %shard_map.108.bottom), channel_id=1, source_target_pairs={{0,16},{8,24},{16,0},{24,8},{1,17},{9,25},{17,1},{25,9},{2,18},{10... | collective-permute-start | bytes 786440 | tf_op jit(solution)/shard_map/ppermute | solution.py:216
  41.6 8.5 %collective-permute-start.22 = (bf16[512,256]{1,0:T(8,128)(2,1)S(1)}, bf16[512,256]{1,0:T(8,128)(2,1)S(1)}, u32[]{:S(2)}, u32[]{:S(2)}) collective-permute-start(bf16[512,256]{1,0:T(8,128)(2,1)S(1)} %shard_map.107.top), channel_id=1, source_target_pairs={{0,8},{8,0},{16,24},{24,16},{1,9},{9,1},{17,25},{25,17},{2,10},{10... | collective-permute-start | bytes 786440 | tf_op jit(solution)/shard_map/ppermute | solution.py:216
  43.4 12.4 %collective-permute-start.18 = (bf16[512,128]{1,0:T(8,128)(2,1)S(1)}, bf16[512,128]{1,0:T(8,128)(2,1)S(1)}, u32[]{:S(2)}, u32[]{:S(2)}) collective-permute-start(bf16[512,128]{1,0:T(8,128)(2,1)S(1)} %get-tuple-element.79), channel_id=1, source_target_pairs={{0,4},{1,5},{2,6},{3,7},{4,0},{5,1},{6,2},{7,3},{8,12},{9,13},{10,... | collective-permute-start | bytes 393224 | tf_op jit(solution)/shard_map/ppermute | solution.py:216
  45.9 9.9 %collective-permute-start.19 = (bf16[512,128]{1,0:T(8,128)(2,1)S(1)}, bf16[512,128]{1,0:T(8,128)(2,1)S(1)}, u32[]{:S(2)}, u32[]{:S(2)}) collective-permute-start(bf16[512,128]{1,0:T(8,128)(2,1)S(1)} %get-tuple-element.80), channel_id=1, source_target_pairs={{0,6},{1,7},{2,4},{3,5},{4,2},{5,3},{6,0},{7,1},{8,14},{9,15},{10,... | collective-permute-start | bytes 393224 | tf_op jit(solution)/shard_map/ppermute | solution.py:216
  47.2 8.6 %collective-permute-start.20 = (bf16[512,128]{1,0:T(8,128)(2,1)S(1)}, bf16[512,128]{1,0:T(8,128)(2,1)S(1)}, u32[]{:S(2)}, u32[]{:S(2)}) collective-permute-start(bf16[512,128]{1,0:T(8,128)(2,1)S(1)} %get-tuple-element.81), channel_id=1, source_target_pairs={{0,2},{1,3},{2,0},{3,1},{4,6},{5,7},{6,4},{7,5},{8,10},{9,11},{10,... | collective-permute-start | bytes 393224 | tf_op jit(solution)/shard_map/ppermute | solution.py:216
  50.1 5.0 %collective-permute-start = (bf16[512,128]{1,0:T(8,128)(2,1)S(1)}, bf16[512,128]{1,0:T(8,128)(2,1)S(1)}, u32[]{:S(2)}, u32[]{:S(2)}) collective-permute-start(bf16[512,128]{1,0:T(8,128)(2,1)S(1)} %get-tuple-element.12.top), channel_id=1, source_target_pairs={{0,16},{8,24},{16,0},{24,8},{1,17},{9,25},{17,1},{25,9},{2,18},{10... | collective-permute-start | bytes 393224 | tf_op jit(solution)/shard_map/cond/branch_1_fun/ppermute | solution.py:216
  50.7 5.0 %collective-permute-start.1 = (bf16[512,128]{1,0:T(8,128)(2,1)S(1)}, bf16[512,128]{1,0:T(8,128)(2,1)S(1)}, u32[]{:S(2)}, u32[]{:S(2)}) collective-permute-start(bf16[512,128]{1,0:T(8,128)(2,1)S(1)} %get-tuple-element.13.bottom), channel_id=1, source_target_pairs={{0,8},{8,0},{16,24},{24,16},{1,9},{9,1},{17,25},{25,17},{2,10},{10... | collective-permute-start | bytes 393224 | tf_op jit(solution)/shard_map/cond/branch_1_fun/ppermute | solution.py:216
  55.8 1.0 %copy-start.8 = (f32[1024,128]{1,0:T(8,128)}, f32[1024,128]{1,0:T(8,128)S(1)}, u32[]{:S(2)}) copy-start(f32[1024,128]{1,0:T(8,128)S(1)} %get-tuple-element.58) | copy-start | bytes 1572868
  (2 other events, 1.8 us)

commit v8 on v7

--- a/solution.py
+++ b/solution.py
@@ -91,11 +91,14 @@
 def forward_kernel(nf, *refs):
     pieces, (right, hidden, own) = refs[:nf], refs[nf:]
     rows, width = hidden.shape
-    half = rows // 2
-    for at in (0, half):
-        part = slice(at, at + half)
-        left = jnp.concatenate([piece[part, :] for piece in pieces], 1)
-        total = dot(left, right[...])
+    step = rows // 2
+    for at in range(0, rows, step):
+        part = slice(at, at + step)
+        total = None
+        for k in range(0, nf, 2):
+            left = jnp.concatenate([pieces[k][part, :], pieces[k + 1][part, :]], 1)
+            product = dot(left, right[k * width : (k + 2) * width, :])
+            total = product if total is None else total + product
         hidden[part, :] = total[:, :width].astype(BF)
         own[part, :] = total[:, width:]
 
@@ -341,26 +344,27 @@
         call(join_kernel, joined[:1], [VMEM] * 3, arrays)[0]
         for arrays in zip(weight_part, root_part, root_got)
     ]
-    for masks in between:
+    for masks in between[:-1]:
         got = [swap(part, "rows", mask) for part, mask in zip(grads, masks)]
-        pairs = grads[0], got[0], grads[1], got[1]
-        last = masks == final
-        shapes = [sds((depth // 2, width), BF)] * 2 if last else joined
-        grads = call(pair_sum_kernel, shapes, [VMEM] * 4, pairs)
+        grads = call(pair_sum_kernel, joined, [VMEM] * 4, (grads[0], got[0], grads[1], got[1]))
+    got = [swap(part, "rows", mask) for part, mask in zip(grads, final)]
+    pairs = grads[0], got[0], grads[1], got[1]
 
     def place(top, top_2, bottom, bottom_2):
         arrays = top, top_2, bottom, bottom_2
         return call(place_kernel, [sds((depth, width), F32)], [VMEM] * 4, arrays)[0]
 
     def finish(operands):
-        grads, pairs = operands
+        pairs = operands
+        shapes = [sds((depth // 2, width), BF)] * 2
+        grads = call(pair_sum_kernel, shapes, [VMEM] * 4, pairs)
         got = [swap(part, "rows", mask) for part, mask in zip(grads, first)]
         return place(grads[0], got[0], grads[1], got[1]), place(*pairs)
 
     def skip(operands):
         return (jnp.zeros((depth, width), F32),) * 2
 
-    operands = tuple(grads), tuple(pairs)
+    operands = tuple(pairs)
     grad_weight, grad_root = lax.cond(block_counts[0] > 0, finish, skip, operands)
     *sums_f, grad_weight, grad_root = lax.optimization_barrier((*sums_f, grad_weight, grad_root))
     (grad_feats,) = call(

time: 57.1 us -> 56.9 us (level)
  waiting for transfers between devices: 14.7 us -> 16.6 us
  starting transfers between devices: 28.1 us -> 26.9 us
  Pallas kernels: 8.39 us -> 7.69 us
    ppermute x25, waiting for transfers between devices: 14.7 us -> 16.6 us  [swap(): lax.ppermute(array, axis, [(i, i ^ mask) for i in range(lax.axis_size(axi...]
    ppermute x25, starting transfers between devices: 28.1 us -> 26.9 us  [swap(): lax.ppermute(array, axis, [(i, i ^ mask) for i in range(lax.axis_size(axi...]
    pallas_call x19, Pallas kernels: 8.39 us -> 7.69 us  [call(): pl.pallas_call(body, out_shape=outs, in_specs=specs, out_specs=[VMEM] * l...]
  transfers between devices with their start and end apart: 25 -> 25, of which waited for: 11 -> 12; matrix products, arithmetic and copies ran while one was open for 0% -> 0% of each run, Pallas kernels for 12% -> 11%
where the time goes in v8:
time: 56.9 us; the launch traced here: 56.7 us
  starting transfers between devices  26.9 us (47%)
  waiting for transfers between devices  16.6 us (29%)
  Pallas kernels  7.69 us (14%)
  local copies, waits for them, and re-layouts  4.57 us (8%)
  between operations  0.86 us (2%)
    ppermute x25, starting transfers between devices, swap(): lax.ppermute(array, axis, [(i, i ^ mask) for i in range(lax.axis_size(axi...  26.9 us
    ppermute x25, waiting for transfers between devices, swap(): lax.ppermute(array, axis, [(i, i ^ mask) for i in range(lax.axis_size(axi...  16.6 us
    pallas_call x19, Pallas kernels, call(): pl.pallas_call(body, out_shape=outs, in_specs=specs, out_specs=[VMEM] * l...  7.69 us
    unnamed x18, local copies, waits for them, and re-layouts  4.57 us
  transfers between devices with their start and end apart: 25, of which 12 were waited for; matrix products, arithmetic and copies ran while one was open for 0% of the time, Pallas kernels for 11%

profile of v8, /device:TPU:0, one launch (start us, length us, event | category | flops | bytes accessed | tf_op | source)
XLA Modules:
  0.0 56.7 jit_solution(10663371268911166182)
XLA Ops:
  0.6 4.1 %collective-permute-start.2 = (bf16[512,128]{1,0:T(8,128)(2,1)}, bf16[512,128]{1,0:T(8,128)(2,1)S(1)}, u32[]{:S(2)}, u32[]{:S(2)}) collective-permute-start(bf16[512,128]{1,0:T(8,128)(2,1)} %feats.1), channel_id=1, source_target_pairs={{0,4},{1,5},{2,6},{3,7},{4,0},{5,1},{6,2},{7,3},{8,12},{9,13},{10,... | collective-permute-start | bytes 393224 | tf_op jit(solution)/shard_map/ppermute | solution.py:219
  4.7 1.6 %collective-permute-start.3 = (bf16[512,128]{1,0:T(8,128)(2,1)}, bf16[512,128]{1,0:T(8,128)(2,1)S(1)}, u32[]{:S(2)}, u32[]{:S(2)}) collective-permute-start(bf16[512,128]{1,0:T(8,128)(2,1)} %feats.1), channel_id=1, source_target_pairs={{0,2},{1,3},{2,0},{3,1},{4,6},{5,7},{6,4},{7,5},{8,10},{9,11},{10,... | collective-permute-start | bytes 393224 | tf_op jit(solution)/shard_map/ppermute | solution.py:219
  6.3 0.9 %copy-done.1 = bf16[1024,128]{1,0:T(8,128)(2,1)S(1)} copy-done((bf16[1024,128]{1,0:T(8,128)(2,1)S(1)}, bf16[1024,128]{1,0:T(8,128)(2,1)}, u32[]{:S(2)}) %copy-start.1) | copy-done | bytes 262168
  7.3 0.9 %copy-done.2 = bf16[1024,128]{1,0:T(8,128)(2,1)S(1)} copy-done((bf16[1024,128]{1,0:T(8,128)(2,1)S(1)}, bf16[1024,128]{1,0:T(8,128)(2,1)}, u32[]{:S(2)}) %copy-start.2) | copy-done | bytes 262168
  8.2 0.9 %copy-done.3 = bf16[512,128]{1,0:T(8,128)(2,1)S(1)} copy-done((bf16[512,128]{1,0:T(8,128)(2,1)S(1)}, bf16[512,128]{1,0:T(8,128)(2,1)}, u32[]{:S(2)}) %copy-start.3) | copy-done | bytes 131096
  9.2 2.1 %collective-permute-done.2.refs_4_ = bf16[512,128]{1,0:T(8,128)(2,1)S(1)} collective-permute-done((bf16[512,128]{1,0:T(8,128)(2,1)}, bf16[512,128]{1,0:T(8,128)(2,1)S(1)}, u32[]{:S(2)}, u32[]{:S(2)}) %collective-permute-start.2) | collective-permute-done | bytes 131104 | tf_op jit(solution)/shard_map/ppermute | solution.py:219
  11.6 1.4 %collective-permute-start.6 = (bf16[512,128]{1,0:T(8,128)(2,1)S(1)}, bf16[512,128]{1,0:T(8,128)(2,1)S(1)}, u32[]{:S(2)}, u32[]{:S(2)}) collective-permute-start(bf16[512,128]{1,0:T(8,128)(2,1)S(1)} %collective-permute-done.2.refs_4_), channel_id=1, source_target_pairs={{0,2},{1,3},{2,0},{3,1},{4,6},{5,7},{6,4},{7,5},{8,10},{9,11},{10,... | collective-permute-start | bytes 393224 | tf_op jit(solution)/shard_map/ppermute | solution.py:219
  13.5 3.0 %collective-permute-done.6.refs_6_ = bf16[512,128]{1,0:T(8,128)(2,1)S(1)} collective-permute-done((bf16[512,128]{1,0:T(8,128)(2,1)S(1)}, bf16[512,128]{1,0:T(8,128)(2,1)S(1)}, u32[]{:S(2)}, u32[]{:S(2)}) %collective-permute-start.6) | collective-permute-done | bytes 131104 | tf_op jit(solution)/shard_map/ppermute | solution.py:219
  17.1 0.8 %collective-permute-done.9.refs_7_ = bf16[512,128]{1,0:T(8,128)(2,1)S(1)} collective-permute-done((bf16[512,128]{1,0:T(8,128)(2,1)S(1)}, bf16[512,128]{1,0:T(8,128)(2,1)S(1)}, u32[]{:S(2)}, u32[]{:S(2)}) %collective-permute-start.9) | collective-permute-done | bytes 131104 | tf_op jit(solution)/shard_map/ppermute | solution.py:219
  18.3 1.6 %collective-permute-start.12 = (bf16[512,128]{1,0:T(8,128)(2,1)S(1)}, bf16[512,128]{1,0:T(8,128)(2,1)S(1)}, u32[]{:S(2)}, u32[]{:S(2)}) collective-permute-start(bf16[512,128]{1,0:T(8,128)(2,1)S(1)} %get-tuple-element.65.hidden), channel_id=1, source_target_pairs={{0,8},{8,0},{16,24},{24,16},{1,9},{9,1},{17,25},{25,17},{2,10},{10... | collective-permute-start | bytes 393224 | tf_op jit(solution)/shard_map/ppermute | solution.py:219
  19.9 1.5 %collective-permute-start.10 = (bf16[512,128]{1,0:T(8,128)(2,1)S(1)}, bf16[512,128]{1,0:T(8,128)(2,1)S(1)}, u32[]{:S(2)}, u32[]{:S(2)}) collective-permute-start(bf16[512,128]{1,0:T(8,128)(2,1)S(1)} %get-tuple-element.65.hidden), channel_id=1, source_target_pairs={{0,16},{8,24},{16,0},{24,8},{1,17},{9,25},{17,1},{25,9},{2,18},{10... | collective-permute-start | bytes 393224 | tf_op jit(solution)/shard_map/ppermute | solution.py:219
  21.9 1.7 %copy-done = bf16[80,128,128]{2,1,0:T(8,128)(2,1)S(1)} copy-done((bf16[80,128,128]{2,1,0:T(8,128)(2,1)S(1)}, bf16[80,128,128]{2,1,0:T(8,128)(2,1)}, u32[]{:S(2)}) %copy-start) | copy-done | bytes 2621464
  23.6 1.1 %shard_map.94.adj.refs_2_ = bf16[512,2048]{1,0:T(8,128)(2,1)S(1)} custom-call(s32[4]{0:T(128)S(1)} %copy-done.6, s32[80]{0:T(128)S(1)} %copy-done.5, bf16[80,128,128]{2,1,0:T(8,128)(2,1)S(1)} %copy-done), custom_call_target="tpu_custom_call" | custom-call | flops 4194304 | bytes 4718928 | tf_op jit(solution)/shard_map/pallas_call | solution.py:28
  24.8 1.4 %shard_map.95.refs_3_.adj_t = bf16[2048,512]{1,0:T(8,128)(2,1)S(1)} custom-call(bf16[512,2048]{1,0:T(8,128)(2,1)S(1)} %shard_map.94.adj.refs_2_), custom_call_target="tpu_custom_call" | custom-call | bytes 4194304 | tf_op jit(solution)/shard_map/pallas_call | solution.py:28
  27.2 0.8 %collective-permute-done.10.refs_0_ = bf16[512,128]{1,0:T(8,128)(2,1)S(1)} collective-permute-done((bf16[512,128]{1,0:T(8,128)(2,1)S(1)}, bf16[512,128]{1,0:T(8,128)(2,1)S(1)}, u32[]{:S(2)}, u32[]{:S(2)}) %collective-permute-start.10) | collective-permute-done | bytes 131104 | tf_op jit(solution)/shard_map/ppermute | solution.py:219
  28.0 1.0 %shard_map.101 = (bf16[512,128]{1,0:T(8,128)(2,1)S(1)}, bf16[512,128]{1,0:T(8,128)(2,1)S(1)}, bf16[512,128]{1,0:T(8,128)(2,1)S(1)}, bf16[512,128]{1,0:T(8,128)(2,1)S(1)}) custom-call(bf16[512,128]{1,0:T(8,128)(2,1)S(1)} %collective-permute-done.10.refs_0_, bf16[512,128]{1,0:T(8,128)(2,1)S(1)} %collective-permute-done.11.refs_1_, ...), custom_call_target="tpu_custom_call" | custom-call | flops 536870912 | bytes 5373952 | tf_op jit(solution)/shard_map/pallas_call | solution.py:28
  29.0 1.8 %collective-permute-start.13 = (bf16[512,128]{1,0:T(8,128)(2,1)S(1)}, bf16[512,128]{1,0:T(8,128)(2,1)S(1)}, u32[]{:S(2)}, u32[]{:S(2)}) collective-permute-start(bf16[512,128]{1,0:T(8,128)(2,1)S(1)} %get-tuple-element.68), channel_id=1, source_target_pairs={{0,8},{8,0},{16,24},{24,16},{1,9},{9,1},{17,25},{25,17},{2,10},{10... | collective-permute-start | bytes 393224 | tf_op jit(solution)/shard_map/ppermute | solution.py:219
  30.8 0.9 %collective-permute-start.14 = (bf16[512,128]{1,0:T(8,128)(2,1)S(1)}, bf16[512,128]{1,0:T(8,128)(2,1)S(1)}, u32[]{:S(2)}, u32[]{:S(2)}) collective-permute-start(bf16[512,128]{1,0:T(8,128)(2,1)S(1)} %get-tuple-element.69), channel_id=1, source_target_pairs={{0,16},{8,24},{16,0},{24,8},{1,17},{9,25},{17,1},{25,9},{2,18},{10... | collective-permute-start | bytes 393224 | tf_op jit(solution)/shard_map/ppermute | solution.py:219
  31.7 0.8 %collective-permute-start.15 = (bf16[512,128]{1,0:T(8,128)(2,1)S(1)}, bf16[512,128]{1,0:T(8,128)(2,1)S(1)}, u32[]{:S(2)}, u32[]{:S(2)}) collective-permute-start(bf16[512,128]{1,0:T(8,128)(2,1)S(1)} %get-tuple-element.70), channel_id=1, source_target_pairs={{0,24},{8,16},{16,8},{24,0},{1,25},{9,17},{17,9},{25,1},{2,26},{10... | collective-permute-start | bytes 393224 | tf_op jit(solution)/shard_map/ppermute | solution.py:219
  33.0 1.8 %collective-permute-start.23 = (bf16[512,128]{1,0:T(8,128)(2,1)S(1)}, bf16[512,128]{1,0:T(8,128)(2,1)S(1)}, u32[]{:S(2)}, u32[]{:S(2)}) collective-permute-start(bf16[512,128]{1,0:T(8,128)(2,1)S(1)} %get-tuple-element.80.root), channel_id=1, source_target_pairs={{0,8},{8,0},{16,24},{24,16},{1,9},{9,1},{17,25},{25,17},{2,10},{10... | collective-permute-start | bytes 393224 | tf_op jit(solution)/shard_map/ppermute | solution.py:219
  34.8 0.9 %collective-permute-start.21 = (bf16[512,128]{1,0:T(8,128)(2,1)S(1)}, bf16[512,128]{1,0:T(8,128)(2,1)S(1)}, u32[]{:S(2)}, u32[]{:S(2)}) collective-permute-start(bf16[512,128]{1,0:T(8,128)(2,1)S(1)} %get-tuple-element.78.root), channel_id=1, source_target_pairs={{0,16},{8,24},{16,0},{24,8},{1,17},{9,25},{17,1},{25,9},{2,18},{10... | collective-permute-start | bytes 393224 | tf_op jit(solution)/shard_map/ppermute | solution.py:219
  36.1 3.0 %collective-permute-done.14.refs_2_ = bf16[512,128]{1,0:T(8,128)(2,1)S(1)} collective-permute-done((bf16[512,128]{1,0:T(8,128)(2,1)S(1)}, bf16[512,128]{1,0:T(8,128)(2,1)S(1)}, u32[]{:S(2)}, u32[]{:S(2)}) %collective-permute-start.14) | collective-permute-done | bytes 131104 | tf_op jit(solution)/shard_map/ppermute | solution.py:219
  39.8 1.5 %collective-permute-start.24 = (bf16[512,256]{1,0:T(8,128)(2,1)S(1)}, bf16[512,256]{1,0:T(8,128)(2,1)S(1)}, u32[]{:S(2)}, u32[]{:S(2)}) collective-permute-start(bf16[512,256]{1,0:T(8,128)(2,1)S(1)} %shard_map.108), channel_id=1, source_target_pairs={{0,16},{8,24},{16,0},{24,8},{1,17},{9,25},{17,1},{25,9},{2,18},{10... | collective-permute-start | bytes 786440 | tf_op jit(solution)/shard_map/ppermute | solution.py:219
  41.4 1.1 %collective-permute-start.22 = (bf16[512,256]{1,0:T(8,128)(2,1)S(1)}, bf16[512,256]{1,0:T(8,128)(2,1)S(1)}, u32[]{:S(2)}, u32[]{:S(2)}) collective-permute-start(bf16[512,256]{1,0:T(8,128)(2,1)S(1)} %shard_map.107), channel_id=1, source_target_pairs={{0,8},{8,0},{16,24},{24,16},{1,9},{9,1},{17,25},{25,17},{2,10},{10... | collective-permute-start | bytes 786440 | tf_op jit(solution)/shard_map/ppermute | solution.py:219
  42.9 2.5 %collective-permute-start.18 = (bf16[512,128]{1,0:T(8,128)(2,1)S(1)}, bf16[512,128]{1,0:T(8,128)(2,1)S(1)}, u32[]{:S(2)}, u32[]{:S(2)}) collective-permute-start(bf16[512,128]{1,0:T(8,128)(2,1)S(1)} %get-tuple-element.73), channel_id=1, source_target_pairs={{0,4},{1,5},{2,6},{3,7},{4,0},{5,1},{6,2},{7,3},{8,12},{9,13},{10,... | collective-permute-start | bytes 393224 | tf_op jit(solution)/shard_map/ppermute | solution.py:219
  45.4 1.3 %collective-permute-start.19 = (bf16[512,128]{1,0:T(8,128)(2,1)S(1)}, bf16[512,128]{1,0:T(8,128)(2,1)S(1)}, u32[]{:S(2)}, u32[]{:S(2)}) collective-permute-start(bf16[512,128]{1,0:T(8,128)(2,1)S(1)} %get-tuple-element.74), channel_id=1, source_target_pairs={{0,6},{1,7},{2,4},{3,5},{4,2},{5,3},{6,0},{7,1},{8,14},{9,15},{10,... | collective-permute-start | bytes 393224 | tf_op jit(solution)/shard_map/ppermute | solution.py:219
  47.2 1.3 %collective-permute-done.24 = bf16[512,256]{1,0:T(8,128)(2,1)S(1)} collective-permute-done((bf16[512,256]{1,0:T(8,128)(2,1)S(1)}, bf16[512,256]{1,0:T(8,128)(2,1)S(1)}, u32[]{:S(2)}, u32[]{:S(2)}) %collective-permute-start.24) | collective-permute-done | bytes 262176 | tf_op jit(solution)/shard_map/ppermute | solution.py:219
  48.5 1.1 %collective-permute-done.22 = bf16[512,256]{1,0:T(8,128)(2,1)S(1)} collective-permute-done((bf16[512,256]{1,0:T(8,128)(2,1)S(1)}, bf16[512,256]{1,0:T(8,128)(2,1)S(1)}, u32[]{:S(2)}, u32[]{:S(2)}) %collective-permute-start.22) | collective-permute-done | bytes 262176 | tf_op jit(solution)/shard_map/ppermute | solution.py:219
  49.6 5.9 %conditional.1 = (f32[1024,128]{1,0:T(8,128)S(1)}, f32[1024,128]{1,0:T(8,128)S(1)}) conditional(s32[]{:T(128)} %bitcast, () %tuple.23, (bf16[512,256]{1,0:T(8,128)(2,1)S(1)}, bf16[512,256]{1,0:T(8,128)(2,1)S(1)}, bf16[512,256]{1,0:T(8,128)(2,1)S(1)}, bf16[512,256]{1,0:T(8,128)(2,1)S(1)}) %tuple.24), branch_computations={%region_0.0_spmd, %region_1.0_spmd} | conditional | bytes 4980832 | solution.py:368
  49.7 0.9 %collective-permute-start = (bf16[512,128]{1,0:T(8,128)(2,1)S(1)}, bf16[512,128]{1,0:T(8,128)(2,1)S(1)}, u32[]{:S(2)}, u32[]{:S(2)}) collective-permute-start(bf16[512,128]{1,0:T(8,128)(2,1)S(1)} %get-tuple-element.12.top), channel_id=1, source_target_pairs={{0,16},{8,24},{16,0},{24,8},{1,17},{9,25},{17,1},{25,9},{2,18},{10... | collective-permute-start | bytes 393224 | tf_op jit(solution)/shard_map/cond/branch_1_fun/ppermute | solution.py:219
  50.6 1.1 %collective-permute-start.1 = (bf16[512,128]{1,0:T(8,128)(2,1)S(1)}, bf16[512,128]{1,0:T(8,128)(2,1)S(1)}, u32[]{:S(2)}, u32[]{:S(2)}) collective-permute-start(bf16[512,128]{1,0:T(8,128)(2,1)S(1)} %get-tuple-element.13.bottom), channel_id=1, source_target_pairs={{0,8},{8,0},{16,24},{24,16},{1,9},{9,1},{17,25},{25,17},{2,10},{10... | collective-permute-start | bytes 393224 | tf_op jit(solution)/shard_map/cond/branch_1_fun/ppermute | solution.py:219
  51.7 3.0 %collective-permute-done.top_2 = bf16[512,128]{1,0:T(8,128)(2,1)S(1)} collective-permute-done((bf16[512,128]{1,0:T(8,128)(2,1)S(1)}, bf16[512,128]{1,0:T(8,128)(2,1)S(1)}, u32[]{:S(2)}, u32[]{:S(2)}) %collective-permute-start) | collective-permute-done | bytes 131104 | tf_op jit(solution)/shard_map/cond/branch_1_fun/ppermute | solution.py:219
  (56 shorter events, 7.6 us)
Async XLA Ops:
  0.6 10.7 %collective-permute-start.2 = (bf16[512,128]{1,0:T(8,128)(2,1)}, bf16[512,128]{1,0:T(8,128)(2,1)S(1)}, u32[]{:S(2)}, u32[]{:S(2)}) collective-permute-start(bf16[512,128]{1,0:T(8,128)(2,1)} %feats.1), channel_id=1, source_target_pairs={{0,4},{1,5},{2,6},{3,7},{4,0},{5,1},{6,2},{7,3},{8,12},{9,13},{10,... | collective-permute-start | bytes 393224 | tf_op jit(solution)/shard_map/ppermute | solution.py:219
  4.7 6.8 %collective-permute-start.3 = (bf16[512,128]{1,0:T(8,128)(2,1)}, bf16[512,128]{1,0:T(8,128)(2,1)S(1)}, u32[]{:S(2)}, u32[]{:S(2)}) collective-permute-start(bf16[512,128]{1,0:T(8,128)(2,1)} %feats.1), channel_id=1, source_target_pairs={{0,2},{1,3},{2,0},{3,1},{4,6},{5,7},{6,4},{7,5},{8,10},{9,11},{10,... | collective-permute-start | bytes 393224 | tf_op jit(solution)/shard_map/ppermute | solution.py:219
  6.3 5.3 %collective-permute-start.4 = (bf16[512,128]{1,0:T(8,128)(2,1)}, bf16[512,128]{1,0:T(8,128)(2,1)S(1)}, u32[]{:S(2)}, u32[]{:S(2)}) collective-permute-start(bf16[512,128]{1,0:T(8,128)(2,1)} %feats.1), channel_id=1, source_target_pairs={{0,1},{1,0},{2,3},{3,2},{4,5},{5,4},{6,7},{7,6},{8,9},{9,8},{10,11... | collective-permute-start | bytes 393224 | tf_op jit(solution)/shard_map/ppermute | solution.py:219
  6.3 1.0 %copy-start.1 = (bf16[1024,128]{1,0:T(8,128)(2,1)S(1)}, bf16[1024,128]{1,0:T(8,128)(2,1)}, u32[]{:S(2)}) copy-start(bf16[1024,128]{1,0:T(8,128)(2,1)} %weight.1) | copy-start | bytes 786436
  9.1 12.8 %copy-start.5 = (s32[80]{0:T(128)S(1)}, s32[80]{0:T(128)}, u32[]{:S(2)}) copy-start(s32[80]{0:T(128)} %all_cols.1) | copy-start | bytes 964
  9.1 12.8 %copy-start.6 = (s32[4]{0:T(128)S(1)}, s32[4]{0:T(128)}, u32[]{:S(2)}) copy-start(s32[4]{0:T(128)} %all_counts.1) | copy-start | bytes 52
  11.6 5.0 %collective-permute-start.6 = (bf16[512,128]{1,0:T(8,128)(2,1)S(1)}, bf16[512,128]{1,0:T(8,128)(2,1)S(1)}, u32[]{:S(2)}, u32[]{:S(2)}) collective-permute-start(bf16[512,128]{1,0:T(8,128)(2,1)S(1)} %collective-permute-done.2.refs_4_), channel_id=1, source_target_pairs={{0,2},{1,3},{2,0},{3,1},{4,6},{5,7},{6,4},{7,5},{8,10},{9,11},{10,... | collective-permute-start | bytes 393224 | tf_op jit(solution)/shard_map/ppermute | solution.py:219
  13.0 3.5 %collective-permute-start.7 = (bf16[512,128]{1,0:T(8,128)(2,1)S(1)}, bf16[512,128]{1,0:T(8,128)(2,1)S(1)}, u32[]{:S(2)}, u32[]{:S(2)}) collective-permute-start(bf16[512,128]{1,0:T(8,128)(2,1)S(1)} %collective-permute-done.2.refs_4_), channel_id=1, source_target_pairs={{0,1},{1,0},{2,3},{3,2},{4,5},{5,4},{6,7},{7,6},{8,9},{9,8},{10,11... | collective-permute-start | bytes 393224 | tf_op jit(solution)/shard_map/ppermute | solution.py:219
  13.0 3.5 %collective-permute-start.8 = (bf16[512,128]{1,0:T(8,128)(2,1)S(1)}, bf16[512,128]{1,0:T(8,128)(2,1)S(1)}, u32[]{:S(2)}, u32[]{:S(2)}) collective-permute-start(bf16[512,128]{1,0:T(8,128)(2,1)S(1)} %collective-permute-done.3.refs_2_), channel_id=1, source_target_pairs={{0,1},{1,0},{2,3},{3,2},{4,5},{5,4},{6,7},{7,6},{8,9},{9,8},{10,11... | collective-permute-start | bytes 393224 | tf_op jit(solution)/shard_map/ppermute | solution.py:219
  16.5 1.4 %collective-permute-start.9 = (bf16[512,128]{1,0:T(8,128)(2,1)S(1)}, bf16[512,128]{1,0:T(8,128)(2,1)S(1)}, u32[]{:S(2)}, u32[]{:S(2)}) collective-permute-start(bf16[512,128]{1,0:T(8,128)(2,1)S(1)} %collective-permute-done.6.refs_6_), channel_id=1, source_target_pairs={{0,1},{1,0},{2,3},{3,2},{4,5},{5,4},{6,7},{7,6},{8,9},{9,8},{10,11... | collective-permute-start | bytes 393224 | tf_op jit(solution)/shard_map/ppermute | solution.py:219
  16.5 9.7 %collective-permute-start.5 = (bf16[2,512,128]{2,1,0:T(8,128)(2,1)S(1)}, bf16[2,512,128]{2,1,0:T(8,128)(2,1)S(1)}, u32[]{:S(2)}, u32[]{:S(2)}) collective-permute-start(bf16[2,512,128]{2,1,0:T(8,128)(2,1)S(1)} %get-tuple-element.55), channel_id=1, source_target_pairs={{0,1},{1,0},{2,3},{3,2},{4,5},{5,4},{6,7},{7,6},{8,9},{9,8},{10,11... | collective-permute-start | bytes 786440 | tf_op jit(solution)/shard_map/ppermute | solution.py:219
  18.3 8.4 %collective-permute-start.12 = (bf16[512,128]{1,0:T(8,128)(2,1)S(1)}, bf16[512,128]{1,0:T(8,128)(2,1)S(1)}, u32[]{:S(2)}, u32[]{:S(2)}) collective-permute-start(bf16[512,128]{1,0:T(8,128)(2,1)S(1)} %get-tuple-element.65.hidden), channel_id=1, source_target_pairs={{0,8},{8,0},{16,24},{24,16},{1,9},{9,1},{17,25},{25,17},{2,10},{10... | collective-permute-start | bytes 393224 | tf_op jit(solution)/shard_map/ppermute | solution.py:219
  19.9 8.1 %collective-permute-start.10 = (bf16[512,128]{1,0:T(8,128)(2,1)S(1)}, bf16[512,128]{1,0:T(8,128)(2,1)S(1)}, u32[]{:S(2)}, u32[]{:S(2)}) collective-permute-start(bf16[512,128]{1,0:T(8,128)(2,1)S(1)} %get-tuple-element.65.hidden), channel_id=1, source_target_pairs={{0,16},{8,24},{16,0},{24,8},{1,17},{9,25},{17,1},{25,9},{2,18},{10... | collective-permute-start | bytes 393224 | tf_op jit(solution)/shard_map/ppermute | solution.py:219
  21.5 6.6 %collective-permute-start.11 = (bf16[512,128]{1,0:T(8,128)(2,1)S(1)}, bf16[512,128]{1,0:T(8,128)(2,1)S(1)}, u32[]{:S(2)}, u32[]{:S(2)}) collective-permute-start(bf16[512,128]{1,0:T(8,128)(2,1)S(1)} %get-tuple-element.65.hidden), channel_id=1, source_target_pairs={{0,24},{8,16},{16,8},{24,0},{1,25},{9,17},{17,9},{25,1},{2,26},{10... | collective-permute-start | bytes 393224 | tf_op jit(solution)/shard_map/ppermute | solution.py:219
  21.9 1.7 %copy-start = (bf16[80,128,128]{2,1,0:T(8,128)(2,1)S(1)}, bf16[80,128,128]{2,1,0:T(8,128)(2,1)}, u32[]{:S(2)}) copy-start(bf16[80,128,128]{2,1,0:T(8,128)(2,1)} %vals.1) | copy-start | bytes 7864324
  26.4 1.6 %copy-start.4 = (bf16[512,128]{1,0:T(8,128)(2,1)S(1)}, bf16[512,128]{1,0:T(8,128)(2,1)}, u32[]{:S(2)}) copy-start(bf16[512,128]{1,0:T(8,128)(2,1)} %refs_5_.1) | copy-start | bytes 393220
  29.0 7.0 %collective-permute-start.13 = (bf16[512,128]{1,0:T(8,128)(2,1)S(1)}, bf16[512,128]{1,0:T(8,128)(2,1)S(1)}, u32[]{:S(2)}, u32[]{:S(2)}) collective-permute-start(bf16[512,128]{1,0:T(8,128)(2,1)S(1)} %get-tuple-element.68), channel_id=1, source_target_pairs={{0,8},{8,0},{16,24},{24,16},{1,9},{9,1},{17,25},{25,17},{2,10},{10... | collective-permute-start | bytes 393224 | tf_op jit(solution)/shard_map/ppermute | solution.py:219
  30.8 8.3 %collective-permute-start.14 = (bf16[512,128]{1,0:T(8,128)(2,1)S(1)}, bf16[512,128]{1,0:T(8,128)(2,1)S(1)}, u32[]{:S(2)}, u32[]{:S(2)}) collective-permute-start(bf16[512,128]{1,0:T(8,128)(2,1)S(1)} %get-tuple-element.69), channel_id=1, source_target_pairs={{0,16},{8,24},{16,0},{24,8},{1,17},{9,25},{17,1},{25,9},{2,18},{10... | collective-permute-start | bytes 393224 | tf_op jit(solution)/shard_map/ppermute | solution.py:219
  31.7 7.4 %collective-permute-start.15 = (bf16[512,128]{1,0:T(8,128)(2,1)S(1)}, bf16[512,128]{1,0:T(8,128)(2,1)S(1)}, u32[]{:S(2)}, u32[]{:S(2)}) collective-permute-start(bf16[512,128]{1,0:T(8,128)(2,1)S(1)} %get-tuple-element.70), channel_id=1, source_target_pairs={{0,24},{8,16},{16,8},{24,0},{1,25},{9,17},{17,9},{25,1},{2,26},{10... | collective-permute-start | bytes 393224 | tf_op jit(solution)/shard_map/ppermute | solution.py:219
  33.0 6.7 %collective-permute-start.23 = (bf16[512,128]{1,0:T(8,128)(2,1)S(1)}, bf16[512,128]{1,0:T(8,128)(2,1)S(1)}, u32[]{:S(2)}, u32[]{:S(2)}) collective-permute-start(bf16[512,128]{1,0:T(8,128)(2,1)S(1)} %get-tuple-element.80.root), channel_id=1, source_target_pairs={{0,8},{8,0},{16,24},{24,16},{1,9},{9,1},{17,25},{25,17},{2,10},{10... | collective-permute-start | bytes 393224 | tf_op jit(solution)/shard_map/ppermute | solution.py:219
  34.8 6.5 %collective-permute-start.21 = (bf16[512,128]{1,0:T(8,128)(2,1)S(1)}, bf16[512,128]{1,0:T(8,128)(2,1)S(1)}, u32[]{:S(2)}, u32[]{:S(2)}) collective-permute-start(bf16[512,128]{1,0:T(8,128)(2,1)S(1)} %get-tuple-element.78.root), channel_id=1, source_target_pairs={{0,16},{8,24},{16,0},{24,8},{1,17},{9,25},{17,1},{25,9},{2,18},{10... | collective-permute-start | bytes 393224 | tf_op jit(solution)/shard_map/ppermute | solution.py:219
  36.0 6.5 %collective-permute-start.17 = (bf16[512,128]{1,0:T(8,128)(2,1)S(1)}, bf16[512,128]{1,0:T(8,128)(2,1)S(1)}, u32[]{:S(2)}, u32[]{:S(2)}) collective-permute-start(bf16[512,128]{1,0:T(8,128)(2,1)S(1)} %get-tuple-element.67.grad_pre.pre.grads), channel_id=1, source_target_pairs={{0,1},{1,0},{2,3},{3,2},{4,5},{5,4},{6,7},{7,6},{8,9},{9,8},{10,11... | collective-permute-start | bytes 393224 | tf_op jit(solution)/shard_map/ppermute | solution.py:219
  39.2 3.3 %collective-permute-start.16 = (bf16[512,128]{1,0:T(8,128)(2,1)S(1)}, bf16[512,128]{1,0:T(8,128)(2,1)S(1)}, u32[]{:S(2)}, u32[]{:S(2)}) collective-permute-start(bf16[512,128]{1,0:T(8,128)(2,1)S(1)} %shard_map.103.hidden.grads), channel_id=1, source_target_pairs={{0,1},{1,0},{2,3},{3,2},{4,5},{5,4},{6,7},{7,6},{8,9},{9,8},{10,11... | collective-permute-start | bytes 393224 | tf_op jit(solution)/shard_map/ppermute | solution.py:219
  39.8 8.8 %collective-permute-start.24 = (bf16[512,256]{1,0:T(8,128)(2,1)S(1)}, bf16[512,256]{1,0:T(8,128)(2,1)S(1)}, u32[]{:S(2)}, u32[]{:S(2)}) collective-permute-start(bf16[512,256]{1,0:T(8,128)(2,1)S(1)} %shard_map.108), channel_id=1, source_target_pairs={{0,16},{8,24},{16,0},{24,8},{1,17},{9,25},{17,1},{25,9},{2,18},{10... | collective-permute-start | bytes 786440 | tf_op jit(solution)/shard_map/ppermute | solution.py:219
  41.4 8.3 %collective-permute-start.22 = (bf16[512,256]{1,0:T(8,128)(2,1)S(1)}, bf16[512,256]{1,0:T(8,128)(2,1)S(1)}, u32[]{:S(2)}, u32[]{:S(2)}) collective-permute-start(bf16[512,256]{1,0:T(8,128)(2,1)S(1)} %shard_map.107), channel_id=1, source_target_pairs={{0,8},{8,0},{16,24},{24,16},{1,9},{9,1},{17,25},{25,17},{2,10},{10... | collective-permute-start | bytes 786440 | tf_op jit(solution)/shard_map/ppermute | solution.py:219
  42.9 12.8 %collective-permute-start.18 = (bf16[512,128]{1,0:T(8,128)(2,1)S(1)}, bf16[512,128]{1,0:T(8,128)(2,1)S(1)}, u32[]{:S(2)}, u32[]{:S(2)}) collective-permute-start(bf16[512,128]{1,0:T(8,128)(2,1)S(1)} %get-tuple-element.73), channel_id=1, source_target_pairs={{0,4},{1,5},{2,6},{3,7},{4,0},{5,1},{6,2},{7,3},{8,12},{9,13},{10,... | collective-permute-start | bytes 393224 | tf_op jit(solution)/shard_map/ppermute | solution.py:219
  45.4 10.2 %collective-permute-start.19 = (bf16[512,128]{1,0:T(8,128)(2,1)S(1)}, bf16[512,128]{1,0:T(8,128)(2,1)S(1)}, u32[]{:S(2)}, u32[]{:S(2)}) collective-permute-start(bf16[512,128]{1,0:T(8,128)(2,1)S(1)} %get-tuple-element.74), channel_id=1, source_target_pairs={{0,6},{1,7},{2,4},{3,5},{4,2},{5,3},{6,0},{7,1},{8,14},{9,15},{10,... | collective-permute-start | bytes 393224 | tf_op jit(solution)/shard_map/ppermute | solution.py:219
  46.7 9.3 %collective-permute-start.20 = (bf16[512,128]{1,0:T(8,128)(2,1)S(1)}, bf16[512,128]{1,0:T(8,128)(2,1)S(1)}, u32[]{:S(2)}, u32[]{:S(2)}) collective-permute-start(bf16[512,128]{1,0:T(8,128)(2,1)S(1)} %get-tuple-element.75), channel_id=1, source_target_pairs={{0,2},{1,3},{2,0},{3,1},{4,6},{5,7},{6,4},{7,5},{8,10},{9,11},{10,... | collective-permute-start | bytes 393224 | tf_op jit(solution)/shard_map/ppermute | solution.py:219
  49.7 5.0 %collective-permute-start = (bf16[512,128]{1,0:T(8,128)(2,1)S(1)}, bf16[512,128]{1,0:T(8,128)(2,1)S(1)}, u32[]{:S(2)}, u32[]{:S(2)}) collective-permute-start(bf16[512,128]{1,0:T(8,128)(2,1)S(1)} %get-tuple-element.12.top), channel_id=1, source_target_pairs={{0,16},{8,24},{16,0},{24,8},{1,17},{9,25},{17,1},{25,9},{2,18},{10... | collective-permute-start | bytes 393224 | tf_op jit(solution)/shard_map/cond/branch_1_fun/ppermute | solution.py:219
  50.6 5.0 %collective-permute-start.1 = (bf16[512,128]{1,0:T(8,128)(2,1)S(1)}, bf16[512,128]{1,0:T(8,128)(2,1)S(1)}, u32[]{:S(2)}, u32[]{:S(2)}) collective-permute-start(bf16[512,128]{1,0:T(8,128)(2,1)S(1)} %get-tuple-element.13.bottom), channel_id=1, source_target_pairs={{0,8},{8,0},{16,24},{24,16},{1,9},{9,1},{17,25},{25,17},{2,10},{10... | collective-permute-start | bytes 393224 | tf_op jit(solution)/shard_map/cond/branch_1_fun/ppermute | solution.py:219
  55.6 1.1 %copy-start.7 = (f32[1024,128]{1,0:T(8,128)}, f32[1024,128]{1,0:T(8,128)S(1)}, u32[]{:S(2)}) copy-start(f32[1024,128]{1,0:T(8,128)S(1)} %get-tuple-element.51) | copy-start | bytes 1572868
  55.6 1.1 %copy-start.8 = (f32[1024,128]{1,0:T(8,128)}, f32[1024,128]{1,0:T(8,128)S(1)}, u32[]{:S(2)}) copy-start(f32[1024,128]{1,0:T(8,128)S(1)} %get-tuple-element.52) | copy-start | bytes 1572868
  (2 other events, 1.9 us)
